TPU v7x, 128 devices: a whole 4x4x4 slice. The times are simulated.
128 devices in a mesh: row: 4 (over y_hi, core), col: 4 (over z), chan: 8 (over x, y_lo).
Axes of the slice: x: 4, y: 4 (y_hi: 2, y_lo: 2; y = y_hi * 2 + y_lo), z: 4, core: 2. Of those that a mesh axis runs over, the one named last changes fastest.
Arguments:
- feature_map: bfloat16 [512, 64, 512], P('chan', 'row', 'col'), may hold values from -6 to 6
- base_kernel: float32 [512, 5, 5], P('chan'), may hold values from -1.25 to 1.25
- base_bias: float32 [512], P('chan'), may hold values from -3 to 3
- base_scale: float32 [512], P('chan'), may hold values from 0.3 to 3
- wave_kernels: float32 [3, 512, 4, 5, 5], P(None, 'chan'), may hold values from -1.25 to 1.25
- wave_scale: float32 [3, 512, 4], P(None, 'chan'), may hold values from 0.3 to 1
- norm_gain: float32 [512], P('chan'), may hold values from 0.5 to 2
- norm_bias: float32 [512], P('chan'), may hold values from -3 to 3
- w_in: bfloat16 [512, 2048], P(None, 'chan'), may hold values from -0.25 to 0.25
- b_in: float32 [2048], P('chan'), may hold values from -3 to 3
- w_out: bfloat16 [2048, 512], P('chan'), may hold values from -0.125 to 0.125
- b_out: float32 [512], P('chan'), may hold values from -3 to 3
- layer_scale: float32 [512], P('chan'), may hold values from 0.5 to 2
- cotangent: bfloat16 [512, 64, 512], P('chan', 'row', 'col'), may hold values from -6 to 6
Outputs:
- output_map: bfloat16 [512, 64, 512], P('chan', 'row', 'col')
- grad_map: bfloat16 [512, 64, 512], P('chan', 'row', 'col')
- grad_w_in: float32 [512, 2048], P(None, 'chan')
- grad_w_out: float32 [2048, 512], P('chan')
All inputs are finite; a program needn't handle non-finite values.
Results may differ from a plain program's by a relative error of at most 0.028.
Values may be sent and summed in bfloat16 or wider, within the bound.
No kernel may reach another device: no remote copies, remote signals or barrier semaphores. Data moves between devices by JAX's collectives and lax.ppermute only.
A program may use at most 128 MiB of HBM per device.

v0:
```python
import math

import jax
import jax.numpy as jnp
from jax import lax
from jax.sharding import PartitionSpec as P

EPSILON = 1e-06
INV_ROOT_TWO = 0.7071067811865476
INV_ROOT_TWO_PI = 0.3989422804014327


def padded_2(block, sides, width):
    for axis, dim in sides:
        count = lax.axis_size(axis)
        forward = [(i, i + 1) for i in range(count - 1)]
        backward = [(target, source) for source, target in forward]
        low = lax.ppermute(
            lax.slice_in_dim(block, block.shape[dim] - width, None, axis=dim), axis, forward
        )
        high = lax.ppermute(lax.slice_in_dim(block, 0, width, axis=dim), axis, backward)
        block = jnp.concatenate([low, block, high], axis=dim)
    return block


def haar_split(source):
    shape_in = source.shape
    blocks = source.reshape(shape_in[:-2] + (shape_in[-2] // 2, 2, shape_in[-1] // 2, 2))
    upleft = blocks[..., :, 0, :, 0]
    upright = blocks[..., :, 0, :, 1]
    lowleft = blocks[..., :, 1, :, 0]
    lowright = blocks[..., :, 1, :, 1]
    return 0.5 * jnp.stack(
        [
            upleft + upright + lowleft + lowright,
            upleft - upright + lowleft - lowright,
            upleft + upright - lowleft - lowright,
            upleft - upright - lowleft + lowright,
        ],
        axis=-3,
    )


def haar_merge(subbands):
    coarse = subbands[..., 0, :, :]
    across = subbands[..., 1, :, :]
    downward = subbands[..., 2, :, :]
    diagonal = subbands[..., 3, :, :]
    upleft = 0.5 * (coarse + across + downward + diagonal)
    upright = 0.5 * (coarse - across + downward - diagonal)
    lowleft = 0.5 * (coarse + across - downward - diagonal)
    lowright = 0.5 * (coarse - across - downward + diagonal)
    blocks = jnp.stack([jnp.stack([upleft, upright], -1), jnp.stack([lowleft, lowright], -1)], -3)
    shape_in = blocks.shape
    return blocks.reshape(shape_in[:-4] + (shape_in[-4] * 2, shape_in[-2] * 2))


def depthwise(padded, kernel):
    rows_out = padded.shape[-2] - kernel.shape[-2] + 1
    cols_out = padded.shape[-1] - kernel.shape[-1] + 1
    summed = jnp.zeros(padded.shape[:-2] + (rows_out, cols_out), jnp.float32)
    for tap_row in range(kernel.shape[-2]):
        for tap_col in range(kernel.shape[-1]):
            summed = (
                summed
                + kernel[..., tap_row, tap_col][..., None, None]
                * padded[..., tap_row : tap_row + rows_out, tap_col : tap_col + cols_out]
            )
    return summed


def mirror(kernel):
    return kernel[..., ::-1, ::-1]


def wavelet_forward(source, base_kernel, base_bias, base_scale, wave_kernels, wave_scale, padder):
    lowpass = source
    branches = []
    for degree in range(wave_kernels.shape[0]):
        subbands = haar_split(lowpass)
        lowpass = subbands[:, 0]
        branches.append(
            wave_scale[degree][:, :, None, None] * depthwise(padder(subbands), wave_kernels[degree])
        )
    coarser = None
    for degree in reversed(range(wave_kernels.shape[0])):
        merged = branches[degree]
        if coarser is not None:
            merged = merged.at[:, 0].add(coarser)
        coarser = haar_merge(merged)
    based = depthwise(padder(source[:, None]), base_kernel[:, None])[:, 0]
    return base_scale[:, None, None] * (based + base_bias[:, None, None]) + coarser


def wavelet_backward(upstream, base_kernel, base_scale, wave_kernels, wave_scale, padder):
    result = depthwise(
        padder((base_scale[:, None, None] * upstream)[:, None]), mirror(base_kernel)[:, None]
    )[:, 0]
    lowpass = upstream
    sources = []
    for degree in range(wave_kernels.shape[0]):
        subbands = haar_split(lowpass)
        lowpass = subbands[:, 0]
        sources.append(
            depthwise(
                padder(wave_scale[degree][:, :, None, None] * subbands),
                mirror(wave_kernels[degree]),
            )
        )
    carried = None
    for degree in reversed(range(wave_kernels.shape[0])):
        merged = sources[degree]
        if carried is not None:
            merged = merged.at[:, 0].add(carried)
        carried = haar_merge(merged)
    return result + carried


def spread(source):
    return padded_2(source.astype(jnp.bfloat16), (("row", 2), ("col", 3)), 2).astype(source.dtype)


def gelu_slope(hidden):
    return (
        0.5 * (1.0 + lax.erf(hidden * INV_ROOT_TWO))
        + hidden * jnp.exp(-0.5 * hidden * hidden) * INV_ROOT_TWO_PI
    )


def channel_sums(first_sum, other_sum):
    return lax.psum((first_sum, other_sum), "chan")


def chan_partial(term_rows, local_chans):
    return lax.psum_scatter(
        term_rows(jnp.int32(0), local_chans * lax.axis_size("chan")).astype(jnp.bfloat16),
        "chan",
        scatter_dimension=0,
        tiled=True,
    ).astype(jnp.float32)


def on_device(
    feature_map,
    base_kernel,
    base_bias,
    base_scale,
    wave_kernels,
    wave_scale,
    norm_gain,
    norm_bias,
    w_in,
    b_in,
    w_out,
    b_out,
    layer_scale,
    cotangent,
):
    local_chans, tile_rows, tile_cols = feature_map.shape
    positions = tile_rows * tile_cols
    chan_count = w_in.shape[0]
    source = feature_map.astype(jnp.float32)
    mixed_map = wavelet_forward(
        source, base_kernel, base_bias, base_scale, wave_kernels, wave_scale, spread
    ).astype(jnp.bfloat16)
    mixed_rows = mixed_map.reshape(local_chans, positions)
    scaled = (
        (layer_scale[:, None, None] * cotangent.astype(jnp.float32))
        .astype(jnp.bfloat16)
        .reshape(local_chans, positions)
    )
    values = mixed_rows.astype(jnp.float32)
    chan_sum, squares = channel_sums(jnp.sum(values, 0), jnp.sum(values * values, 0))
    average = chan_sum / chan_count
    rescale = lax.rsqrt(squares / chan_count - average * average + EPSILON)
    centred = (values - average) * rescale
    normed_loc = (centred * norm_gain[:, None] + norm_bias[:, None]).astype(jnp.bfloat16)
    normed, scaled_all = (
        lax.all_gather(normed_loc, "chan", axis=0, tiled=True),
        lax.all_gather(scaled, "chan", axis=0, tiled=True),
    )
    hidden = (
        lax.dot_general(w_in, normed, (((0,), (0,)), ((), ())), preferred_element_type=jnp.float32)
        + b_in[:, None]
    )
    activated = jax.nn.gelu(hidden, approximate=False).astype(jnp.bfloat16)

    def forward_rows(row_start, row_count):
        return lax.dot_general(
            w_out, activated, (((0,), (0,)), ((), ())), preferred_element_type=jnp.float32
        )

    projected = chan_partial(forward_rows, local_chans)
    grad_activated = jnp.dot(w_out, scaled_all, preferred_element_type=jnp.float32)
    grad_hidden = (grad_activated * gelu_slope(hidden)).astype(jnp.bfloat16)
    part_out = lax.dot_general(
        activated, scaled_all, (((1,), (1,)), ((), ())), preferred_element_type=jnp.float32
    )
    part_in = lax.dot_general(
        normed, grad_hidden, (((1,), (1,)), ((), ())), preferred_element_type=jnp.float32
    )

    def backward_rows(row_start, row_count):
        return jnp.dot(w_in, grad_hidden, preferred_element_type=jnp.float32)

    grad_normed = chan_partial(backward_rows, local_chans)
    weighted = grad_normed * norm_gain[:, None]
    grad_sum, grad_dot = channel_sums(jnp.sum(weighted, 0), jnp.sum(weighted * centred, 0))
    grad_mixed = rescale * (weighted - grad_sum / chan_count - centred * grad_dot / chan_count)
    grad_in, grad_out = (
        lax.psum(part_in.astype(jnp.bfloat16), ("row", "col")).astype(jnp.float32),
        lax.psum(part_out.astype(jnp.bfloat16), ("row", "col")).astype(jnp.float32),
    )
    output_map = (
        source
        + layer_scale[:, None, None]
        * (projected.reshape(local_chans, tile_rows, tile_cols) + b_out[:, None, None])
    ).astype(jnp.bfloat16)
    backward = wavelet_backward(
        grad_mixed.reshape(local_chans, tile_rows, tile_cols),
        base_kernel,
        base_scale,
        wave_kernels,
        wave_scale,
        spread,
    )
    grad_map = (cotangent.astype(jnp.float32) + backward).astype(jnp.bfloat16)
    grad_factor = 1.0 / math.sqrt(float(positions * lax.axis_size("row") * lax.axis_size("col")))
    return (output_map, grad_map, grad_in * grad_factor, grad_out * grad_factor)


def solution(mesh):
    return jax.shard_map(
        on_device,
        mesh=mesh,
        in_specs=(
            P("chan", "row", "col"),
            P("chan", None, None),
            P("chan"),
            P("chan"),
            P(None, "chan", None, None, None),
            P(None, "chan", None),
            P("chan"),
            P("chan"),
            P(None, "chan"),
            P("chan"),
            P("chan", None),
            P("chan"),
            P("chan"),
            P("chan", "row", "col"),
        ),
        out_specs=(
            P("chan", "row", "col"),
            P("chan", "row", "col"),
            P(None, "chan"),
            P("chan", None),
        ),
        check_vma=False,
    )
```

profile of v0, /device:TPU:1, one launch (start us, length us, event | category | flops | bytes accessed | tf_op | source)
XLA Modules:
  0.0 604.0 jit_solution(2574440720858553044)
XLA Ops:
  11.4 6.2 %collective-permute-start.12 = (bf16[64,4,2,16]{0,3,2,1:T(8,128)(2,1)S(1)}, bf16[64,4,2,16]{0,3,2,1:T(8,128)(2,1)S(1)}, u32[]{:S(2)}, u32[]{:S(2)}) collective-permute-start(bf16[64,4,2,16]{0,3,2,1:T(8,128)(2,1)S(1)} %fusion.226), channel_id=1, source_target_pairs={{0,32},{32,64},{64,96},{1,33},{33,65},{65,97},{2,34},{34,66},{66,9... | collective-permute-start | bytes 49160 | tf_op jit(solution)/shard_map/ppermute | solution.py:18
  17.6 1.9 collective-permute-start.13
  19.6 5.1 collective-permute-start.8
  24.7 1.9 collective-permute-start.9
  26.7 5.1 collective-permute-start.4
  33.7 3.5 collective-permute-start.14
  38.5 2.3 collective-permute-start
  45.0 1.9 collective-permute-start.5
  47.0 1.9 collective-permute-done.1
  48.9 3.4 collective-permute-start.2
  53.7 4.0 collective-permute-start.10
  59.3 3.0 collective-permute-done.11
  63.4 3.4 collective-permute-start.6
  68.5 2.8 collective-permute-done.7
  71.8 3.6 fusion.73
  76.8 3.4 add_convert_fusion.1
  80.7 26.3 %all-reduce.1 = (f32[2048]{0:T(1024)S(1)}, f32[2048]{0:T(1024)S(1)}) all-reduce(f32[2048]{0:T(1024)S(1)} %bitcast.545, f32[2048]{0:T(1024)S(1)} %bitcast.544), channel_id=1, replica_groups=mesh['row'=4,'col'=4,'chan'=8] {'chan'}, use_global_device_ids=true, to_apply=%region_3.0 | all-reduce | flops 4096 | bytes 32768 | tf_op jit(solution)/shard_map/psum | solution.py:131
  107.1 2.2 add_convert_fusion
  109.2 1.9 copy.177
  111.2 56.5 %all-gather.3.cloned.1.call-done = bf16[512,2048]{1,0:T(8,128)(2,1)} async-done(((bf16[64,2048]{1,0:T(8,128)(2,1)}), bf16[512,2048]{1,0:T(8,128)(2,1)}) %all-gather.3.cloned.1.call-update) | async-done | bytes 2097168 | tf_op jit(solution)/shard_map/all_gather | solution.py:179
  167.7 7.9 %fusion.7 = (bf16[256,2048]{0,1:T(8,128)(2,1)}, f32[256,2048]{0,1:T(8,128)}) fusion(f32[256]{0:T(256)} %param.31, bf16[512,2048]{1,0:T(8,128)(2,1)} %all-gather.3.cloned.1.call-done, bf16[512,256]{1,0:T(8,128)(2,1)S(1)} %copy-done), kind=kOutput, calls=%fused_computation.13 | convolution fusion | flops 571473920 | bytes 5506048 | tf_op jit(solution)/shard_map/dot_general | solution.py:183
  175.6 2.0 fusion
  177.6 2.5 copy.197
  181.4 50.7 %reduce-scatter.7.cloned.1.call-done = bf16[64,2048]{1,0:T(8,128)(2,1)} async-done(((bf16[512,2048]{1,0:T(8,128)(2,1)}), bf16[64,2048]{1,0:T(8,128)(2,1)}) %reduce-scatter.7.cloned.1.call-update) | async-done | bytes 262160
  235.7 51.7 %all-gather.5.cloned.1.call-done = bf16[512,2048]{1,0:T(8,128)(2,1)} async-done(((bf16[64,2048]{1,0:T(8,128)(2,1)}), bf16[512,2048]{1,0:T(8,128)(2,1)}) %all-gather.5.cloned.1.call-update) | async-done | bytes 2097168 | tf_op jit(solution)/shard_map/all_gather | solution.py:180
  287.4 3.5 convolution_convert_fusion.2
  290.9 2.8 fusion.4
  295.3 2.0 fusion.1
  297.2 2.5 copy.199
  302.7 130.8 %all-reduce.5.cloned.1.call-done = (bf16[512,256]{1,0:T(8,128)(2,1)}, bf16[256,512]{1,0:T(8,128)(2,1)}) async-done(((bf16[512,256]{1,0:T(8,128)(2,1)}, bf16[256,512]{1,0:T(8,128)(2,1)}), (bf16[512,256]{1,0:T(8,128)(2,1)}, bf16[256,512]{1,0:T(8,128)(2,1)})) %all-reduce.5.cloned.1.call-update) | async-done | bytes 524304 | tf_op jit(solution)/shard_map/psum | solution.py:211
  437.0 53.2 %reduce-scatter.9.cloned.1.call-done = bf16[64,2048]{1,0:T(8,128)(2,1)} async-done(((bf16[512,2048]{1,0:T(8,128)(2,1)}), bf16[64,2048]{1,0:T(8,128)(2,1)}) %reduce-scatter.9.cloned.1.call-update) | async-done | bytes 262160
  492.8 26.4 %all-reduce = (f32[2048]{0:T(1024)S(1)}, f32[2048]{0:T(1024)S(1)}) all-reduce(f32[2048]{0:T(1024)S(1)} %get-tuple-element.65, f32[2048]{0:T(1024)S(1)} %get-tuple-element.64), channel_id=1, replica_groups=mesh['row'=4,'col'=4,'chan'=8] {'chan'}, use_global_device_ids=true, to_apply=%region_9.0 | all-reduce | flops 4096 | bytes 32768 | tf_op jit(solution)/shard_map/psum | solution.py:131
  522.7 12.4 %collective-permute-start.28 = (bf16[64,4,2,16]{0,3,2,1:T(8,128)(2,1)S(1)}, bf16[64,4,2,16]{0,3,2,1:T(8,128)(2,1)S(1)}, u32[]{:S(2)}, u32[]{:S(2)}) collective-permute-start(bf16[64,4,2,16]{0,3,2,1:T(8,128)(2,1)S(1)} %fusion.227), channel_id=1, source_target_pairs={{0,32},{32,64},{64,96},{1,33},{33,65},{65,97},{2,34},{34,66},{66,9... | collective-permute-start | bytes 49160 | tf_op jit(solution)/shard_map/ppermute | solution.py:18
  535.1 1.9 collective-permute-start.29
  537.2 5.1 collective-permute-start.16
  542.3 1.9 collective-permute-start.17
  544.3 5.1 collective-permute-start.24
  549.5 3.2 collective-permute-start.30
  554.0 1.9 collective-permute-start.25
  557.1 4.0 collective-permute-start.20
  562.4 1.9 collective-permute-start.21
  564.4 4.0 collective-permute-start.18
  569.7 4.0 collective-permute-start.26
  575.3 2.9 collective-permute-done.27
  579.6 3.2 collective-permute-start.22
  584.6 2.8 collective-permute-done.23
  587.9 3.5 fusion.22
  593.1 3.4 fusion.21
  (404 shorter events, 49.4 us)
Async XLA Ops:
  7.2 160.6 %copy-start = (bf16[512,256]{1,0:T(8,128)(2,1)S(1)}, bf16[512,256]{1,0:T(8,128)(2,1)}, u32[]{:S(2)}) copy-start(bf16[512,256]{1,0:T(8,128)(2,1)} %param.30) | copy-start | bytes 786436
  7.2 160.6 %all-gather.3.cloned.1.call-start = ((), (), s32[]{:S(2)}) async-start(), calls=%async_computation.2 | async-start | bytes 2359296 | tf_op jit(solution)/shard_map/all_gather | solution.py:179
  11.4 22.2 %collective-permute-start.12 = (bf16[64,4,2,16]{0,3,2,1:T(8,128)(2,1)S(1)}, bf16[64,4,2,16]{0,3,2,1:T(8,128)(2,1)S(1)}, u32[]{:S(2)}, u32[]{:S(2)}) collective-permute-start(bf16[64,4,2,16]{0,3,2,1:T(8,128)(2,1)S(1)} %fusion.226), channel_id=1, source_target_pairs={{0,32},{32,64},{64,96},{1,33},{33,65},{65,97},{2,34},{34,66},{66,9... | collective-permute-start | bytes 49160 | tf_op jit(solution)/shard_map/ppermute | solution.py:18
  17.6 16.0 %collective-permute-start.13 = (bf16[64,4,2,16]{0,3,2,1:T(8,128)(2,1)S(1)}, bf16[64,4,2,16]{0,3,2,1:T(8,128)(2,1)S(1)}, u32[]{:S(2)}, u32[]{:S(2)}) collective-permute-start(bf16[64,4,2,16]{0,3,2,1:T(8,128)(2,1)S(1)} %fusion.226), channel_id=1, source_target_pairs={{32,0},{64,32},{96,64},{33,1},{65,33},{97,65},{34,2},{66,34},{98,6... | collective-permute-start | bytes 49160 | tf_op jit(solution)/shard_map/ppermute | solution.py:21
  19.6 32.7 %collective-permute-start.8 = (bf16[64,4,2,32]{0,3,2,1:T(8,128)(2,1)S(1)}, bf16[64,4,2,32]{0,3,2,1:T(8,128)(2,1)S(1)}, u32[]{:S(2)}, u32[]{:S(2)}) collective-permute-start(bf16[64,4,2,32]{0,3,2,1:T(8,128)(2,1)S(1)} %get-tuple-element.163), channel_id=1, source_target_pairs={{0,32},{32,64},{64,96},{1,33},{33,65},{65,97},{2,34},{34,66},{66,9... | collective-permute-start | bytes 98312 | tf_op jit(solution)/shard_map/ppermute | solution.py:18
  24.7 28.9 %collective-permute-start.9 = (bf16[64,4,2,32]{0,3,2,1:T(8,128)(2,1)S(1)}, bf16[64,4,2,32]{0,3,2,1:T(8,128)(2,1)S(1)}, u32[]{:S(2)}, u32[]{:S(2)}) collective-permute-start(bf16[64,4,2,32]{0,3,2,1:T(8,128)(2,1)S(1)} %get-tuple-element.164), channel_id=1, source_target_pairs={{32,0},{64,32},{96,64},{33,1},{65,33},{97,65},{34,2},{66,34},{98,6... | collective-permute-start | bytes 98312 | tf_op jit(solution)/shard_map/ppermute | solution.py:21
  26.7 36.6 %collective-permute-start.4 = (bf16[64,4,2,64]{0,3,2,1:T(8,128)(2,1)S(1)}, bf16[64,4,2,64]{0,3,2,1:T(8,128)(2,1)S(1)}, u32[]{:S(2)}, u32[]{:S(2)}) collective-permute-start(bf16[64,4,2,64]{0,3,2,1:T(8,128)(2,1)S(1)} %get-tuple-element.122), channel_id=1, source_target_pairs={{0,32},{32,64},{64,96},{1,33},{33,65},{65,97},{2,34},{34,66},{66,9... | collective-permute-start | bytes 196616 | tf_op jit(solution)/shard_map/ppermute | solution.py:18
  33.7 4.9 collective-permute-start.14
  37.2 4.6 collective-permute-start.15
  38.5 6.5 %collective-permute-start = (bf16[64,1,2,128]{0,3,2,1:T(8,128)(2,1)S(1)}, bf16[64,1,2,128]{0,3,2,1:T(8,128)(2,1)S(1)}, u32[]{:S(2)}, u32[]{:S(2)}) collective-permute-start(bf16[64,1,2,128]{0,3,2,1:T(8,128)(2,1)S(1)} %get-tuple-element.120), channel_id=1, source_target_pairs={{0,32},{32,64},{64,96},{1,33},{33,65},{65,97},{2,34},{34,66},{66,9... | collective-permute-start | bytes 98312 | tf_op jit(solution)/shard_map/ppermute | solution.py:18
  41.8 7.1 %collective-permute-start.1 = (bf16[64,1,2,128]{0,3,2,1:T(8,128)(2,1)S(1)}, bf16[64,1,2,128]{0,3,2,1:T(8,128)(2,1)S(1)}, u32[]{:S(2)}, u32[]{:S(2)}) collective-permute-start(bf16[64,1,2,128]{0,3,2,1:T(8,128)(2,1)S(1)} %get-tuple-element.121), channel_id=1, source_target_pairs={{32,0},{64,32},{96,64},{33,1},{65,33},{97,65},{34,2},{66,34},{98,6... | collective-permute-start | bytes 98312 | tf_op jit(solution)/shard_map/ppermute | solution.py:21
  45.0 18.2 %collective-permute-start.5 = (bf16[64,4,2,64]{0,3,2,1:T(8,128)(2,1)S(1)}, bf16[64,4,2,64]{0,3,2,1:T(8,128)(2,1)S(1)}, u32[]{:S(2)}, u32[]{:S(2)}) collective-permute-start(bf16[64,4,2,64]{0,3,2,1:T(8,128)(2,1)S(1)} %get-tuple-element.123), channel_id=1, source_target_pairs={{32,0},{64,32},{96,64},{33,1},{65,33},{97,65},{34,2},{66,34},{98,6... | collective-permute-start | bytes 196616 | tf_op jit(solution)/shard_map/ppermute | solution.py:21
  48.9 8.8 %collective-permute-start.2 = (bf16[64,1,20,2]{0,3,2,1:T(2,128)(2,1)S(1)}, bf16[64,1,20,2]{0,3,2,1:T(2,128)(2,1)S(1)}, u32[]{:S(2)}, u32[]{:S(2)}) collective-permute-start(bf16[64,1,20,2]{0,3,2,1:T(2,128)(2,1)S(1)} %get-tuple-element.114), channel_id=1, source_target_pairs={{0,8},{8,16},{16,24},{1,9},{9,17},{17,25},{2,10},{10,18},{18,26},{... | collective-permute-start | bytes 15368 | tf_op jit(solution)/shard_map/ppermute | solution.py:18
  52.3 6.7 %collective-permute-start.3 = (bf16[64,1,20,2]{0,3,2,1:T(2,128)(2,1)S(1)}, bf16[64,1,20,2]{0,3,2,1:T(2,128)(2,1)S(1)}, u32[]{:S(2)}, u32[]{:S(2)}) collective-permute-start(bf16[64,1,20,2]{0,3,2,1:T(2,128)(2,1)S(1)} %get-tuple-element.115), channel_id=1, source_target_pairs={{8,0},{16,8},{24,16},{9,1},{17,9},{25,17},{10,2},{18,10},{26,18},{... | collective-permute-start | bytes 15368 | tf_op jit(solution)/shard_map/ppermute | solution.py:21
  53.7 5.6 collective-permute-start.10
  57.7 4.5 collective-permute-start.11
  63.4 5.1 collective-permute-start.6
  66.7 4.6 collective-permute-start.7
  111.2 120.9 %reduce-scatter.7.cloned.1.call-start = ((), (), s32[]{:S(2)}) async-start(), calls=%async_computation.4 | async-start | bytes 2359296
  180.1 53.3 %copy-start.116 = (f32[64]{0:T(128)S(1)}, f32[64]{0:T(128)}, u32[]{:S(2)}) copy-start(f32[64]{0:T(128)} %param.34) | copy-start | bytes 772
  180.1 53.3 %copy-start.117 = (f32[64]{0:T(128)S(1)}, f32[64]{0:T(128)}, u32[]{:S(2)}) copy-start(f32[64]{0:T(128)} %param.33) | copy-start | bytes 772
  180.1 107.3 %all-gather.5.cloned.1.call-start = ((), (), s32[]{:S(2)}) async-start(), calls=%async_computation.3 | async-start | bytes 2359296 | tf_op jit(solution)/shard_map/all_gather | solution.py:180
  235.4 55.5 %copy-start.4 = (bf16[256,512]{1,0:T(8,128)(2,1)S(1)}, bf16[256,512]{1,0:T(8,128)(2,1)}, u32[]{:S(2)}) copy-start(bf16[256,512]{1,0:T(8,128)(2,1)} %param.32) | copy-start | bytes 786436
  235.4 198.0 %all-reduce.5.cloned.1.call-start = ((), (), s32[]{:S(2)}) async-start(), calls=%async_computation.6 | async-start | bytes 1048576 | tf_op jit(solution)/shard_map/psum | solution.py:211
  295.2 195.0 %reduce-scatter.9.cloned.1.call-start = ((), (), s32[]{:S(2)}) async-start(), calls=%async_computation.5 | async-start | bytes 2359296
  299.8 191.7 %copy-start.88 = (f32[64]{0:T(128)S(1)}, f32[64]{0:T(128)}, u32[]{:S(2)}) copy-start(f32[64]{0:T(128)} %param.28) | copy-start | bytes 772
  522.3 38.8 %copy-start.59 = (f32[64,4]{0,1:T(4,128)S(1)}, f32[64,4]{0,1:T(4,128)}, u32[]{:S(2)}) copy-start(f32[64,4]{0,1:T(4,128)} %copy-done.58) | copy-start | bytes 3076
  522.3 38.8 %copy-start.61 = (f32[64,4]{0,1:T(4,128)S(1)}, f32[64,4]{0,1:T(4,128)}, u32[]{:S(2)}) copy-start(f32[64,4]{0,1:T(4,128)} %copy-done.60) | copy-start | bytes 3076
  522.4 38.8 %copy-start.63 = (f32[64,4]{0,1:T(4,128)S(1)}, f32[64,4]{0,1:T(4,128)}, u32[]{:S(2)}) copy-start(f32[64,4]{0,1:T(4,128)} %copy-done.62) | copy-start | bytes 3076
  522.4 38.8 %copy-start.65 = (f32[64,4]{0,1:T(4,128)S(1)}, f32[64,4]{0,1:T(4,128)}, u32[]{:S(2)}) copy-start(f32[64,4]{0,1:T(4,128)} %copy-done.64) | copy-start | bytes 3076
  522.4 38.8 %copy-start.67 = (f32[64,4]{0,1:T(4,128)S(1)}, f32[64,4]{0,1:T(4,128)}, u32[]{:S(2)}) copy-start(f32[64,4]{0,1:T(4,128)} %copy-done.66) | copy-start | bytes 3076
  522.4 38.8 %copy-start.69 = (f32[64,4]{0,1:T(4,128)S(1)}, f32[64,4]{0,1:T(4,128)}, u32[]{:S(2)}) copy-start(f32[64,4]{0,1:T(4,128)} %copy-done.68) | copy-start | bytes 3076
  522.7 26.8 %collective-permute-start.28 = (bf16[64,4,2,16]{0,3,2,1:T(8,128)(2,1)S(1)}, bf16[64,4,2,16]{0,3,2,1:T(8,128)(2,1)S(1)}, u32[]{:S(2)}, u32[]{:S(2)}) collective-permute-start(bf16[64,4,2,16]{0,3,2,1:T(8,128)(2,1)S(1)} %fusion.227), channel_id=1, source_target_pairs={{0,32},{32,64},{64,96},{1,33},{33,65},{65,97},{2,34},{34,66},{66,9... | collective-permute-start | bytes 49160 | tf_op jit(solution)/shard_map/ppermute | solution.py:18
  535.1 14.3 %collective-permute-start.29 = (bf16[64,4,2,16]{0,3,2,1:T(8,128)(2,1)S(1)}, bf16[64,4,2,16]{0,3,2,1:T(8,128)(2,1)S(1)}, u32[]{:S(2)}, u32[]{:S(2)}) collective-permute-start(bf16[64,4,2,16]{0,3,2,1:T(8,128)(2,1)S(1)} %fusion.227), channel_id=1, source_target_pairs={{32,0},{64,32},{96,64},{33,1},{65,33},{97,65},{34,2},{66,34},{98,6... | collective-permute-start | bytes 49160 | tf_op jit(solution)/shard_map/ppermute | solution.py:21
  537.2 25.2 %collective-permute-start.16 = (bf16[64,1,2,128]{0,3,2,1:T(8,128)(2,1)S(1)}, bf16[64,1,2,128]{0,3,2,1:T(8,128)(2,1)S(1)}, u32[]{:S(2)}, u32[]{:S(2)}) collective-permute-start(bf16[64,1,2,128]{0,3,2,1:T(8,128)(2,1)S(1)} %get-tuple-element.116), channel_id=1, source_target_pairs={{0,32},{32,64},{64,96},{1,33},{33,65},{65,97},{2,34},{34,66},{66,9... | collective-permute-start | bytes 98312 | tf_op jit(solution)/shard_map/ppermute | solution.py:18
  542.3 22.0 %collective-permute-start.17 = (bf16[64,1,2,128]{0,3,2,1:T(8,128)(2,1)S(1)}, bf16[64,1,2,128]{0,3,2,1:T(8,128)(2,1)S(1)}, u32[]{:S(2)}, u32[]{:S(2)}) collective-permute-start(bf16[64,1,2,128]{0,3,2,1:T(8,128)(2,1)S(1)} %get-tuple-element.117), channel_id=1, source_target_pairs={{32,0},{64,32},{96,64},{33,1},{65,33},{97,65},{34,2},{66,34},{98,6... | collective-permute-start | bytes 98312 | tf_op jit(solution)/shard_map/ppermute | solution.py:21
  544.3 24.1 %collective-permute-start.24 = (bf16[64,4,2,32]{0,3,2,1:T(8,128)(2,1)S(1)}, bf16[64,4,2,32]{0,3,2,1:T(8,128)(2,1)S(1)}, u32[]{:S(2)}, u32[]{:S(2)}) collective-permute-start(bf16[64,4,2,32]{0,3,2,1:T(8,128)(2,1)S(1)} %get-tuple-element.161), channel_id=1, source_target_pairs={{0,32},{32,64},{64,96},{1,33},{33,65},{65,97},{2,34},{34,66},{66,9... | collective-permute-start | bytes 98312 | tf_op jit(solution)/shard_map/ppermute | solution.py:18
  549.5 4.5 collective-permute-start.30
  552.7 4.4 collective-permute-start.31
  554.0 15.7 %collective-permute-start.25 = (bf16[64,4,2,32]{0,3,2,1:T(8,128)(2,1)S(1)}, bf16[64,4,2,32]{0,3,2,1:T(8,128)(2,1)S(1)}, u32[]{:S(2)}, u32[]{:S(2)}) collective-permute-start(bf16[64,4,2,32]{0,3,2,1:T(8,128)(2,1)S(1)} %get-tuple-element.162), channel_id=1, source_target_pairs={{32,0},{64,32},{96,64},{33,1},{65,33},{97,65},{34,2},{66,34},{98,6... | collective-permute-start | bytes 98312 | tf_op jit(solution)/shard_map/ppermute | solution.py:21
  557.1 22.4 %collective-permute-start.20 = (bf16[64,4,2,64]{0,3,2,1:T(8,128)(2,1)S(1)}, bf16[64,4,2,64]{0,3,2,1:T(8,128)(2,1)S(1)}, u32[]{:S(2)}, u32[]{:S(2)}) collective-permute-start(bf16[64,4,2,64]{0,3,2,1:T(8,128)(2,1)S(1)} %get-tuple-element.118), channel_id=1, source_target_pairs={{0,32},{32,64},{64,96},{1,33},{33,65},{65,97},{2,34},{34,66},{66,9... | collective-permute-start | bytes 196616 | tf_op jit(solution)/shard_map/ppermute | solution.py:18
  562.4 17.1 %collective-permute-start.21 = (bf16[64,4,2,64]{0,3,2,1:T(8,128)(2,1)S(1)}, bf16[64,4,2,64]{0,3,2,1:T(8,128)(2,1)S(1)}, u32[]{:S(2)}, u32[]{:S(2)}) collective-permute-start(bf16[64,4,2,64]{0,3,2,1:T(8,128)(2,1)S(1)} %get-tuple-element.119), channel_id=1, source_target_pairs={{32,0},{64,32},{96,64},{33,1},{65,33},{97,65},{34,2},{66,34},{98,6... | collective-permute-start | bytes 196616 | tf_op jit(solution)/shard_map/ppermute | solution.py:21
  564.4 9.4 %collective-permute-start.18 = (bf16[64,1,20,2]{0,3,2,1:T(2,128)(2,1)S(1)}, bf16[64,1,20,2]{0,3,2,1:T(2,128)(2,1)S(1)}, u32[]{:S(2)}, u32[]{:S(2)}) collective-permute-start(bf16[64,1,20,2]{0,3,2,1:T(2,128)(2,1)S(1)} %get-tuple-element.112), channel_id=1, source_target_pairs={{0,8},{8,16},{16,24},{1,9},{9,17},{17,25},{2,10},{10,18},{18,26},{... | collective-permute-start | bytes 15368 | tf_op jit(solution)/shard_map/ppermute | solution.py:18
  568.4 6.7 %collective-permute-start.19 = (bf16[64,1,20,2]{0,3,2,1:T(2,128)(2,1)S(1)}, bf16[64,1,20,2]{0,3,2,1:T(2,128)(2,1)S(1)}, u32[]{:S(2)}, u32[]{:S(2)}) collective-permute-start(bf16[64,1,20,2]{0,3,2,1:T(2,128)(2,1)S(1)} %get-tuple-element.113), channel_id=1, source_target_pairs={{8,0},{16,8},{24,16},{9,1},{17,9},{25,17},{10,2},{18,10},{26,18},{... | collective-permute-start | bytes 15368 | tf_op jit(solution)/shard_map/ppermute | solution.py:21
  569.7 5.5 collective-permute-start.26
  573.7 4.5 collective-permute-start.27
  579.6 5.0 collective-permute-start.22
  582.8 4.6 collective-permute-start.23
  (109 other events, 1761.9 us)
Sparse Core Ops, SparseCore 0:
  111.3 56.3 all-gather.2
  180.2 51.8 reduce-scatter.6
  235.5 51.8 all-gather.4
  295.3 138.0 all-reduce.4
  435.8 54.3 reduce-scatter.8
where the time goes:
time: 608 us; the launch traced here: 604 us
  waiting for transfers between devices  359 us (59%)
  starting transfers between devices  101 us (17%)
  blocking collectives  52.7 us (9%)
  other arithmetic  32.9 us (5%)
  local copies, waits for them, and re-layouts  22.7 us (4%)
  matrix products  19.5 us (3%)
  between operations  16.8 us (3%)
    psum x1, waiting for transfers between devices, on_device(): lax.psum(part_in.astype(jnp.bfloat16), ('row', 'col')).astype(jnp.float32)  131 us
    unnamed x7, waiting for transfers between devices  104 us
    ppermute x16, starting transfers between devices, padded_2(): lax.ppermute(lax.slice_in_dim(block, block.shape[dim] - width, None, axis...  74 us
    all_gather x1, waiting for transfers between devices, on_device(): lax.all_gather(normed_loc, 'chan', axis=0, tiled=True)  56.5 us
    psum x2, blocking collectives, channel_sums(): return lax.psum((first_sum, other_sum), 'chan')  52.7 us
    all_gather x1, waiting for transfers between devices, on_device(): lax.all_gather(scaled, 'chan', axis=0, tiled=True)  51.7 us
    ppermute x16, starting transfers between devices, padded_2(): lax.ppermute(lax.slice_in_dim(block, 0, width, axis=dim), axis, backward)  26.1 us
    ppermute x16, waiting for transfers between devices, padded_2(): lax.ppermute(lax.slice_in_dim(block, 0, width, axis=dim), axis, backward)  15.7 us
  transfers between devices with their start and end apart: 37, of which 12 were waited for; matrix products, arithmetic and copies ran while one was open for 3% of the time, Pallas kernels for 0%

commit v1 on v0

v1 whole, which is shorter than its diff:
```python
import jax
import jax.numpy as jnp
from jax import lax
from jax.experimental import pallas as pl
from jax.experimental.pallas import tpu as pltpu
from jax.sharding import Mesh, PartitionSpec as P

EPSILON = 1e-06
INV_ROOT_TWO = 0.7071067811865476
INV_ROOT_TWO_PI = 0.3989422804014327
F32 = jnp.float32
BF16 = jnp.bfloat16

CHANS = 512
PLANES = 4
HALVES = 2
SUB = PLANES * HALVES
ROWS = 32
COLS = 512
BAND = 256
SPOTS = HALVES * BAND
HID = 256
GROUP = 16
X = 4
Y = 2
VMEM_LIMIT = 48 * 1024 * 1024


def lanes(width=COLS):
    return lax.broadcasted_iota(jnp.int32, (SUB, width), 1)


def sublanes(width=COLS):
    return lax.broadcasted_iota(jnp.int32, (SUB, width), 0)


def turn(value, shift):
    return pltpu.roll(value, shift % value.shape[1], 1)


def pair_lanes(value, step, lane):
    return jnp.where((lane & step) == 0, value + turn(value, -step), turn(value, step) - value)


def fill_edges(ref, rows):
    low = sublanes() < PLANES
    for edge in range(2):
        ref[edge] = jnp.where(low, 0.0, pltpu.roll(ref[rows + edge], PLANES, 0))
        ref[rows + 2 + edge] = jnp.where(low, pltpu.roll(ref[2 + edge], PLANES, 0), 0.0)


def convolve(source, rows, step, taps, first, mirrored, shifted, target, start):
    lane = lanes()

    def shift_row(row, carry):
        value = source[row]
        for move in range(5):
            offset = (move - 2) * step
            if offset == 0:
                shifted[move, row] = value
            else:
                kept = (lane < COLS - offset) if offset > 0 else (lane >= -offset)
                shifted[move, row] = jnp.where(kept, turn(value, -offset), 0.0)
        return carry

    lax.fori_loop(0, rows + 4, shift_row, 0)
    chunk = min(rows, 8)

    def do_chunk(index, carry):
        base = index * chunk
        for block in range(COLS // 128):
            cols = slice(block * 128, block * 128 + 128)
            sums = [None] * chunk
            for move in range(5):
                coefs = []
                for tap_row in range(5):
                    place = tap_row * 5 + move
                    coefs.append(taps[first + (24 - place if mirrored else place)])
                for row in range(chunk + 4):
                    value = shifted[move, base + row, :, cols]
                    for tap_row in range(5):
                        out = row - tap_row
                        if 0 <= out < chunk:
                            term = coefs[tap_row] * value
                            sums[out] = term if sums[out] is None else sums[out] + term
            for row in range(chunk):
                target[start + base + row, :, cols] = sums[row]
        return carry

    lax.fori_loop(0, rows // chunk, do_chunk, 0)


def wavelet(plane, taps, mirrored, shifted, level_1, level_2, level_3, conv_0, conv_1, conv_2, conv_3):
    lane = lanes()
    fill_edges(plane, ROWS)

    def split_1(row, carry):
        upper, lower = plane[2 + 2 * row], plane[3 + 2 * row]
        level_1[0, 2 + row] = pair_lanes(0.5 * (upper + lower), 1, lane)
        level_1[1, 2 + row] = pair_lanes(0.5 * (upper - lower), 1, lane)
        return carry

    lax.fori_loop(0, ROWS // 2, split_1, 0)
    fill_edges(level_1.at[0], ROWS // 2)
    fill_edges(level_1.at[1], ROWS // 2)

    for source, target, rows, step in ((level_1.at[0], level_2, ROWS // 4, 2), (level_2, level_3, ROWS // 8, 4)):
        for row in range(rows):
            upper, lower = source[2 + 2 * row], source[3 + 2 * row]
            across = pair_lanes(0.5 * (upper + lower), step, lane)
            down = pair_lanes(0.5 * (upper - lower), step, lane)
            target[2 + row] = jnp.where((lane & (step - 1)) == 0, across, turn(down, 1))
        fill_edges(target, rows)

    convolve(plane, ROWS, 1, taps, 0, mirrored, shifted, conv_0, 0)
    convolve(level_1.at[0], ROWS // 2, 2, taps, 25, mirrored, shifted, conv_1.at[0], 0)
    convolve(level_1.at[1], ROWS // 2, 2, taps, 50, mirrored, shifted, conv_1.at[1], 0)
    convolve(level_2, ROWS // 4, 4, taps, 75, mirrored, shifted, conv_2, 0)
    convolve(level_3, ROWS // 8, 8, taps, 100, mirrored, shifted, conv_3, 0)

    for source, target, rows, step in ((conv_3, conv_2, ROWS // 8, 4), (conv_2, conv_1.at[0], ROWS // 4, 2)):
        for row in range(rows):
            kept = source[row]
            moved = turn(kept, -1)
            for half, value in ((0, kept + moved), (1, kept - moved)):
                merged = pair_lanes(0.5 * value, step, lane)
                place = 2 * row + half
                target[place] = target[place] + jnp.where((lane & (step - 1)) == 0, merged, 0.0)


def merged_rows(row, conv_1, lane):
    across, down = conv_1[0, row], conv_1[1, row]
    return pair_lanes(0.5 * (across + down), 1, lane), pair_lanes(0.5 * (across - down), 1, lane)


def tile_in(tiles, first, row_block, col):
    parts = [tiles[(2 * half + row_block) * 4 + col, first : first + PLANES].astype(F32) for half in range(HALVES)]
    return jnp.swapaxes(jnp.concatenate(parts, 0), 0, 1)


def forward_kernel(
    tiles, taps, shift, scale, sent, plane, shifted, level_1, level_2, level_3, conv_0, conv_1, conv_2, conv_3, second
):
    for row_block in range(2):
        for col in range(4):
            cols = slice(col * 128, col * 128 + 128)
            plane[2 + row_block * 16 : 18 + row_block * 16, :, cols] = tile_in(tiles, 0, row_block, col)
            second[row_block * 16 : 16 + row_block * 16, :, cols] = tile_in(tiles, PLANES, row_block, col)
    wavelet(plane, taps, False, shifted, level_1, level_2, level_3, conv_0, conv_1, conv_2, conv_3)
    lane = lanes()
    bias, layer = shift[...], scale[...]

    def finish(pair, carry):
        rows = merged_rows(pair, conv_1, lane)
        for half in range(2):
            row = 2 * pair + half
            mixed = conv_0[row] + bias + rows[half]
            scaled = layer * second[row]
            both = jnp.concatenate([mixed, scaled], 0).astype(BF16)
            for band in range(COLS // BAND):
                block = 2 * row + band
                part = both[:, band * BAND : band * BAND + BAND]
                for twin in range(Y):
                    sent[block // GROUP, twin, block % GROUP] = part
        return carry

    lax.fori_loop(0, ROWS // 2, finish, 0)


def backward_kernel(
    parts, tiles, taps, scale, shift, sent, plane, shifted, level_1, level_2, level_3, conv_0, conv_1, conv_2, conv_3, second
):
    def gather(block, carry):
        both = parts[block // GROUP, 0, block % GROUP].astype(F32) + parts[block // GROUP, 1, block % GROUP].astype(F32)
        cols = pl.ds(pl.multiple_of((block % 2) * BAND, BAND), BAND)
        second[block // 2, :, cols] = both[:SUB]
        plane[2 + block // 2, :, cols] = both[SUB:]
        return carry

    lax.fori_loop(0, 2 * ROWS, gather, 0)
    wavelet(plane, taps, True, shifted, level_1, level_2, level_3, conv_0, conv_1, conv_2, conv_3)
    lane = lanes()

    def finish(pair, carry):
        rows = merged_rows(pair, conv_1, lane)
        for half in range(2):
            row = 2 * pair + half
            conv_0[row] = conv_0[row] + rows[half]
        return carry

    lax.fori_loop(0, ROWS // 2, finish, 0)
    layer, bias = scale[...], shift[...]
    for row_block in range(2):
        for col in range(4):
            cols = slice(col * 128, col * 128 + 128)
            rows = slice(row_block * 16, row_block * 16 + 16)
            projected = layer[:, cols] * (second[rows, :, cols] + bias[:, cols])
            output = tile_in(tiles, 0, row_block, col) + projected
            grad = tile_in(tiles, PLANES, row_block, col) + conv_0[rows, :, cols]
            for first, value in ((0, output), (PLANES, grad)):
                turned = jnp.swapaxes(value, 0, 1).astype(BF16)
                for half in range(HALVES):
                    place = (2 * half + row_block) * 4 + col
                    sent[place, first : first + PLANES] = turned[half * PLANES : half * PLANES + PLANES]


def plane_scratch():
    return [
        pltpu.VMEM((ROWS + 4, SUB, COLS), F32),
        pltpu.VMEM((5, ROWS + 4, SUB, COLS), F32),
        pltpu.VMEM((2, ROWS // 2 + 4, SUB, COLS), F32),
        pltpu.VMEM((ROWS // 4 + 4, SUB, COLS), F32),
        pltpu.VMEM((ROWS // 8 + 4, SUB, COLS), F32),
        pltpu.VMEM((ROWS, SUB, COLS), F32),
        pltpu.VMEM((2, ROWS // 2, SUB, COLS), F32),
        pltpu.VMEM((ROWS // 4, SUB, COLS), F32),
        pltpu.VMEM((ROWS // 8, SUB, COLS), F32),
        pltpu.VMEM((ROWS, SUB, COLS), F32),
    ]


def regroup(first, second, low):
    return (
        jnp.where(low, first, pltpu.roll(second, PLANES, 0)),
        jnp.where(low, pltpu.roll(first, PLANES, 0), second),
    )


def dot(left, right, left_dim, right_dim):
    return lax.dot_general(left, right, (((left_dim,), (right_dim,)), ((), ())), preferred_element_type=F32)


def mlp_kernel(
    order, received, pack_0, pack_1, pack_2, pack_3, biases, gain, bias, sent, weight_sums, mixed, scaled, projected, grads
):
    low = sublanes(BAND) < PLANES

    def arrange(index, carry):
        rows = pl.ds(pl.multiple_of(index * 16, 16), 16)
        for half in range(HALVES):
            cols = slice(half * BAND, half * BAND + BAND)
            pieces = []
            for pair in range(2):
                one = received[4 * index + 2 * pair].astype(F32)
                two = received[4 * index + 2 * pair + 1].astype(F32)
                pieces.append((regroup(one[:SUB], two[:SUB], low)[half], regroup(one[SUB:], two[SUB:], low)[half]))
            mixed[rows, cols] = jnp.concatenate([pieces[0][0], pieces[1][0]], 0)
            scaled[rows, cols] = jnp.concatenate([pieces[0][1], pieces[1][1]], 0).astype(BF16)
        return carry

    lax.fori_loop(0, CHANS // 16, arrange, 0)
    values = mixed[...]
    average = jnp.sum(values, 0, keepdims=True) / CHANS
    rescale = lax.rsqrt(jnp.sum(values * values, 0, keepdims=True) / CHANS - average * average + EPSILON)
    gains = gain[...]
    normed = (((values - average) * rescale) * gains + bias[...]).astype(BF16)
    normed_turned = normed.T
    scaled_now = scaled[...]
    scaled_turned = scaled_now.T
    for index, pack in enumerate((pack_0, pack_1, pack_2, pack_3)):
        w_in, w_out = pack[:CHANS], pack[CHANS : 2 * CHANS]
        hidden = dot(normed_turned, w_in, 1, 0) + biases[index : index + 1]
        spread = 0.5 * (1.0 + lax.erf(hidden * INV_ROOT_TWO))
        activated = (hidden * spread).astype(BF16)
        slope = spread + hidden * jnp.exp(-0.5 * hidden * hidden) * INV_ROOT_TWO_PI
        grad_hidden = (dot(scaled_turned, w_out, 1, 0) * slope).astype(BF16)
        part = dot(w_out, activated, 1, 1)
        projected[...] = part if index == 0 else projected[...] + part
        part = dot(w_in, grad_hidden, 1, 1)
        grads[...] = part if index == 0 else grads[...] + part
        owner = order[0] ^ index
        for arr, value in ((0, dot(normed, grad_hidden, 1, 0)), (1, dot(scaled_now, activated, 1, 0))):
            rounded = value.astype(BF16)
            for piece in range(GROUP):
                weight_sums[owner, piece, arr] = rounded[piece * 32 : piece * 32 + 32]
    weighted = grads[...] * gains
    centred = (mixed[...] - average) * rescale
    sum_one = jnp.sum(weighted, 0, keepdims=True) / CHANS
    sum_two = jnp.sum(weighted * centred, 0, keepdims=True) / CHANS
    grads[...] = rescale * (weighted - sum_one - centred * sum_two)

    def hand_out(index, carry):
        rows = pl.ds(pl.multiple_of(index * 8, 8), 8)
        halves = []
        for ref in (projected, grads):
            value = ref[rows]
            halves.append(regroup(value[:, :BAND], value[:, BAND:], low))
        for place in range(2):
            sent[2 * index + place] = jnp.concatenate([halves[0][place], halves[1][place]], 0).astype(BF16)
        return carry

    lax.fori_loop(0, CHANS // 8, hand_out, 0)


def call(kernel, outs, scratch, ops, smem_first=False):
    spaces = [pl.BlockSpec(memory_space=pltpu.VMEM) for _ in ops]
    if smem_first:
        spaces[0] = pl.BlockSpec(memory_space=pltpu.SMEM)
    out_spaces = jax.tree.map(lambda _: pl.BlockSpec(memory_space=pltpu.VMEM), outs)
    return pl.pallas_call(
        kernel,
        out_shape=outs,
        in_specs=spaces,
        out_specs=out_spaces,
        scratch_shapes=scratch,
        compiler_params=pltpu.CompilerParams(vmem_limit_bytes=VMEM_LIMIT),
    )(*ops)


def three_parts(value):
    high = lax.reduce_precision(value, 8, 7)
    middle = lax.reduce_precision(value - high, 8, 7)
    return [part.astype(BF16) for part in (high, middle, value - high - middle)]


def own_planes(array, dim, place):
    return lax.dynamic_slice_in_dim(array, place * PLANES, PLANES, dim)


def over_halves(array):
    return jnp.concatenate([array, array], -2)


def tap_table(base_kernel, base_scale, wave_kernels, wave_scale):
    base = (base_scale[:, None, None] * base_kernel).reshape(PLANES, 25).T[:, :, None]
    waves = (wave_scale[..., None, None] * wave_kernels).reshape(3, PLANES, 4, 25).transpose(0, 2, 3, 1)[..., None]
    lane = jnp.arange(128)[None, None, :]

    def choose(level, period, bands):
        table = jnp.zeros((25, PLANES, 128), F32)
        for residue, band in bands:
            table = jnp.where(lane % period == residue, waves[level, band], table)
        return table

    tables = [
        jnp.broadcast_to(base, (25, PLANES, 128)),
        choose(0, 2, ((0, 0), (1, 1))),
        choose(0, 2, ((0, 2), (1, 3))),
        choose(1, 4, ((0, 0), (2, 1), (1, 2), (3, 3))),
        choose(2, 8, ((0, 0), (4, 1), (1, 2), (5, 3))),
    ]
    return over_halves(jnp.concatenate(tables, 0))


def on_device(
    feature_map,
    base_kernel,
    base_bias,
    base_scale,
    wave_kernels,
    wave_scale,
    norm_gain,
    norm_bias,
    w_in,
    b_in,
    w_out,
    b_out,
    layer_scale,
    cotangent,
):
    group = ("row", "col")
    everyone = ("x", "y", "row", "col")
    place = lax.axis_index("row") * 4 + lax.axis_index("col")
    x_here = lax.axis_index("x")
    y_here = lax.axis_index("y")

    norms = jnp.stack(three_parts(jnp.concatenate([norm_gain, norm_bias])))
    other = lax.ppermute(norms, "y", [(0, 1), (1, 0)])
    norms = jnp.concatenate([jnp.where(y_here == 0, norms, other), jnp.where(y_here == 0, other, norms)], 1)
    pack = jnp.concatenate(
        [w_in, w_out.T, jnp.stack(three_parts(b_in)), norms, jnp.zeros((10, HID), BF16)], 0
    )
    packs = [pack] + [lax.ppermute(pack, "x", [(i, i ^ step) for i in range(X)]) for step in range(1, X)]

    tiles = jnp.concatenate(
        [feature_map.reshape(GROUP, PLANES, 16, 128), cotangent.reshape(GROUP, PLANES, 16, 128)], 1
    )
    tiles = lax.all_to_all(tiles, group, split_axis=0, concat_axis=0, tiled=True)

    scale_own = own_planes(base_scale, 0, place)
    taps = tap_table(
        own_planes(base_kernel, 0, place),
        scale_own,
        own_planes(wave_kernels, 1, place),
        own_planes(wave_scale, 1, place),
    )

    def rows_of(vector):
        return over_halves(jnp.broadcast_to(vector[:, None], (PLANES, COLS)))

    layer = rows_of(own_planes(layer_scale, 0, place))
    sent = call(
        forward_kernel,
        jax.ShapeDtypeStruct((X, Y, GROUP, 2 * SUB, BAND), BF16),
        plane_scratch(),
        (tiles, taps, rows_of(scale_own * own_planes(base_bias, 0, place)), layer),
    )
    received = lax.all_to_all(
        sent.reshape(X * Y * GROUP, 2 * SUB, BAND), everyone, split_axis=0, concat_axis=0, tiled=True
    )

    extras = jnp.stack([one[2 * CHANS : 2 * CHANS + 6] for one in packs]).astype(F32)
    biases = extras[:, 0] + extras[:, 1] + extras[:, 2]
    vectors = (extras[:, 3] + extras[:, 4] + extras[:, 5])[x_here ^ jnp.arange(X)]
    vectors = vectors.reshape(X, Y, 2, CHANS // (X * Y)).transpose(2, 0, 1, 3).reshape(2, CHANS, 1)

    sent, weight_sums = call(
        mlp_kernel,
        (
            jax.ShapeDtypeStruct((X * Y * GROUP, 2 * SUB, BAND), BF16),
            jax.ShapeDtypeStruct((X, GROUP, 2, 32, HID), BF16),
        ),
        [
            pltpu.VMEM((CHANS, SPOTS), F32),
            pltpu.VMEM((CHANS, SPOTS), BF16),
            pltpu.VMEM((CHANS, SPOTS), F32),
            pltpu.VMEM((CHANS, SPOTS), F32),
        ],
        (x_here.astype(jnp.int32).reshape(1), received, *packs, biases, vectors[0], vectors[1]),
        smem_first=True,
    )
    received = lax.all_to_all(sent, everyone, split_axis=0, concat_axis=0, tiled=True)
    sent = call(
        backward_kernel,
        jax.ShapeDtypeStruct((GROUP, 2 * PLANES, 16, 128), BF16),
        plane_scratch(),
        (
            received.reshape(X, Y, GROUP, 2 * SUB, BAND),
            tiles,
            taps,
            layer,
            rows_of(own_planes(b_out, 0, place)),
        ),
    )
    results = lax.all_to_all(sent, group, split_axis=0, concat_axis=0, tiled=True)
    output_map = results[:, :PLANES].reshape(feature_map.shape)
    grad_map = results[:, PLANES:].reshape(feature_map.shape)

    pieces = lax.all_to_all(
        weight_sums.reshape(X * GROUP, 2, 32, HID), ("x", "row", "col"), split_axis=0, concat_axis=0, tiled=True
    )
    piece = jnp.sum(pieces.astype(F32), 0).astype(BF16)
    wholes = lax.all_to_all(
        jnp.broadcast_to(piece, (GROUP,) + piece.shape), group, split_axis=0, concat_axis=0, tiled=True
    )
    factor = 1.0 / (64.0 * 512.0) ** 0.5
    grad_in = wholes[:, 0].reshape(CHANS, HID).astype(F32) * factor
    grad_out = wholes[:, 1].reshape(CHANS, HID).T.astype(F32) * factor
    return (output_map, grad_map, grad_in, grad_out)


def solution(mesh):
    grid = Mesh(mesh.devices.reshape(4, 4, X, Y), ("row", "col", "x", "y"))
    chan = ("x", "y")
    return jax.shard_map(
        on_device,
        mesh=grid,
        in_specs=(
            P(chan, "row", "col"),
            P(chan, None, None),
            P(chan),
            P(chan),
            P(None, chan, None, None, None),
            P(None, chan, None),
            P(chan),
            P(chan),
            P(None, chan),
            P(chan),
            P(chan, None),
            P(chan),
            P(chan),
            P(chan, "row", "col"),
        ),
        out_specs=(
            P(chan, "row", "col"),
            P(chan, "row", "col"),
            P(None, chan),
            P(chan, None),
        ),
        check_vma=False,
    )
```

time: 608 us -> 170 us (0.28)
  waiting for transfers between devices: 359 us -> 53.9 us
  starting transfers between devices: 101 us -> 34.9 us
  Pallas kernels: 0 us -> 39.9 us
  blocking collectives: 52.7 us -> 23.3 us
  other arithmetic: 32.9 us -> 6.76 us
  matrix products: 19.5 us -> 0 us
  between operations: 16.8 us -> 1.01 us
  local copies, waits for them, and re-layouts: 22.7 us -> 9.77 us
    psum x1 -> x0, waiting for transfers between devices: 131 us -> none  [on_device(): lax.psum(part_in.astype(jnp.bfloat16), ('row', 'col')).astype(jnp.float32)]
    all_gather x2 -> x0, waiting for transfers between devices: 108 us -> none  [the longest x1 56.5 us: on_device(): lax.all_gather(normed_loc, 'chan', axis=0, tiled=True)]
    unnamed x7 -> x0, waiting for transfers between devices: 104 us -> none
    ppermute x32 -> x4, starting transfers between devices: 100 us -> 6.33 us  [the longest x3 4.12 us: on_device(): lax.ppermute(pack, 'x', [(i, i ^ step) for i in range(X)])]
    all_to_all x0 -> x5, waiting for transfers between devices: none -> 53.9 us  [the longest x1 16.4 us: on_device(): lax.all_to_all(sent.reshape(X * Y * GROUP, 2 * SUB, BAND), everyone, spli...]
    psum x2 -> x0, blocking collectives: 52.7 us -> none  [channel_sums(): return lax.psum((first_sum, other_sum), 'chan')]
    pallas_call x0 -> x3, Pallas kernels: none -> 39.9 us  [call(): pl.pallas_call(kernel, out_shape=outs, in_specs=spaces, out_specs=out_spa...]
    all_to_all x0 -> x5, starting transfers between devices: none -> 28.6 us  [the longest x1 8.75 us: on_device(): lax.all_to_all(tiles, group, split_axis=0, concat_axis=0, tiled=True)]
  transfers between devices with their start and end apart: 37 -> 9, of which waited for: 12 -> 5; matrix products, arithmetic and copies ran while one was open for 3% -> 7% of each run, Pallas kernels for 0% -> 19%
where the time goes in v1:
time: 170 us
  waiting for transfers between devices  53.9 us (32%)
  Pallas kernels  39.9 us (23%)
  starting transfers between devices  34.9 us (21%)
  blocking collectives  23.3 us (14%)
  local copies, waits for them, and re-layouts  9.77 us (6%)
  other arithmetic  6.76 us (4%)
    pallas_call x3, Pallas kernels, call(): pl.pallas_call(kernel, out_shape=outs, in_specs=spaces, out_specs=out_spa...  39.9 us
    all_to_all x1, blocking collectives, on_device(): lax.all_to_all(sent, everyone, split_axis=0, concat_axis=0, tiled=True)  23.3 us
    all_to_all x1, waiting for transfers between devices, on_device(): lax.all_to_all(sent.reshape(X * Y * GROUP, 2 * SUB, BAND), everyone, spli...  16.4 us
    all_to_all x1, waiting for transfers between devices, on_device(): lax.all_to_all(weight_sums.reshape(X * GROUP, 2, 32, HID), ('x', 'row', '...  13.2 us
    all_to_all x1, waiting for transfers between devices, on_device(): lax.all_to_all(jnp.broadcast_to(piece, (GROUP,) + piece.shape), group, sp...  10.9 us
    all_to_all x1, waiting for transfers between devices, on_device(): lax.all_to_all(sent, group, split_axis=0, concat_axis=0, tiled=True)  9.82 us
    all_to_all x1, starting transfers between devices, on_device(): lax.all_to_all(tiles, group, split_axis=0, concat_axis=0, tiled=True)  8.75 us
    all_to_all x1, starting transfers between devices, on_device(): lax.all_to_all(sent.reshape(X * Y * GROUP, 2 * SUB, BAND), everyone, spli...  6.22 us
  transfers between devices with their start and end apart: 9, of which 5 were waited for; matrix products, arithmetic and copies ran while one was open for 7% of the time, Pallas kernels for 19%

profile of v1, /device:TPU:1, one launch (start us, length us, event | category | flops | bytes accessed | tf_op | source)
XLA Modules:
  0.0 169.6 jit_solution(12154981094765150592)
XLA Ops:
  0.7 0.8 reduce-precision_convert_fusion.3
  1.6 2.2 %collective-permute-start = (bf16[3,128]{1,0:T(4,128)(2,1)S(1)}, bf16[3,128]{1,0:T(4,128)(2,1)S(1)}, u32[]{:S(2)}, u32[]{:S(2)}) collective-permute-start(bf16[3,128]{1,0:T(4,128)(2,1)S(1)} %pad_maximum_fusion.6), channel_id=1, source_target_pairs={{0,1},{1,0},{2,3},{3,2},{4,5},{5,4},{6,7},{7,6},{8,9},{9,8},{10,11... | collective-permute-start | bytes 2312 | tf_op jit(solution)/shard_map/ppermute | solution.py:368
  3.8 1.9 %pad_maximum_fusion = bf16[16,8,16,128]{3,2,1,0:T(8,128)(2,1)} fusion(bf16[16,4,16,128]{3,2,1,0:T(8,128)(2,1)} %bitcast.75, bf16[16,4,16,128]{3,2,1,0:T(8,128)(2,1)} %bitcast.76), kind=kLoop, calls=%fused_computation.1 | loop fusion | flops 262144 | bytes 1048576 | tf_op jit(solution)/shard_map/concatenate | solution.py:375
  5.6 8.8 %all-to-all-start = ((bf16[16,8,16,128]{3,2,1,0:T(8,128)(2,1)}), bf16[16,8,16,128]{3,2,1,0:T(8,128)(2,1)S(1)}, u32[]{:S(2)}, u32[]{:S(2)}) async-start(bf16[16,8,16,128]{3,2,1,0:T(8,128)(2,1)} %pad_maximum_fusion), calls=%async_computation | async-start | bytes 1048576 | tf_op jit(solution)/shard_map/all_to_all | solution.py:378
  14.6 0.1 dynamic-slice_multiply_fusion
  14.7 0.2 copy.160
  14.9 0.1 copy.161
  15.0 0.1 copy.162
  15.2 0.1 copy.184
  15.5 0.1 copy.159
  15.7 0.1 copy.163
  15.8 0.1 copy.164
  15.9 0.1 copy.165
  16.3 0.1 copy.169
  16.7 0.1 select_dynamic-update-slice_fusion.3
  16.9 0.1 select_dynamic-update-slice_fusion.2
  17.0 0.2 select_dynamic-update-slice_fusion.1
  17.2 0.2 select_dynamic-update-slice_fusion
  17.4 0.1 copy.173
  17.7 0.3 concatenate.67.pack_0
  18.0 1.3 collective-permute-start.1
  19.6 2.5 %collective-permute-start.2 = (bf16[1040,256]{1,0:T(8,128)(2,1)S(1)}, bf16[1040,256]{1,0:T(8,128)(2,1)}, u32[]{:S(2)}, u32[]{:S(2)}) collective-permute-start(bf16[1040,256]{1,0:T(8,128)(2,1)S(1)} %concatenate.67.pack_0), channel_id=1, source_target_pairs={{0,4},{2,6},{4,0},{6,2},{1,5},{3,7},{5,1},{7,3},{8,12},{10,14},{12... | collective-permute-start | bytes 1597448 | tf_op jit(solution)/shard_map/ppermute | solution.py:373
  22.2 0.3 collective-permute-start.3
  22.5 3.6 %all-to-all-done.tiles = bf16[16,8,16,128]{3,2,1,0:T(8,128)(2,1)S(1)} async-done(((bf16[16,8,16,128]{3,2,1,0:T(8,128)(2,1)}), bf16[16,8,16,128]{3,2,1,0:T(8,128)(2,1)S(1)}, u32[]{:S(2)}, u32[]{:S(2)}) %all-to-all-start) | async-done | bytes 524320 | tf_op jit(solution)/shard_map/all_to_all | solution.py:378
  26.1 15.5 %shard_map.165 = bf16[4,2,16,16,256]{4,3,2,1,0:T(8,128)(2,1)} custom-call(bf16[16,8,16,128]{3,2,1,0:T(8,128)(2,1)S(1)} %all-to-all-done.tiles, f32[125,8,128]{2,1,0:T(8,128)S(1)} %pad_maximum_fusion.1.taps, f32[8,512]{1,0:T(8,128)S(1)} %get-tuple-element.73.shift, f32[8,512]{1,0:T(8,128)S(1)} %get-tuple-element.74.scale), custom_call_target="tpu_custom_call" | custom-call | tf_op jit(solution)/shard_map/pallas_call | solution.py:300
  41.6 6.2 %all-to-all-start.1 = ((bf16[128,16,256]{2,1,0:T(8,128)(2,1)}), bf16[128,16,256]{2,1,0:T(8,128)(2,1)S(1)}, u32[]{:S(2)}, u32[]{:S(2)}) async-start(bf16[128,16,256]{2,1,0:T(8,128)(2,1)} %bitcast.20), calls=%async_computation.1 | async-start | bytes 2097152 | tf_op jit(solution)/shard_map/all_to_all | solution.py:398
  47.8 0.8 copy-done.1
  48.6 0.7 slice_bitcast_fusion.3
  49.3 0.7 slice_bitcast_fusion.2
  50.0 0.6 gather_fusion
  50.7 0.2 squeeze.6.gain
  50.9 0.2 squeeze.7.bias
  51.1 16.4 %all-to-all-done.1.received = bf16[128,16,256]{2,1,0:T(8,128)(2,1)S(1)} async-done(((bf16[128,16,256]{2,1,0:T(8,128)(2,1)}), bf16[128,16,256]{2,1,0:T(8,128)(2,1)S(1)}, u32[]{:S(2)}, u32[]{:S(2)}) %all-to-all-start.1) | async-done | bytes 1048608 | tf_op jit(solution)/shard_map/all_to_all | solution.py:398
  67.5 1.0 copy-done.2
  68.6 7.9 %shard_map.166 = (bf16[128,16,256]{2,1,0:T(8,128)(2,1)S(1)}, bf16[4,16,2,32,256]{4,3,2,1,0:T(8,128)(2,1)}) custom-call(s32[1]{0:T(128)} %bitcast.order, bf16[128,16,256]{2,1,0:T(8,128)(2,1)S(1)} %all-to-all-done.1.received, bf16[1040,256]{1,0:T(8,128)(2,1)S(1)} %concatenate.67.pack_0, bf16[1040,256]{1,0:T(8,128)(2,1)S(1)} %copy-done.2, ...), custom_call_target="tpu_custom_call" | custom-call | tf_op jit(solution)/shard_map/pallas_call | solution.py:300
  76.5 23.3 %all_to_all.30 = bf16[128,16,256]{2,1,0:T(8,128)(2,1)S(1)} all-to-all(bf16[128,16,256]{2,1,0:T(8,128)(2,1)S(1)} %get-tuple-element.6), channel_id=1, replica_groups=mesh['row'=4,'col'=4,'x'=4,'y'=2] {'x','y','row','col'}, dimensions={0} | all-to-all | bytes 2097152 | tf_op jit(solution)/shard_map/all_to_all | solution.py:422
  99.8 5.7 %all-to-all-start.4 = ((bf16[64,2,32,256]{3,2,1,0:T(8,128)(2,1)}), bf16[64,2,32,256]{3,2,1,0:T(8,128)(2,1)}, u32[]{:S(2)}, u32[]{:S(2)}) async-start(bf16[64,2,32,256]{3,2,1,0:T(8,128)(2,1)} %bitcast.71), calls=%async_computation.4 | async-start | bytes 4194304 | tf_op jit(solution)/shard_map/all_to_all | solution.py:439
  105.6 16.5 %shard_map.167 = bf16[16,8,16,128]{3,2,1,0:T(8,128)(2,1)} custom-call(bf16[4,2,16,16,256]{4,3,2,1,0:T(8,128)(2,1)S(1)} %bitcast.69, bf16[16,8,16,128]{3,2,1,0:T(8,128)(2,1)S(1)} %all-to-all-done.tiles, f32[125,8,128]{2,1,0:T(8,128)S(1)} %pad_maximum_fusion.1.taps, f32[8,512]{1,0:T(8,128)S(1)} %get-tuple-element.74.scale, f32[8,512]{1,0:T(8,128)S(1)} %pad_maximum_fusion.4.shift), custom_call_target="tpu_custom_call" | custom-call | tf_op jit(solution)/shard_map/pallas_call | solution.py:300
  122.2 13.2 %all-to-all-done.4 = bf16[64,2,32,256]{3,2,1,0:T(8,128)(2,1)} async-done(((bf16[64,2,32,256]{3,2,1,0:T(8,128)(2,1)}), bf16[64,2,32,256]{3,2,1,0:T(8,128)(2,1)}, u32[]{:S(2)}, u32[]{:S(2)}) %all-to-all-start.4) | async-done | bytes 2097184 | tf_op jit(solution)/shard_map/all_to_all | solution.py:439
  135.3 4.0 %all-to-all-start.3 = ((bf16[16,8,16,128]{3,2,1,0:T(8,128)(2,1)}), bf16[16,8,16,128]{3,2,1,0:T(8,128)(2,1)S(1)}, u32[]{:S(2)}, u32[]{:S(2)}) async-start(bf16[16,8,16,128]{3,2,1,0:T(8,128)(2,1)} %shard_map.167), calls=%async_computation.3 | async-start | bytes 1048576 | tf_op jit(solution)/shard_map/all_to_all | solution.py:435
  139.4 1.9 %reduce_sum.12 = bf16[2,32,256]{2,1,0:T(8,128)(2,1)S(1)} reduce(bf16[64,2,32,256]{3,2,1,0:T(8,128)(2,1)} %all-to-all-done.4, bf16[]{:T(256)} %constant.101.clone.1), dimensions={0}, to_apply=%region_0.1 | reduce | flops 1032192 | bytes 2129922 | tf_op jit(solution)/shard_map/reduce_sum | solution.py:442
  141.3 9.8 %all-to-all-done.3 = bf16[16,8,16,128]{3,2,1,0:T(8,128)(2,1)S(1)} async-done(((bf16[16,8,16,128]{3,2,1,0:T(8,128)(2,1)}), bf16[16,8,16,128]{3,2,1,0:T(8,128)(2,1)S(1)}, u32[]{:S(2)}, u32[]{:S(2)}) %all-to-all-start.3) | async-done | bytes 524320 | tf_op jit(solution)/shard_map/all_to_all | solution.py:435
  151.1 0.9 broadcast_in_dim.227
  152.0 3.9 %all-to-all-start.5 = ((bf16[16,2,32,256]{3,2,1,0:T(8,128)(2,1)}), bf16[16,2,32,256]{3,2,1,0:T(8,128)(2,1)S(1)}, u32[]{:S(2)}, u32[]{:S(2)}) async-start(bf16[16,2,32,256]{3,2,1,0:T(8,128)(2,1)} %broadcast_in_dim.227), calls=%async_computation.5 | async-start | bytes 1048576 | tf_op jit(solution)/shard_map/all_to_all | solution.py:443
  155.9 0.8 fusion.7
  156.7 10.9 %all-to-all-done.5 = bf16[16,2,32,256]{3,2,1,0:T(8,128)(2,1)S(1)} async-done(((bf16[16,2,32,256]{3,2,1,0:T(8,128)(2,1)}), bf16[16,2,32,256]{3,2,1,0:T(8,128)(2,1)S(1)}, u32[]{:S(2)}, u32[]{:S(2)}) %all-to-all-start.5) | async-done | bytes 524320 | tf_op jit(solution)/shard_map/all_to_all | solution.py:443
  167.7 0.9 convert_multiply_fusion
  168.6 1.0 copy.183
  (74 shorter events, 1.9 us)
Async XLA Ops:
  0.6 14.4 %copy-start = (f32[64,5,5]{0,2,1:T(8,128)S(1)}, f32[64,5,5]{0,2,1:T(8,128)}, u32[]{:S(2)}) copy-start(f32[64,5,5]{0,2,1:T(8,128)} %param.15) | copy-start | bytes 19204
  0.7 13.8 %copy-start.7 = (f32[256]{0:T(256)S(1)}, f32[256]{0:T(256)}, u32[]{:S(2)}) copy-start(f32[256]{0:T(256)} %param.23) | copy-start | bytes 3076
  0.7 13.8 %copy-start.6 = (f32[3,64,4]{1,2,0:T(4,128)S(1)}, f32[3,64,4]{1,2,0:T(4,128)}, u32[]{:S(2)}) copy-start(f32[3,64,4]{1,2,0:T(4,128)} %param.19) | copy-start | bytes 9220
  0.7 13.9 %copy-start.5 = (f32[3,64,4,5,5]{1,2,4,3,0:T(4,128)S(1)}, f32[3,64,4,5,5]{1,2,4,3,0:T(4,128)}, u32[]{:S(2)}) copy-start(f32[3,64,4,5,5]{1,2,4,3,0:T(4,128)} %param.18) | copy-start | bytes 230404
  0.7 14.6 %copy-start.8 = (f32[64]{0:T(128)S(1)}, f32[64]{0:T(128)}, u32[]{:S(2)}) copy-start(f32[64]{0:T(128)} %param.16) | copy-start | bytes 772
  0.7 14.6 %copy-start.9 = (f32[64]{0:T(128)S(1)}, f32[64]{0:T(128)}, u32[]{:S(2)}) copy-start(f32[64]{0:T(128)} %param.17) | copy-start | bytes 772
  0.7 16.7 %copy-start.4 = (bf16[256,512]{1,0:T(8,128)(2,1)S(1)}, bf16[256,512]{1,0:T(8,128)(2,1)}, u32[]{:S(2)}) copy-start(bf16[256,512]{1,0:T(8,128)(2,1)} %param.24) | copy-start | bytes 786436
  0.7 16.9 %copy-start.3 = (bf16[512,256]{1,0:T(8,128)(2,1)S(1)}, bf16[512,256]{1,0:T(8,128)(2,1)}, u32[]{:S(2)}) copy-start(bf16[512,256]{1,0:T(8,128)(2,1)} %param.22) | copy-start | bytes 786436
  1.6 16.0 %collective-permute-start = (bf16[3,128]{1,0:T(4,128)(2,1)S(1)}, bf16[3,128]{1,0:T(4,128)(2,1)S(1)}, u32[]{:S(2)}, u32[]{:S(2)}) collective-permute-start(bf16[3,128]{1,0:T(4,128)(2,1)S(1)} %pad_maximum_fusion.6), channel_id=1, source_target_pairs={{0,1},{1,0},{2,3},{3,2},{4,5},{5,4},{6,7},{7,6},{8,9},{9,8},{10,11... | collective-permute-start | bytes 2312 | tf_op jit(solution)/shard_map/ppermute | solution.py:368
  5.6 13.7 %copy-start.10 = (f32[64]{0:T(128)S(1)}, f32[64]{0:T(128)}, u32[]{:S(2)}) copy-start(f32[64]{0:T(128)} %param.26) | copy-start | bytes 772
  5.6 20.5 %all-to-all-start = ((bf16[16,8,16,128]{3,2,1,0:T(8,128)(2,1)}), bf16[16,8,16,128]{3,2,1,0:T(8,128)(2,1)S(1)}, u32[]{:S(2)}, u32[]{:S(2)}) async-start(bf16[16,8,16,128]{3,2,1,0:T(8,128)(2,1)} %pad_maximum_fusion), calls=%async_computation | async-start | bytes 1048576 | tf_op jit(solution)/shard_map/all_to_all | solution.py:378
  18.0 29.8 %collective-permute-start.1 = (bf16[1040,256]{1,0:T(8,128)(2,1)S(1)}, bf16[1040,256]{1,0:T(8,128)(2,1)S(1)}, u32[]{:S(2)}, u32[]{:S(2)}) collective-permute-start(bf16[1040,256]{1,0:T(8,128)(2,1)S(1)} %concatenate.67.pack_0), channel_id=1, source_target_pairs={{0,2},{2,0},{4,6},{6,4},{1,3},{3,1},{5,7},{7,5},{8,10},{10,8},{12,... | collective-permute-start | bytes 1597448 | tf_op jit(solution)/shard_map/ppermute | solution.py:373
  19.6 29.1 %collective-permute-start.2 = (bf16[1040,256]{1,0:T(8,128)(2,1)S(1)}, bf16[1040,256]{1,0:T(8,128)(2,1)}, u32[]{:S(2)}, u32[]{:S(2)}) collective-permute-start(bf16[1040,256]{1,0:T(8,128)(2,1)S(1)} %concatenate.67.pack_0), channel_id=1, source_target_pairs={{0,4},{2,6},{4,0},{6,2},{1,5},{3,7},{5,1},{7,3},{8,12},{10,14},{12... | collective-permute-start | bytes 1597448 | tf_op jit(solution)/shard_map/ppermute | solution.py:373
  22.2 27.1 %collective-permute-start.3 = (bf16[1040,256]{1,0:T(8,128)(2,1)S(1)}, bf16[1040,256]{1,0:T(8,128)(2,1)}, u32[]{:S(2)}, u32[]{:S(2)}) collective-permute-start(bf16[1040,256]{1,0:T(8,128)(2,1)S(1)} %concatenate.67.pack_0), channel_id=1, source_target_pairs={{0,6},{2,4},{4,2},{6,0},{1,7},{3,5},{5,3},{7,1},{8,14},{10,12},{12... | collective-permute-start | bytes 1597448 | tf_op jit(solution)/shard_map/ppermute | solution.py:373
  41.6 25.9 %all-to-all-start.1 = ((bf16[128,16,256]{2,1,0:T(8,128)(2,1)}), bf16[128,16,256]{2,1,0:T(8,128)(2,1)S(1)}, u32[]{:S(2)}, u32[]{:S(2)}) async-start(bf16[128,16,256]{2,1,0:T(8,128)(2,1)} %bitcast.20), calls=%async_computation.1 | async-start | bytes 2097152 | tf_op jit(solution)/shard_map/all_to_all | solution.py:398
  47.8 0.8 copy-start.1
  67.5 1.0 copy-start.2
  99.8 5.7 %copy-start.11 = (f32[64]{0:T(128)S(1)}, f32[64]{0:T(128)}, u32[]{:S(2)}) copy-start(f32[64]{0:T(128)} %param.25) | copy-start | bytes 772
  99.8 35.5 %all-to-all-start.4 = ((bf16[64,2,32,256]{3,2,1,0:T(8,128)(2,1)}), bf16[64,2,32,256]{3,2,1,0:T(8,128)(2,1)}, u32[]{:S(2)}, u32[]{:S(2)}) async-start(bf16[64,2,32,256]{3,2,1,0:T(8,128)(2,1)} %bitcast.71), calls=%async_computation.4 | async-start | bytes 4194304 | tf_op jit(solution)/shard_map/all_to_all | solution.py:439
  135.3 15.8 %all-to-all-start.3 = ((bf16[16,8,16,128]{3,2,1,0:T(8,128)(2,1)}), bf16[16,8,16,128]{3,2,1,0:T(8,128)(2,1)S(1)}, u32[]{:S(2)}, u32[]{:S(2)}) async-start(bf16[16,8,16,128]{3,2,1,0:T(8,128)(2,1)} %shard_map.167), calls=%async_computation.3 | async-start | bytes 1048576 | tf_op jit(solution)/shard_map/all_to_all | solution.py:435
  152.0 15.7 %all-to-all-start.5 = ((bf16[16,2,32,256]{3,2,1,0:T(8,128)(2,1)}), bf16[16,2,32,256]{3,2,1,0:T(8,128)(2,1)S(1)}, u32[]{:S(2)}, u32[]{:S(2)}) async-start(bf16[16,2,32,256]{3,2,1,0:T(8,128)(2,1)} %broadcast_in_dim.227), calls=%async_computation.5 | async-start | bytes 1048576 | tf_op jit(solution)/shard_map/all_to_all | solution.py:443

commit v2 on v1

v2 whole, which is shorter than its diff:
```python
import jax
import jax.numpy as jnp
from jax import lax
from jax.experimental import pallas as pl
from jax.experimental.pallas import tpu as pltpu
from jax.sharding import Mesh, PartitionSpec as P

EPSILON = 1e-06
INV_ROOT_TWO = 0.7071067811865476
INV_ROOT_TWO_PI = 0.3989422804014327
F32 = jnp.float32
BF16 = jnp.bfloat16

CHANS = 512
PLANES = 4
HALVES = 2
SUB = PLANES * HALVES
ROWS = 32
COLS = 512
LINE = 128
LINES = 4
SPOTS = LINES * LINE
HID = 256
GROUP = 16
X = 4
Y = 2
PLANE_VMEM = 12 * 1024 * 1024
MLP_VMEM = 56 * 1024 * 1024


def lanes(width=COLS):
    return lax.broadcasted_iota(jnp.int32, (SUB, width), 1)


def sublanes(width=COLS):
    return lax.broadcasted_iota(jnp.int32, (SUB, width), 0)


def turn(value, shift):
    return pltpu.roll(value, shift % value.shape[1], 1)


def pair_lanes(value, step, lane):
    return jnp.where((lane & step) == 0, value + turn(value, -step), turn(value, step) - value)


def loop(count, step, body):
    def some(index, carry):
        for inner in range(step):
            body(index * step + inner)
        return carry

    if count == step:
        some(0, 0)
    else:
        lax.fori_loop(0, count // step, some, 0)


def fill_edges(ref, rows):
    low = sublanes() < PLANES
    for edge in range(2):
        ref[edge] = jnp.where(low, 0.0, pltpu.roll(ref[rows + edge], PLANES, 0))
        ref[rows + 2 + edge] = jnp.where(low, pltpu.roll(ref[2 + edge], PLANES, 0), 0.0)


def convolve(source, rows, step, taps, first, mirrored, target):
    lane = lanes()
    chunk = 4

    def do_chunk(index):
        base = index * chunk
        totals = [None] * chunk
        for move in range(5):
            coefs = []
            for tap_row in range(5):
                place = tap_row * 5 + move
                coefs.append(taps[first + (24 - place if mirrored else place)])
            blocks = [[None] * (COLS // 128) for _ in range(chunk)]
            for block in range(COLS // 128):
                for row in range(chunk + 4):
                    value = source[base + row, :, block * 128 : block * 128 + 128]
                    for out in range(max(0, row - 4), min(chunk, row + 1)):
                        term = coefs[row - out] * value
                        blocks[out][block] = term if blocks[out][block] is None else blocks[out][block] + term
            offset = (move - 2) * step
            for out in range(chunk):
                summed = jnp.concatenate(blocks[out], 1)
                if offset:
                    kept = (lane < COLS - offset) if offset > 0 else (lane >= -offset)
                    summed = jnp.where(kept, turn(summed, -offset), 0.0)
                totals[out] = summed if totals[out] is None else totals[out] + summed
        for out in range(chunk):
            target[base + out] = totals[out]

    loop(rows // chunk, 1, do_chunk)


def wavelet(plane, taps, mirrored, level_1, level_2, level_3, conv_0, conv_1, conv_2, conv_3):
    lane = lanes()
    fill_edges(plane, ROWS)

    def split_1(row):
        upper, lower = plane[2 + 2 * row], plane[3 + 2 * row]
        level_1[0, 2 + row] = pair_lanes(0.5 * (upper + lower), 1, lane)
        level_1[1, 2 + row] = pair_lanes(0.5 * (upper - lower), 1, lane)

    loop(ROWS // 2, 4, split_1)
    fill_edges(level_1.at[0], ROWS // 2)
    fill_edges(level_1.at[1], ROWS // 2)

    for source, target, rows, step in ((level_1.at[0], level_2, ROWS // 4, 2), (level_2, level_3, ROWS // 8, 4)):
        for row in range(rows):
            upper, lower = source[2 + 2 * row], source[3 + 2 * row]
            across = pair_lanes(0.5 * (upper + lower), step, lane)
            down = pair_lanes(0.5 * (upper - lower), step, lane)
            target[2 + row] = jnp.where((lane & (step - 1)) == 0, across, turn(down, 1))
        fill_edges(target, rows)

    convolve(plane, ROWS, 1, taps, 0, mirrored, conv_0)
    convolve(level_1.at[0], ROWS // 2, 2, taps, 25, mirrored, conv_1.at[0])
    convolve(level_1.at[1], ROWS // 2, 2, taps, 50, mirrored, conv_1.at[1])
    convolve(level_2, ROWS // 4, 4, taps, 75, mirrored, conv_2)
    convolve(level_3, ROWS // 8, 8, taps, 100, mirrored, conv_3)

    for source, target, rows, step in ((conv_3, conv_2, ROWS // 8, 4), (conv_2, conv_1.at[0], ROWS // 4, 2)):
        for row in range(rows):
            kept = source[row]
            moved = turn(kept, -1)
            for half, value in ((0, kept + moved), (1, kept - moved)):
                merged = pair_lanes(0.5 * value, step, lane)
                place = 2 * row + half
                target[place] = target[place] + jnp.where((lane & (step - 1)) == 0, merged, 0.0)


def merged_rows(row, conv_1, lane):
    across, down = conv_1[0, row], conv_1[1, row]
    return pair_lanes(0.5 * (across + down), 1, lane), pair_lanes(0.5 * (across - down), 1, lane)


def tile_of(half, row_block, col):
    return (half * 4 + col) * 2 + row_block


def tile_in(tiles, row_block, col):
    parts = [tiles[tile_of(half, row_block, col)].astype(F32) for half in range(HALVES)]
    return jnp.swapaxes(jnp.concatenate(parts, 0), 0, 1)


def regroup(first, second, low):
    return (
        jnp.where(low, first, pltpu.roll(second, PLANES, 0)),
        jnp.where(low, pltpu.roll(first, PLANES, 0), second),
    )


def forward_kernel(tiles, taps, shift, sent, plane, level_1, level_2, level_3, conv_0, conv_1, conv_2, conv_3):
    for row_block in range(2):
        for col in range(4):
            cols = slice(col * LINE, col * LINE + LINE)
            plane[2 + row_block * 16 : 18 + row_block * 16, :, cols] = tile_in(tiles, row_block, col)
    wavelet(plane, taps, False, level_1, level_2, level_3, conv_0, conv_1, conv_2, conv_3)
    lane = lanes()
    bias = shift[...]
    low = sublanes(LINE) < PLANES

    def finish(group):
        rows = []
        for pair in range(LINES // 2):
            merged = merged_rows(2 * group + pair, conv_1, lane)
            for half in range(2):
                rows.append(conv_0[LINES * group + 2 * pair + half] + bias + merged[half])
        for col in range(4):
            cols = slice(col * LINE, col * LINE + LINE)
            pairs = [regroup(rows[q][:, cols], rows[q + 1][:, cols], low) for q in (0, 2)]
            for half in range(HALVES):
                block = jnp.concatenate([pairs[0][half], pairs[1][half]], 0).astype(BF16)
                for twin in range(Y):
                    sent[group % X, twin, tile_of(half, group // X, col)] = block

    loop(ROWS // LINES, 2, finish)


def backward_kernel(
    parts, tiles, taps, scale, shift, sent, plane, level_1, level_2, level_3, conv_0, conv_1, conv_2, conv_3, second
):
    low = sublanes(LINE) < PLANES

    def gather(group):
        for col in range(4):
            cols = slice(col * LINE, col * LINE + LINE)
            both = []
            for half in range(HALVES):
                place = tile_of(half, group // X, col)
                both.append(parts[group % X, 0, place].astype(F32) + parts[group % X, 1, place].astype(F32))
            for start, target, first in ((0, second, 0), (2 * SUB, plane, 2)):
                for pair in range(LINES // 2):
                    area = slice(start + pair * SUB, start + pair * SUB + SUB)
                    rows = regroup(both[0][area], both[1][area], low)
                    for half in range(2):
                        target[first + LINES * group + 2 * pair + half, :, cols] = rows[half]

    loop(ROWS // LINES, 2, gather)
    wavelet(plane, taps, True, level_1, level_2, level_3, conv_0, conv_1, conv_2, conv_3)
    lane = lanes()

    def finish(pair):
        rows = merged_rows(pair, conv_1, lane)
        for half in range(2):
            row = 2 * pair + half
            conv_0[row] = conv_0[row] + rows[half]

    loop(ROWS // 2, 4, finish)
    layer, bias = scale[...], shift[...]
    for row_block in range(2):
        for col in range(4):
            cols = slice(col * LINE, col * LINE + LINE)
            rows = slice(row_block * 16, row_block * 16 + 16)
            projected = layer[:, cols] * (second[rows, :, cols] + bias[:, cols])
            output = tile_in(tiles, row_block, col) + projected
            for first, value in ((0, output), (PLANES, conv_0[rows, :, cols])):
                turned = jnp.swapaxes(value, 0, 1).astype(BF16)
                for half in range(HALVES):
                    place = tile_of(half, row_block, col)
                    sent[place, first : first + PLANES] = turned[half * PLANES : half * PLANES + PLANES]


def plane_scratch():
    return [
        pltpu.VMEM((ROWS + 4, SUB, COLS), F32),
        pltpu.VMEM((2, ROWS // 2 + 4, SUB, COLS), F32),
        pltpu.VMEM((ROWS // 4 + 4, SUB, COLS), F32),
        pltpu.VMEM((ROWS // 8 + 4, SUB, COLS), F32),
        pltpu.VMEM((ROWS, SUB, COLS), F32),
        pltpu.VMEM((2, ROWS // 2, SUB, COLS), F32),
        pltpu.VMEM((ROWS // 4, SUB, COLS), F32),
        pltpu.VMEM((ROWS // 8, SUB, COLS), F32),
    ]


def dot(left, right, left_dim, right_dim):
    return lax.dot_general(left, right, (((left_dim,), (right_dim,)), ((), ())), preferred_element_type=F32)


def hidden_parts(pack, core, bias, normed_turned, scaled_turned):
    mine, others = pack[0, :CHANS], pack[1, :CHANS]
    w_in = jnp.where(core == 0, mine, others)
    w_out = jnp.where(core == 0, others, mine)
    w_out = jnp.concatenate([w_out[:HID], w_out[HID:]], 1).T
    hidden = dot(normed_turned, w_in, 1, 0) + bias
    spread = 0.5 * (1.0 + lax.erf(hidden * INV_ROOT_TWO))
    activated = (hidden * spread).astype(BF16)
    slope = spread + hidden * jnp.exp(-0.5 * hidden * hidden) * INV_ROOT_TWO_PI
    grad_hidden = (dot(scaled_turned, w_out, 1, 0) * slope).astype(BF16)
    return w_in, w_out, activated, grad_hidden


def mlp_kernel(
    order, biases, gain, bias, received_at, received_scaled_at,
    mine_0, mine_1, mine_2, mine_3, others_0, others_1, others_2, others_3, sent_at, kept_at, given_at,
    received, received_scaled, packs, mixed, scaled, projected, grads, sent, kept, given, arrived, left,
):
    halves = ((mine_0, others_0), (mine_1, others_1), (mine_2, others_2), (mine_3, others_3))
    sources = (received_at, received_scaled_at, *[half for pair in halves for half in pair])
    targets = (received, received_scaled, *[packs.at[index, half] for index in range(X) for half in range(2)])
    arrivals = [
        pltpu.make_async_copy(source, target, arrived.at[i]) for i, (source, target) in enumerate(zip(sources, targets))
    ]
    for copy in arrivals:
        copy.start()
    departures = []

    def depart(source, target):
        copy = pltpu.make_async_copy(source, target, left.at[len(departures)])
        copy.start()
        departures.append(copy)

    arrivals[0].wait()
    low = sublanes(LINE) < PLANES

    def arrange(index):
        for pair in range(2):
            one = received[4 * index + 2 * pair].astype(F32)
            two = received[4 * index + 2 * pair + 1].astype(F32)
            rows = pl.ds(pl.multiple_of(index * 16 + pair * SUB, SUB), SUB)
            for half in range(2):
                area = slice(half * SUB, half * SUB + SUB)
                lines = regroup(one[area], two[area], low)
                for line in range(2):
                    place = (2 * half + line) * LINE
                    mixed[rows, place : place + LINE] = lines[line]

    loop(CHANS // 16, 4, arrange)
    arrivals[1].wait()
    share = CHANS // (X * Y)
    for block in range(X * Y):
        for line in range(LINES):
            scaled[block * share : block * share + share, line * LINE : line * LINE + LINE] = received_scaled[block, line]
    values = mixed[...]
    average = jnp.sum(values, 0, keepdims=True) / CHANS
    rescale = lax.rsqrt(jnp.sum(values * values, 0, keepdims=True) / CHANS - average * average + EPSILON)
    gains = gain[...]
    normed = (((values - average) * rescale) * gains + bias[...]).astype(BF16)
    scaled_now = scaled[...]
    normed_turned, scaled_turned = normed.T, scaled_now.T
    for index in range(X):
        arrivals[2 + 2 * index].wait()
        arrivals[3 + 2 * index].wait()
        w_in, w_out, activated, grad_hidden = hidden_parts(
            packs.at[index], order[1], biases[index : index + 1], normed_turned, scaled_turned
        )
        part = dot(w_out, activated, 1, 1)
        projected[...] = part if index == 0 else projected[...] + part
        part = dot(w_in, grad_hidden, 1, 1)
        grads[...] = part if index == 0 else grads[...] + part
        owner = order[0] ^ index
        for arr, value in ((0, dot(normed, grad_hidden, 1, 0)), (1, dot(scaled_now, activated, 1, 0))):
            rounded = value.astype(BF16)
            for piece in range(GROUP // 2):
                first, second = rounded[piece * 64 : piece * 64 + 32], rounded[piece * 64 + 32 : piece * 64 + 64]
                for part in range(4):
                    cut = (slice(part % 2 * 16, part % 2 * 16 + 16), slice(part // 2 * 128, part // 2 * 128 + 128))
                    kept[owner, piece, arr * 4 + part] = jnp.where(order[1] == 0, first[cut], second[cut])
                    given[owner, piece, arr * 4 + part] = jnp.where(order[1] == 0, second[cut], first[cut])
        depart(given.at[owner], given_at.at[owner])
        depart(kept.at[owner], kept_at.at[owner])
    weighted = grads[...] * gains
    centred = (mixed[...] - average) * rescale
    sum_one = jnp.sum(weighted, 0, keepdims=True) / CHANS
    sum_two = jnp.sum(weighted * centred, 0, keepdims=True) / CHANS
    grads[...] = rescale * (weighted - sum_one - centred * sum_two)

    def hand_out(index):
        rows = pl.ds(pl.multiple_of(index * SUB, SUB), SUB)
        blocks = [[], []]
        for ref in (projected, grads):
            value = ref[rows]
            for half in range(2):
                place = 2 * half * LINE
                pair = regroup(value[:, place : place + LINE], value[:, place + LINE : place + 2 * LINE], low)
                for which in range(2):
                    blocks[which].append(pair[which])
        for which in range(2):
            sent[2 * index + which] = jnp.concatenate(blocks[which], 0).astype(BF16)

    quarter = CHANS // SUB // 4
    for part in range(4):
        loop(quarter, 4, lambda index: hand_out(part * quarter + index))
        area = pl.ds(part * 2 * quarter, 2 * quarter)
        depart(sent.at[area], sent_at.at[area])
    for copy in departures:
        copy.wait()


def finish_kernel(results, cotangent, output_map, grad_map, grad_in, grad_out):
    output_map[...] = results[:, :PLANES]
    grad_map[...] = (cotangent[...].astype(F32) + results[:, PLANES : 2 * PLANES].astype(F32)).astype(BF16)
    factor = 1.0 / (64.0 * 512.0) ** 0.5
    for half in range(2):
        cols = slice(half * 128, half * 128 + 128)
        for pair in range(GROUP // 4):
            blocks = []
            for piece in range(4 * pair, 4 * pair + 4):
                for part in range(2):
                    rows = slice(piece * 32 + part * 16, piece * 32 + part * 16 + 16)
                    grad_in[rows, cols] = results[piece, 2 * PLANES + half * 2 + part].astype(F32) * factor
                    blocks.append(results[piece, 2 * PLANES + 4 + half * 2 + part])
            block = jnp.concatenate(blocks, 0).astype(F32) * factor
            grad_out[cols, pair * 128 : pair * 128 + 128] = block.T


def call(kernel, outs, scratch, ops):
    spaces = [
        pl.BlockSpec(memory_space=pltpu.SMEM if op.dtype == jnp.int32 else pltpu.VMEM) for op in ops
    ]
    out_spaces = jax.tree.map(lambda _: pl.BlockSpec(memory_space=pltpu.VMEM), outs)
    return pl.pallas_call(
        kernel,
        out_shape=outs,
        in_specs=spaces,
        out_specs=out_spaces,
        scratch_shapes=scratch,
        compiler_params=pltpu.CompilerParams(vmem_limit_bytes=PLANE_VMEM),
    )(*ops)


def prepare_kernel(order, cotangent, layer, w_in, w_out, b_in, norms, other, scaled, mine, others):
    for block in range(0, CHANS // (X * Y), 16):
        rows = [
            jnp.swapaxes(cotangent[part : part + SUB].astype(F32) * layer[part : part + SUB], 0, 1)
            for part in (block, block + SUB)
        ]
        rounded = jnp.concatenate(rows, 1).astype(BF16)
        for where in range(X):
            for twin in range(Y):
                scaled[where * Y + twin, :, block : block + 16] = rounded[where * LINES : where * LINES + LINES]
    for half in range(2):
        area = slice(half * HID, half * HID + HID)
        first, second = w_in[area], w_out[:, area]
        mine[area] = jnp.where(order[1] == 0, first, second)
        others[area] = jnp.where(order[1] == 0, second, first)
    left = [b_in[...], jnp.concatenate([norms[...], other[...]], 1)]
    rows = []
    for _ in range(3):
        parts = [value.astype(BF16).astype(F32) for value in left]
        left = [value - part for value, part in zip(left, parts)]
        rows.extend(parts)
    small = jnp.concatenate(rows + [jnp.zeros((10, HID), F32)], 0).astype(BF16)
    mine[CHANS:] = small
    others[CHANS:] = small


def summed(*terms):
    total = terms[0].astype(F32)
    for term in terms[1:]:
        total = total + term.astype(F32)
    return total.astype(BF16)


def own_planes(array, dim, place):
    return lax.dynamic_slice_in_dim(array, place * PLANES, PLANES, dim)


def over_halves(array):
    return jnp.concatenate([array, array], -2)


def tap_table(base_kernel, base_scale, wave_kernels, wave_scale):
    base = (base_scale[:, None, None] * base_kernel).reshape(PLANES, 25).T[:, :, None]
    waves = (wave_scale[..., None, None] * wave_kernels).reshape(3, PLANES, 4, 25).transpose(0, 2, 3, 1)[..., None]
    lane = jnp.arange(128)[None, None, :]

    def choose(level, period, bands):
        table = jnp.zeros((25, PLANES, 128), F32)
        for residue, band in bands:
            table = jnp.where(lane % period == residue, waves[level, band], table)
        return table

    tables = [
        jnp.broadcast_to(base, (25, PLANES, 128)),
        choose(0, 2, ((0, 0), (1, 1))),
        choose(0, 2, ((0, 2), (1, 3))),
        choose(1, 4, ((0, 0), (2, 1), (1, 2), (3, 3))),
        choose(2, 8, ((0, 0), (4, 1), (1, 2), (5, 3))),
    ]
    return over_halves(jnp.concatenate(tables, 0))


def on_device(
    feature_map,
    base_kernel,
    base_bias,
    base_scale,
    wave_kernels,
    wave_scale,
    norm_gain,
    norm_bias,
    w_in,
    b_in,
    w_out,
    b_out,
    layer_scale,
    cotangent,
):
    group = ("hi", "col", "core")
    everyone = ("x", "y", "hi", "col", "core")
    core_here = lax.axis_index("core")
    place = lax.axis_index("hi") * 8 + lax.axis_index("col") * 2 + core_here
    x_here = lax.axis_index("x")
    y_here = lax.axis_index("y")

    tiles = lax.all_to_all(
        feature_map.reshape(GROUP, PLANES, 16, 128), group, split_axis=0, concat_axis=0, tiled=True
    )
    share = CHANS // (X * Y)
    norms = jnp.concatenate([norm_gain, norm_bias]).reshape(1, 2 * share)
    other = lax.ppermute(norms, "y", [(0, 1), (1, 0)])
    order = jnp.stack([x_here, core_here]).astype(jnp.int32)
    scaled, mine, others = call(
        prepare_kernel,
        (
            jax.ShapeDtypeStruct((X * Y, LINES, share, LINE), BF16),
            jax.ShapeDtypeStruct((CHANS + 16, HID), BF16),
            jax.ShapeDtypeStruct((CHANS + 16, HID), BF16),
        ),
        [],
        (
            order,
            cotangent,
            jnp.broadcast_to(layer_scale[:, None, None], (share, 1, LINE)),
            w_in,
            w_out,
            b_in.reshape(1, HID),
            norms,
            other,
        ),
    )
    mine = [mine] + [lax.ppermute(mine, "x", [(i, i ^ step) for i in range(X)]) for step in range(1, X)]
    others = [others] + [lax.ppermute(one, "core", [(0, 1), (1, 0)]) for one in mine[1:]]
    scaled = lax.all_to_all(scaled, ("x", "y"), split_axis=0, concat_axis=0, tiled=True)

    scale_own = own_planes(base_scale, 0, place)
    taps = tap_table(
        own_planes(base_kernel, 0, place),
        scale_own,
        own_planes(wave_kernels, 1, place),
        own_planes(wave_scale, 1, place),
    )

    def rows_of(vector):
        return over_halves(jnp.broadcast_to(vector[:, None], (PLANES, COLS)))

    layer = rows_of(own_planes(layer_scale, 0, place))
    sent = call(
        forward_kernel,
        jax.ShapeDtypeStruct((X, Y, GROUP, 2 * SUB, LINE), BF16),
        plane_scratch(),
        (tiles, taps, rows_of(scale_own * own_planes(base_bias, 0, place))),
    )
    received = lax.all_to_all(
        sent.reshape(X * Y * GROUP, 2 * SUB, LINE), everyone, split_axis=0, concat_axis=0, tiled=True
    )

    extras = jnp.stack([one[CHANS : CHANS + 6] for one in mine])
    extras = jnp.sum(extras.reshape(X, 3, 2, HID).astype(F32), 1)
    biases = extras[:, 0]
    norms = extras[:, 1].reshape(X, Y, 2, share)[x_here ^ jnp.arange(X)][:, y_here ^ jnp.arange(Y)]
    vectors = norms.transpose(2, 0, 1, 3).reshape(2, CHANS, 1)

    anywhere = pl.BlockSpec(memory_space=pl.ANY)
    nearby = pl.BlockSpec(memory_space=pltpu.VMEM)
    blocks = (X * Y * GROUP, 4 * SUB, LINE)
    pieces = (X, GROUP // 2, 8, 16, 128)
    sent, kept, given = pl.pallas_call(
        mlp_kernel,
        out_shape=tuple(jax.ShapeDtypeStruct(shape, BF16) for shape in (blocks, pieces, pieces)),
        in_specs=[pl.BlockSpec(memory_space=pltpu.SMEM)] + [nearby] * 3 + [anywhere] * 10,
        out_specs=(anywhere,) * 3,
        scratch_shapes=[
            pltpu.VMEM(received.shape, BF16),
            pltpu.VMEM(scaled.shape, BF16),
            pltpu.VMEM((X, 2, CHANS + 16, HID), BF16),
            pltpu.VMEM((CHANS, SPOTS), F32),
            pltpu.VMEM((CHANS, SPOTS), BF16),
            pltpu.VMEM((CHANS, SPOTS), F32),
            pltpu.VMEM((CHANS, SPOTS), F32),
            pltpu.VMEM(blocks, BF16),
            pltpu.VMEM(pieces, BF16),
            pltpu.VMEM(pieces, BF16),
            pltpu.SemaphoreType.DMA((10,)),
            pltpu.SemaphoreType.DMA((12,)),
        ],
        compiler_params=pltpu.CompilerParams(vmem_limit_bytes=MLP_VMEM),
    )(
        order,
        biases,
        vectors[0],
        vectors[1],
        received,
        scaled,
        *mine,
        *others,
    )
    received = lax.all_to_all(sent, everyone, split_axis=0, concat_axis=0, tiled=True)

    given = lax.ppermute(given, "core", [(0, 1), (1, 0)])
    pieces = summed(kept, given).reshape(X * GROUP // 2, 8, 16, 128)
    pieces = lax.all_to_all(pieces, ("x", "hi", "col"), split_axis=0, concat_axis=0, tiled=True)
    piece = jnp.sum(pieces.astype(F32), 0).astype(BF16)

    sent = call(
        backward_kernel,
        jax.ShapeDtypeStruct((GROUP, 2 * PLANES, 16, 128), BF16),
        plane_scratch() + [pltpu.VMEM((ROWS, SUB, COLS), F32)],
        (
            received.reshape(X, Y, GROUP, 4 * SUB, LINE),
            tiles,
            taps,
            layer,
            rows_of(own_planes(b_out, 0, place)),
        ),
    )
    sent = jnp.concatenate([sent, jnp.broadcast_to(piece, (GROUP,) + piece.shape)], 1)
    results = lax.all_to_all(sent, group, split_axis=0, concat_axis=0, tiled=True)
    output_map, grad_map, grad_in, grad_out = call(
        finish_kernel,
        (
            jax.ShapeDtypeStruct((GROUP, PLANES, 16, 128), BF16),
            jax.ShapeDtypeStruct((GROUP, PLANES, 16, 128), BF16),
            jax.ShapeDtypeStruct((CHANS, HID), F32),
            jax.ShapeDtypeStruct((HID, CHANS), F32),
        ),
        [],
        (results, cotangent.reshape(GROUP, PLANES, 16, 128)),
    )
    output_map, grad_map = output_map.reshape(feature_map.shape), grad_map.reshape(feature_map.shape)
    return (output_map, grad_map, grad_in, grad_out)


def solution(mesh):
    grid = Mesh(mesh.devices.reshape(2, 2, 4, X, Y), ("hi", "core", "col", "x", "y"))
    chan, row = ("x", "y"), ("hi", "core")
    return jax.shard_map(
        on_device,
        mesh=grid,
        in_specs=(
            P(chan, row, "col"),
            P(chan, None, None),
            P(chan),
            P(chan),
            P(None, chan, None, None, None),
            P(None, chan, None),
            P(chan),
            P(chan),
            P(None, chan),
            P(chan),
            P(chan, None),
            P(chan),
            P(chan),
            P(chan, row, "col"),
        ),
        out_specs=(
            P(chan, row, "col"),
            P(chan, row, "col"),
            P(None, chan),
            P(chan, None),
        ),
        check_vma=False,
    )
```

time: 170 us -> 138 us (0.81)
  waiting for transfers between devices: 53.9 us -> 35.9 us
  Pallas kernels: 39.9 us -> 23.6 us
  starting transfers between devices: 34.9 us -> 39.6 us
  local copies, waits for them, and re-layouts: 9.77 us -> 7.77 us
    pallas_call x3 -> x4, Pallas kernels: 39.9 us -> 14.2 us  [call(): pl.pallas_call(kernel, out_shape=outs, in_specs=spaces, out_specs=out_spa...]
    all_to_all x5, waiting for transfers between devices: 53.9 us -> 35.8 us  [the longest x1 16.3 us: on_device(): lax.all_to_all(sent, everyone, split_axis=0, concat_axis=0, tiled=True)]
    pallas_call x0 -> x1, Pallas kernels: none -> 9.37 us  [on_device(): pl.pallas_call(mlp_kernel, out_shape=tuple((jax.ShapeDtypeStruct(shape, B...]
    all_to_all x5, starting transfers between devices: 28.6 us -> 32.6 us  [the longest x1 10.2 us: on_device(): lax.all_to_all(sent.reshape(X * Y * GROUP, 2 * SUB, LINE), everyone, spli...]
    ppermute x3 -> x7, starting transfers between devices: 4.12 us -> 6.58 us  [the longest x3 4.03 us: on_device(): lax.ppermute(mine, 'x', [(i, i ^ step) for i in range(X)])]
    ppermute x1, starting transfers between devices: 2.2 us -> 0.42 us  [on_device(): other = lax.ppermute(norms, 'y', [(0, 1), (1, 0)])]
    concatenate x2 -> x1, other arithmetic: 1.87 us -> 0.1 us  [on_device(): jnp.concatenate([sent, jnp.broadcast_to(piece, (GROUP,) + piece.shape)], 1)]
    convert_element_type x4 -> x1, other arithmetic: 0.86 us -> 2.58 us  [summed(): return total.astype(BF16)]
  transfers between devices with their start and end apart: 9 -> 13, of which waited for: 5 -> 4; matrix products, arithmetic and copies ran while one was open for 7% -> 9% of each run, Pallas kernels for 19% -> 9%
where the time goes in v2:
time: 138 us
  starting transfers between devices  39.6 us (29%)
  waiting for transfers between devices  35.9 us (26%)
  Pallas kernels  23.6 us (17%)
  blocking collectives  22.8 us (17%)
  local copies, waits for them, and re-layouts  7.77 us (6%)
  other arithmetic  6.93 us (5%)
    all_to_all x1, blocking collectives, on_device(): lax.all_to_all(sent, group, split_axis=0, concat_axis=0, tiled=True)  22.8 us
    all_to_all x1, waiting for transfers between devices, on_device(): lax.all_to_all(sent, everyone, split_axis=0, concat_axis=0, tiled=True)  16.3 us
    pallas_call x4, Pallas kernels, call(): pl.pallas_call(kernel, out_shape=outs, in_specs=spaces, out_specs=out_spa...  14.2 us
    all_to_all x1, waiting for transfers between devices, on_device(): lax.all_to_all(pieces, ('x', 'hi', 'col'), split_axis=0, concat_axis=0, t...  10.5 us
    all_to_all x1, starting transfers between devices, on_device(): lax.all_to_all(sent.reshape(X * Y * GROUP, 2 * SUB, LINE), everyone, spli...  10.2 us
    all_to_all x1, starting transfers between devices, on_device(): lax.all_to_all(feature_map.reshape(GROUP, PLANES, 16, 128), group, split_...  9.6 us
    pallas_call x1, Pallas kernels, on_device(): pl.pallas_call(mlp_kernel, out_shape=tuple((jax.ShapeDtypeStruct(shape, B...  9.37 us
    all_to_all x1, waiting for transfers between devices, on_device(): lax.all_to_all(sent.reshape(X * Y * GROUP, 2 * SUB, LINE), everyone, spli...  7.75 us
  transfers between devices with their start and end apart: 13, of which 4 were waited for; matrix products, arithmetic and copies ran while one was open for 9% of the time, Pallas kernels for 9%

profile of v2, /device:TPU:1, one launch (start us, length us, event | category | flops | bytes accessed | tf_op | source)
XLA Modules:
  0.0 137.6 jit_solution(11919610883742494301)
XLA Ops:
  0.7 9.6 %all-to-all-start = ((bf16[16,4,16,128]{3,2,1,0:T(8,128)(2,1)}), bf16[16,4,16,128]{3,2,1,0:T(8,128)(2,1)S(1)}, u32[]{:S(2)}, u32[]{:S(2)}) async-start(bf16[16,4,16,128]{3,2,1,0:T(8,128)(2,1)} %bitcast.53), calls=%async_computation | async-start | bytes 524288 | tf_op jit(solution)/shard_map/all_to_all | solution.py:471
  10.3 0.7 maximum_bitcast_fusion.norms
  11.1 0.4 collective-permute-start
  11.6 0.8 constant_dynamic-slice_fusion
  12.3 1.1 dynamic-slice_multiply_fusion
  13.4 0.2 copy.99
  13.6 0.1 copy.100
  13.7 0.1 copy.101
  13.8 0.1 copy.115
  14.2 0.1 copy.98
  14.4 0.1 copy.102
  14.5 0.1 copy.103
  14.7 0.1 select_dynamic-update-slice_fusion.3
  14.8 0.1 select_dynamic-update-slice_fusion.2
  15.1 0.1 copy.104
  15.2 0.1 copy.105
  15.5 0.2 select_dynamic-update-slice_fusion.1
  15.6 0.1 copy.108
  16.0 0.1 broadcast_in_dim.191.layer
  16.2 1.5 %shard_map.165 = (bf16[8,4,64,128]{3,2,1,0:T(8,128)(2,1)}, bf16[528,256]{1,0:T(8,128)(2,1)S(1)}, bf16[528,256]{1,0:T(8,128)(2,1)S(1)}) custom-call(s32[2]{0:T(128)S(1)} %pad_add_fusion.order, bf16[64,16,128]{2,1,0:T(8,128)(2,1)S(1)} %copy-done.1, f32[64,1,128]{2,1,0:T(1,128)S(1)} %broadcast_in_dim.191.layer, bf16[512,256]{1,0:T(8,128)(2,1)S(1)} %copy-done.4, ...), custom_call_target="tpu_custom_call" | custom-call | tf_op jit(solution)/shard_map/pallas_call | solution.py:376
  17.7 1.3 all-to-all-done.tiles
  19.0 4.1 %all-to-all-start.2 = ((bf16[8,4,64,128]{3,2,1,0:T(8,128)(2,1)}), bf16[8,4,64,128]{3,2,1,0:T(8,128)(2,1)S(1)}, u32[]{:S(2)}, u32[]{:S(2)}) async-start(bf16[8,4,64,128]{3,2,1,0:T(8,128)(2,1)} %get-tuple-element.15), calls=%async_computation.2 | async-start | bytes 1048576 | tf_op jit(solution)/shard_map/all_to_all | solution.py:499
  23.1 0.2 select_dynamic-update-slice_fusion
  23.3 1.5 %collective-permute-start.1 = (bf16[528,256]{1,0:T(8,128)(2,1)S(1)}, bf16[528,256]{1,0:T(8,128)(2,1)S(1)}, u32[]{:S(2)}, u32[]{:S(2)}) collective-permute-start(bf16[528,256]{1,0:T(8,128)(2,1)S(1)} %get-tuple-element.14.mine_0), channel_id=1, source_target_pairs={{0,2},{2,0},{4,6},{6,4},{1,3},{3,1},{5,7},{7,5},{8,10},{10,8},{12,... | collective-permute-start | bytes 811016 | tf_op jit(solution)/shard_map/ppermute | solution.py:497
  24.9 2.4 %collective-permute-start.2 = (bf16[528,256]{1,0:T(8,128)(2,1)S(1)}, bf16[528,256]{1,0:T(8,128)(2,1)S(1)}, u32[]{:S(2)}, u32[]{:S(2)}) collective-permute-start(bf16[528,256]{1,0:T(8,128)(2,1)S(1)} %get-tuple-element.14.mine_0), channel_id=1, source_target_pairs={{0,4},{2,6},{4,0},{6,2},{1,5},{3,7},{5,1},{7,3},{8,12},{10,14},{12... | collective-permute-start | bytes 811016 | tf_op jit(solution)/shard_map/ppermute | solution.py:497
  27.5 5.9 %shard_map.166 = bf16[4,2,16,16,128]{4,3,2,1,0:T(8,128)(2,1)} custom-call(bf16[16,4,16,128]{3,2,1,0:T(8,128)(2,1)S(1)} %all-to-all-done.tiles, f32[125,8,128]{2,1,0:T(8,128)S(1)} %pad_maximum_fusion.1.taps, f32[8,512]{1,0:T(8,128)S(1)} %pad_maximum_fusion.2.shift), custom_call_target="tpu_custom_call" | custom-call | tf_op jit(solution)/shard_map/pallas_call | solution.py:376
  33.4 10.2 %all-to-all-start.1 = ((bf16[128,16,128]{2,1,0:T(8,128)(2,1)}), bf16[128,16,128]{2,1,0:T(8,128)(2,1)S(1)}, u32[]{:S(2)}, u32[]{:S(2)}) async-start(bf16[128,16,128]{2,1,0:T(8,128)(2,1)} %bitcast.26), calls=%async_computation.1 | async-start | bytes 1048576 | tf_op jit(solution)/shard_map/all_to_all | solution.py:519
  43.7 1.6 %collective-permute-start.4 = (bf16[528,256]{1,0:T(8,128)(2,1)S(1)}, bf16[528,256]{1,0:T(8,128)(2,1)S(1)}, u32[]{:S(2)}, u32[]{:S(2)}) collective-permute-start(bf16[528,256]{1,0:T(8,128)(2,1)S(1)} %collective-permute-done.1.mine_1), channel_id=1, source_target_pairs={{0,32},{32,0},{1,33},{33,1},{2,34},{34,2},{3,35},{35,3},{4,36},{36... | collective-permute-start | bytes 811016 | tf_op jit(solution)/shard_map/ppermute | solution.py:498
  45.4 0.4 collective-permute-start.6
  45.9 0.6 gather_fusion
  46.5 0.6 gather_fusion.1
  47.1 0.9 squeeze.10.bias
  48.0 0.9 squeeze.9.gain
  48.9 0.6 copy.117
  49.5 7.7 %all-to-all-done.1.received_at = bf16[128,16,128]{2,1,0:T(8,128)(2,1)S(1)} async-done(((bf16[128,16,128]{2,1,0:T(8,128)(2,1)}), bf16[128,16,128]{2,1,0:T(8,128)(2,1)S(1)}, u32[]{:S(2)}, u32[]{:S(2)}) %all-to-all-start.1) | async-done | bytes 524320 | tf_op jit(solution)/shard_map/all_to_all | solution.py:519
  57.3 0.8 copy-done.9
  58.1 9.4 %shard_map.167 = (bf16[128,32,128]{2,1,0:T(8,128)(2,1)}, bf16[4,8,8,16,128]{4,3,2,1,0:T(8,128)(2,1)}, bf16[4,8,8,16,128]{4,3,2,1,0:T(8,128)(2,1)}) custom-call(s32[2]{0:T(128)} %copy-done.6, f32[4,256]{1,0:T(4,128)} %bitcast.56, f32[512,1]{1,0:T(8,128)} %squeeze.9.gain, f32[512,1]{1,0:T(8,128)} %squeeze.10.bias, bf16[128,16,128]{2,1,0:T(8,128)(2,1)} %copy-done.9, ...), custom_call_target="tpu_custom_call" | custom-call | tf_op jit(solution)/shard_map/pallas_call | solution.py:533
  67.5 0.5 collective-permute-start.7
  67.9 3.9 %all-to-all-start.3 = ((bf16[128,32,128]{2,1,0:T(8,128)(2,1)}), bf16[128,32,128]{2,1,0:T(8,128)(2,1)S(1)}, u32[]{:S(2)}, u32[]{:S(2)}) async-start(bf16[128,32,128]{2,1,0:T(8,128)(2,1)} %get-tuple-element.17), calls=%async_computation.3 | async-start | bytes 2097152 | tf_op jit(solution)/shard_map/all_to_all | solution.py:563
  71.9 2.6 %add_convert_fusion = bf16[4,8,8,16,128]{4,3,2,1,0:T(8,128)(2,1)} fusion(bf16[4,8,8,16,128]{4,3,2,1,0:T(8,128)(2,1)} %collective-permute-done.7, bf16[4,8,8,16,128]{4,3,2,1,0:T(8,128)(2,1)S(1)} %copy-done.10), kind=kLoop, calls=%fused_computation.2 | loop fusion | flops 2097152 | bytes 3145728 | tf_op jit(solution)/shard_map/convert_element_type | solution.py:416
  74.5 16.3 %all-to-all-done.3 = bf16[128,32,128]{2,1,0:T(8,128)(2,1)S(1)} async-done(((bf16[128,32,128]{2,1,0:T(8,128)(2,1)}), bf16[128,32,128]{2,1,0:T(8,128)(2,1)S(1)}, u32[]{:S(2)}, u32[]{:S(2)}) %all-to-all-start.3) | async-done | bytes 1048608 | tf_op jit(solution)/shard_map/all_to_all | solution.py:563
  90.8 4.8 %all-to-all-start.4 = ((bf16[32,8,16,128]{3,2,1,0:T(8,128)(2,1)}), bf16[32,8,16,128]{3,2,1,0:T(8,128)(2,1)}, u32[]{:S(2)}, u32[]{:S(2)}) async-start(bf16[32,8,16,128]{3,2,1,0:T(8,128)(2,1)} %bitcast.28), calls=%async_computation.4 | async-start | bytes 2097152 | tf_op jit(solution)/shard_map/all_to_all | solution.py:567
  95.9 5.5 %shard_map.168 = bf16[16,8,16,128]{3,2,1,0:T(8,128)(2,1)S(1)} custom-call(bf16[4,2,16,32,128]{4,3,2,1,0:T(8,128)(2,1)S(1)} %bitcast.49, bf16[16,4,16,128]{3,2,1,0:T(8,128)(2,1)S(1)} %all-to-all-done.tiles, f32[125,8,128]{2,1,0:T(8,128)S(1)} %pad_maximum_fusion.1.taps, f32[8,512]{1,0:T(8,128)S(1)} %get-tuple-element.54.scale, ...), custom_call_target="tpu_custom_call" | custom-call | tf_op jit(solution)/shard_map/pallas_call | solution.py:376
  101.5 10.5 %all-to-all-done.4 = bf16[32,8,16,128]{3,2,1,0:T(8,128)(2,1)} async-done(((bf16[32,8,16,128]{3,2,1,0:T(8,128)(2,1)}), bf16[32,8,16,128]{3,2,1,0:T(8,128)(2,1)}, u32[]{:S(2)}, u32[]{:S(2)}) %all-to-all-start.4) | async-done | bytes 1048608 | tf_op jit(solution)/shard_map/all_to_all | solution.py:567
  111.9 1.4 %reduce_sum.22 = bf16[8,16,128]{2,1,0:T(8,128)(2,1)S(1)} reduce(bf16[32,8,16,128]{3,2,1,0:T(8,128)(2,1)} %all-to-all-done.4, bf16[]{:T(256)} %constant.104.clone.1), dimensions={0}, to_apply=%region_1.2 | reduce | flops 507904 | bytes 1081346 | tf_op jit(solution)/shard_map/reduce_sum | solution.py:568
  113.4 0.1 pad_maximum_fusion
  113.5 22.8 %all_to_all.30.results = bf16[16,16,16,128]{3,2,1,0:T(8,128)(2,1)S(1)} all-to-all(bf16[16,16,16,128]{3,2,1,0:T(8,128)(2,1)S(1)} %pad_maximum_fusion), channel_id=1, replica_groups=mesh['hi'=2,'core'=2,'col'=4,'x'=4,'y'=2] {'hi','col','core'}, dimensions={0} | all-to-all | bytes 2097152 | tf_op jit(solution)/shard_map/all_to_all | solution.py:583
  136.3 1.3 shard_map.169
  (92 shorter events, 2.1 us)
Async XLA Ops:
  0.6 13.1 %copy-start = (f32[64,5,5]{0,2,1:T(8,128)S(1)}, f32[64,5,5]{0,2,1:T(8,128)}, u32[]{:S(2)}) copy-start(f32[64,5,5]{0,2,1:T(8,128)} %param.15) | copy-start | bytes 19204
  0.6 13.3 %copy-start.16 = (f32[64]{0:T(128)S(1)}, f32[64]{0:T(128)}, u32[]{:S(2)}) copy-start(f32[64]{0:T(128)} %param.16) | copy-start | bytes 772
  0.7 13.3 %copy-start.17 = (f32[64]{0:T(128)S(1)}, f32[64]{0:T(128)}, u32[]{:S(2)}) copy-start(f32[64]{0:T(128)} %param.17) | copy-start | bytes 772
  0.7 15.4 %copy-start.15 = (f32[64]{0:T(128)S(1)}, f32[64]{0:T(128)}, u32[]{:S(2)}) copy-start(f32[64]{0:T(128)} %param.26) | copy-start | bytes 772
  0.7 15.5 %copy-start.7 = (f32[256]{0:T(256)S(1)}, f32[256]{0:T(256)}, u32[]{:S(2)}) copy-start(f32[256]{0:T(256)} %param.23) | copy-start | bytes 3076
  0.7 15.5 %copy-start.4 = (bf16[512,256]{1,0:T(8,128)(2,1)S(1)}, bf16[512,256]{1,0:T(8,128)(2,1)}, u32[]{:S(2)}) copy-start(bf16[512,256]{1,0:T(8,128)(2,1)} %w_in.1) | copy-start | bytes 786436
  0.7 15.5 %copy-start.5 = (bf16[256,512]{1,0:T(8,128)(2,1)S(1)}, bf16[256,512]{1,0:T(8,128)(2,1)}, u32[]{:S(2)}) copy-start(bf16[256,512]{1,0:T(8,128)(2,1)} %w_out.1) | copy-start | bytes 786436
  0.7 15.5 %copy-start.1 = (bf16[64,16,128]{2,1,0:T(8,128)(2,1)S(1)}, bf16[64,16,128]{2,1,0:T(8,128)(2,1)}, u32[]{:S(2)}) copy-start(bf16[64,16,128]{2,1,0:T(8,128)(2,1)} %cotangent.1) | copy-start | bytes 786436
  0.7 18.3 %all-to-all-start = ((bf16[16,4,16,128]{3,2,1,0:T(8,128)(2,1)}), bf16[16,4,16,128]{3,2,1,0:T(8,128)(2,1)S(1)}, u32[]{:S(2)}, u32[]{:S(2)}) async-start(bf16[16,4,16,128]{3,2,1,0:T(8,128)(2,1)} %bitcast.53), calls=%async_computation | async-start | bytes 524288 | tf_op jit(solution)/shard_map/all_to_all | solution.py:471
  11.1 5.0 %collective-permute-start = (f32[1,128]{1,0:T(1,128)S(1)}, f32[1,128]{1,0:T(1,128)S(1)}, u32[]{:S(2)}, u32[]{:S(2)}) collective-permute-start(f32[1,128]{1,0:T(1,128)S(1)} %maximum_bitcast_fusion.norms), channel_id=1, source_target_pairs={{0,1},{1,0},{2,3},{3,2},{4,5},{5,4},{6,7},{7,6},{8,9},{9,8},{10,11... | collective-permute-start | bytes 1544 | tf_op jit(solution)/shard_map/ppermute | solution.py:476
  15.1 3.9 %copy-start.6 = (s32[2]{0:T(128)}, s32[2]{0:T(128)S(1)}, u32[]{:S(2)}) copy-start(s32[2]{0:T(128)S(1)} %pad_add_fusion.order) | copy-start | bytes 28
  17.7 9.7 %copy-start.3 = (bf16[528,256]{1,0:T(8,128)(2,1)}, bf16[528,256]{1,0:T(8,128)(2,1)S(1)}, u32[]{:S(2)}) copy-start(bf16[528,256]{1,0:T(8,128)(2,1)S(1)} %get-tuple-element.16.others_0) | copy-start | bytes 811012
  17.7 25.8 %copy-start.2 = (bf16[528,256]{1,0:T(8,128)(2,1)}, bf16[528,256]{1,0:T(8,128)(2,1)S(1)}, u32[]{:S(2)}) copy-start(bf16[528,256]{1,0:T(8,128)(2,1)S(1)} %get-tuple-element.14.mine_0) | copy-start | bytes 811012
  19.0 14.3 %all-to-all-start.2 = ((bf16[8,4,64,128]{3,2,1,0:T(8,128)(2,1)}), bf16[8,4,64,128]{3,2,1,0:T(8,128)(2,1)S(1)}, u32[]{:S(2)}, u32[]{:S(2)}) async-start(bf16[8,4,64,128]{3,2,1,0:T(8,128)(2,1)} %get-tuple-element.15), calls=%async_computation.2 | async-start | bytes 1048576 | tf_op jit(solution)/shard_map/all_to_all | solution.py:499
  23.3 20.2 %collective-permute-start.1 = (bf16[528,256]{1,0:T(8,128)(2,1)S(1)}, bf16[528,256]{1,0:T(8,128)(2,1)S(1)}, u32[]{:S(2)}, u32[]{:S(2)}) collective-permute-start(bf16[528,256]{1,0:T(8,128)(2,1)S(1)} %get-tuple-element.14.mine_0), channel_id=1, source_target_pairs={{0,2},{2,0},{4,6},{6,4},{1,3},{3,1},{5,7},{7,5},{8,10},{10,8},{12,... | collective-permute-start | bytes 811016 | tf_op jit(solution)/shard_map/ppermute | solution.py:497
  24.9 18.8 %collective-permute-start.2 = (bf16[528,256]{1,0:T(8,128)(2,1)S(1)}, bf16[528,256]{1,0:T(8,128)(2,1)S(1)}, u32[]{:S(2)}, u32[]{:S(2)}) collective-permute-start(bf16[528,256]{1,0:T(8,128)(2,1)S(1)} %get-tuple-element.14.mine_0), channel_id=1, source_target_pairs={{0,4},{2,6},{4,0},{6,2},{1,5},{3,7},{5,1},{7,3},{8,12},{10,14},{12... | collective-permute-start | bytes 811016 | tf_op jit(solution)/shard_map/ppermute | solution.py:497
  27.3 16.4 %collective-permute-start.3 = (bf16[528,256]{1,0:T(8,128)(2,1)S(1)}, bf16[528,256]{1,0:T(8,128)(2,1)S(1)}, u32[]{:S(2)}, u32[]{:S(2)}) collective-permute-start(bf16[528,256]{1,0:T(8,128)(2,1)S(1)} %get-tuple-element.14.mine_0), channel_id=1, source_target_pairs={{0,6},{2,4},{4,2},{6,0},{1,7},{3,5},{5,3},{7,1},{8,14},{10,12},{12... | collective-permute-start | bytes 811016 | tf_op jit(solution)/shard_map/ppermute | solution.py:497
  33.4 23.9 %copy-start.8 = (bf16[8,4,64,128]{3,2,1,0:T(8,128)(2,1)}, bf16[8,4,64,128]{3,2,1,0:T(8,128)(2,1)S(1)}, u32[]{:S(2)}) copy-start(bf16[8,4,64,128]{3,2,1,0:T(8,128)(2,1)S(1)} %all-to-all-done.2.received_scaled_at) | copy-start | bytes 1572868
  33.4 23.9 %all-to-all-start.1 = ((bf16[128,16,128]{2,1,0:T(8,128)(2,1)}), bf16[128,16,128]{2,1,0:T(8,128)(2,1)S(1)}, u32[]{:S(2)}, u32[]{:S(2)}) async-start(bf16[128,16,128]{2,1,0:T(8,128)(2,1)} %bitcast.26), calls=%async_computation.1 | async-start | bytes 1048576 | tf_op jit(solution)/shard_map/all_to_all | solution.py:519
  43.6 13.7 %copy-start.11 = (bf16[528,256]{1,0:T(8,128)(2,1)}, bf16[528,256]{1,0:T(8,128)(2,1)S(1)}, u32[]{:S(2)}) copy-start(bf16[528,256]{1,0:T(8,128)(2,1)S(1)} %collective-permute-done.1.mine_1) | copy-start | bytes 811012
  43.6 13.7 %copy-start.12 = (bf16[528,256]{1,0:T(8,128)(2,1)}, bf16[528,256]{1,0:T(8,128)(2,1)S(1)}, u32[]{:S(2)}) copy-start(bf16[528,256]{1,0:T(8,128)(2,1)S(1)} %collective-permute-done.2.mine_2) | copy-start | bytes 811012
  43.7 13.6 %copy-start.13 = (bf16[528,256]{1,0:T(8,128)(2,1)}, bf16[528,256]{1,0:T(8,128)(2,1)S(1)}, u32[]{:S(2)}) copy-start(bf16[528,256]{1,0:T(8,128)(2,1)S(1)} %collective-permute-done.3.mine_3) | copy-start | bytes 811012
  43.7 5.8 %collective-permute-start.4 = (bf16[528,256]{1,0:T(8,128)(2,1)S(1)}, bf16[528,256]{1,0:T(8,128)(2,1)S(1)}, u32[]{:S(2)}, u32[]{:S(2)}) collective-permute-start(bf16[528,256]{1,0:T(8,128)(2,1)S(1)} %collective-permute-done.1.mine_1), channel_id=1, source_target_pairs={{0,32},{32,0},{1,33},{33,1},{2,34},{34,2},{3,35},{35,3},{4,36},{36... | collective-permute-start | bytes 811016 | tf_op jit(solution)/shard_map/ppermute | solution.py:498
  45.3 4.2 %collective-permute-start.5 = (bf16[528,256]{1,0:T(8,128)(2,1)S(1)}, bf16[528,256]{1,0:T(8,128)(2,1)}, u32[]{:S(2)}, u32[]{:S(2)}) collective-permute-start(bf16[528,256]{1,0:T(8,128)(2,1)S(1)} %collective-permute-done.2.mine_2), channel_id=1, source_target_pairs={{0,32},{32,0},{1,33},{33,1},{2,34},{34,2},{3,35},{35,3},{4,36},{36... | collective-permute-start | bytes 811016 | tf_op jit(solution)/shard_map/ppermute | solution.py:498
  45.4 4.1 %collective-permute-start.6 = (bf16[528,256]{1,0:T(8,128)(2,1)S(1)}, bf16[528,256]{1,0:T(8,128)(2,1)}, u32[]{:S(2)}, u32[]{:S(2)}) collective-permute-start(bf16[528,256]{1,0:T(8,128)(2,1)S(1)} %collective-permute-done.3.mine_3), channel_id=1, source_target_pairs={{0,32},{32,0},{1,33},{33,1},{2,34},{34,2},{3,35},{35,3},{4,36},{36... | collective-permute-start | bytes 811016 | tf_op jit(solution)/shard_map/ppermute | solution.py:498
  49.5 7.8 %copy-start.14 = (bf16[528,256]{1,0:T(8,128)(2,1)}, bf16[528,256]{1,0:T(8,128)(2,1)S(1)}, u32[]{:S(2)}) copy-start(bf16[528,256]{1,0:T(8,128)(2,1)S(1)} %collective-permute-done.4.others_1) | copy-start | bytes 811012
  57.3 0.8 copy-start.9
  67.5 4.4 %collective-permute-start.7 = (bf16[4,8,8,16,128]{4,3,2,1,0:T(8,128)(2,1)}, bf16[4,8,8,16,128]{4,3,2,1,0:T(8,128)(2,1)}, u32[]{:S(2)}, u32[]{:S(2)}) collective-permute-start(bf16[4,8,8,16,128]{4,3,2,1,0:T(8,128)(2,1)} %get-tuple-element.19), channel_id=1, source_target_pairs={{0,32},{32,0},{1,33},{33,1},{2,34},{34,2},{3,35},{35,3},{4,36},{36... | collective-permute-start | bytes 3145736 | tf_op jit(solution)/shard_map/ppermute | solution.py:565
  67.9 4.0 %copy-start.10 = (bf16[4,8,8,16,128]{4,3,2,1,0:T(8,128)(2,1)S(1)}, bf16[4,8,8,16,128]{4,3,2,1,0:T(8,128)(2,1)}, u32[]{:S(2)}) copy-start(bf16[4,8,8,16,128]{4,3,2,1,0:T(8,128)(2,1)} %get-tuple-element.18) | copy-start | bytes 3145732
  67.9 22.9 %all-to-all-start.3 = ((bf16[128,32,128]{2,1,0:T(8,128)(2,1)}), bf16[128,32,128]{2,1,0:T(8,128)(2,1)S(1)}, u32[]{:S(2)}, u32[]{:S(2)}) async-start(bf16[128,32,128]{2,1,0:T(8,128)(2,1)} %get-tuple-element.17), calls=%async_computation.3 | async-start | bytes 2097152 | tf_op jit(solution)/shard_map/all_to_all | solution.py:563
  90.8 4.9 %copy-start.18 = (f32[64]{0:T(128)S(1)}, f32[64]{0:T(128)}, u32[]{:S(2)}) copy-start(f32[64]{0:T(128)} %param.25) | copy-start | bytes 772
  90.8 21.1 %all-to-all-start.4 = ((bf16[32,8,16,128]{3,2,1,0:T(8,128)(2,1)}), bf16[32,8,16,128]{3,2,1,0:T(8,128)(2,1)}, u32[]{:S(2)}, u32[]{:S(2)}) async-start(bf16[32,8,16,128]{3,2,1,0:T(8,128)(2,1)} %bitcast.28), calls=%async_computation.4 | async-start | bytes 2097152 | tf_op jit(solution)/shard_map/all_to_all | solution.py:567

commit v3 on v2

--- a/solution.py
+++ b/solution.py
@@ -255,7 +255,7 @@
 
 
 def mlp_kernel(
-    order, biases, gain, bias, received_at, received_scaled_at,
+    order, biases, vectors, received_at, received_scaled_at,
     mine_0, mine_1, mine_2, mine_3, others_0, others_1, others_2, others_3, sent_at, kept_at, given_at,
     received, received_scaled, packs, mixed, scaled, projected, grads, sent, kept, given, arrived, left,
 ):
@@ -298,8 +298,11 @@
     values = mixed[...]
     average = jnp.sum(values, 0, keepdims=True) / CHANS
     rescale = lax.rsqrt(jnp.sum(values * values, 0, keepdims=True) / CHANS - average * average + EPSILON)
-    gains = gain[...]
-    normed = (((values - average) * rescale) * gains + bias[...]).astype(BF16)
+    gains, shifts = [
+        jnp.concatenate([jnp.broadcast_to(vectors[row : row + 1], (LINE, CHANS)).T] * (SPOTS // LINE), 1)
+        for row in range(2)
+    ]
+    normed = (((values - average) * rescale) * gains + shifts).astype(BF16)
     scaled_now = scaled[...]
     normed_turned, scaled_turned = normed.T, scaled_now.T
     for index in range(X):
@@ -312,17 +315,16 @@
         projected[...] = part if index == 0 else projected[...] + part
         part = dot(w_in, grad_hidden, 1, 1)
         grads[...] = part if index == 0 else grads[...] + part
-        owner = order[0] ^ index
         for arr, value in ((0, dot(normed, grad_hidden, 1, 0)), (1, dot(scaled_now, activated, 1, 0))):
             rounded = value.astype(BF16)
             for piece in range(GROUP // 2):
                 first, second = rounded[piece * 64 : piece * 64 + 32], rounded[piece * 64 + 32 : piece * 64 + 64]
                 for part in range(4):
                     cut = (slice(part % 2 * 16, part % 2 * 16 + 16), slice(part // 2 * 128, part // 2 * 128 + 128))
-                    kept[owner, piece, arr * 4 + part] = jnp.where(order[1] == 0, first[cut], second[cut])
-                    given[owner, piece, arr * 4 + part] = jnp.where(order[1] == 0, second[cut], first[cut])
-        depart(given.at[owner], given_at.at[owner])
-        depart(kept.at[owner], kept_at.at[owner])
+                    kept[index, piece, arr * 4 + part] = jnp.where(order[1] == 0, first[cut], second[cut])
+                    given[index, piece, arr * 4 + part] = jnp.where(order[1] == 0, second[cut], first[cut])
+        depart(given.at[index], given_at.at[index])
+        depart(kept.at[index], kept_at.at[index])
     weighted = grads[...] * gains
     centred = (mixed[...] - average) * rescale
     sum_one = jnp.sum(weighted, 0, keepdims=True) / CHANS
@@ -349,6 +351,12 @@
         depart(sent.at[area], sent_at.at[area])
     for copy in departures:
         copy.wait()
+
+
+def sum_kernel(first, second, third, fourth, after, total):
+    for place in range(first.shape[0]):
+        parts = [ref[place].astype(F32) for ref in (first, second, third, fourth)]
+        total[place] = (parts[0] + parts[1] + parts[2] + parts[3]).astype(BF16)
 
 
 def finish_kernel(results, cotangent, output_map, grad_map, grad_in, grad_out):
@@ -368,7 +376,7 @@
             grad_out[cols, pair * 128 : pair * 128 + 128] = block.T
 
 
-def call(kernel, outs, scratch, ops):
+def call(kernel, outs, scratch, ops, microseconds):
     spaces = [
         pl.BlockSpec(memory_space=pltpu.SMEM if op.dtype == jnp.int32 else pltpu.VMEM) for op in ops
     ]
@@ -380,6 +388,7 @@
         out_specs=out_spaces,
         scratch_shapes=scratch,
         compiler_params=pltpu.CompilerParams(vmem_limit_bytes=PLANE_VMEM),
+        cost_estimate=pl.CostEstimate(flops=0, bytes_accessed=int(microseconds * 3.5e6), transcendentals=0),
     )(*ops)
 
 
@@ -493,6 +502,7 @@
             norms,
             other,
         ),
+        1,
     )
     mine = [mine] + [lax.ppermute(mine, "x", [(i, i ^ step) for i in range(X)]) for step in range(1, X)]
     others = [others] + [lax.ppermute(one, "core", [(0, 1), (1, 0)]) for one in mine[1:]]
@@ -515,6 +525,7 @@
         jax.ShapeDtypeStruct((X, Y, GROUP, 2 * SUB, LINE), BF16),
         plane_scratch(),
         (tiles, taps, rows_of(scale_own * own_planes(base_bias, 0, place))),
+        6,
     )
     received = lax.all_to_all(
         sent.reshape(X * Y * GROUP, 2 * SUB, LINE), everyone, split_axis=0, concat_axis=0, tiled=True
@@ -524,7 +535,7 @@
     extras = jnp.sum(extras.reshape(X, 3, 2, HID).astype(F32), 1)
     biases = extras[:, 0]
     norms = extras[:, 1].reshape(X, Y, 2, share)[x_here ^ jnp.arange(X)][:, y_here ^ jnp.arange(Y)]
-    vectors = norms.transpose(2, 0, 1, 3).reshape(2, CHANS, 1)
+    vectors = norms.transpose(2, 0, 1, 3).reshape(2, CHANS)
 
     anywhere = pl.BlockSpec(memory_space=pl.ANY)
     nearby = pl.BlockSpec(memory_space=pltpu.VMEM)
@@ -533,7 +544,7 @@
     sent, kept, given = pl.pallas_call(
         mlp_kernel,
         out_shape=tuple(jax.ShapeDtypeStruct(shape, BF16) for shape in (blocks, pieces, pieces)),
-        in_specs=[pl.BlockSpec(memory_space=pltpu.SMEM)] + [nearby] * 3 + [anywhere] * 10,
+        in_specs=[pl.BlockSpec(memory_space=pltpu.SMEM)] + [nearby] * 2 + [anywhere] * 10,
         out_specs=(anywhere,) * 3,
         scratch_shapes=[
             pltpu.VMEM(received.shape, BF16),
@@ -553,8 +564,7 @@
     )(
         order,
         biases,
-        vectors[0],
-        vectors[1],
+        vectors,
         received,
         scaled,
         *mine,
@@ -563,9 +573,10 @@
     received = lax.all_to_all(sent, everyone, split_axis=0, concat_axis=0, tiled=True)
 
     given = lax.ppermute(given, "core", [(0, 1), (1, 0)])
-    pieces = summed(kept, given).reshape(X * GROUP // 2, 8, 16, 128)
-    pieces = lax.all_to_all(pieces, ("x", "hi", "col"), split_axis=0, concat_axis=0, tiled=True)
-    piece = jnp.sum(pieces.astype(F32), 0).astype(BF16)
+    parts = [summed(kept[step], given[step]) for step in range(X)]
+    parts = parts[:1] + [
+        lax.ppermute(parts[step], "x", [(i, i ^ step) for i in range(X)]) for step in range(1, X)
+    ]
 
     sent = call(
         backward_kernel,
@@ -578,7 +589,11 @@
             layer,
             rows_of(own_planes(b_out, 0, place)),
         ),
-    )
+        6,
+    )
+    pieces = call(sum_kernel, jax.ShapeDtypeStruct(parts[0].shape, BF16), [], (*parts, sent[0, 0]), 1)
+    pieces = lax.all_to_all(pieces, ("hi", "col"), split_axis=0, concat_axis=0, tiled=True)
+    piece = summed(*[pieces[chip] for chip in range(GROUP // 2)])
     sent = jnp.concatenate([sent, jnp.broadcast_to(piece, (GROUP,) + piece.shape)], 1)
     results = lax.all_to_all(sent, group, split_axis=0, concat_axis=0, tiled=True)
     output_map, grad_map, grad_in, grad_out = call(
@@ -591,6 +606,7 @@
         ),
         [],
         (results, cotangent.reshape(GROUP, PLANES, 16, 128)),
+        1,
     )
     output_map, grad_map = output_map.reshape(feature_map.shape), grad_map.reshape(feature_map.shape)
     return (output_map, grad_map, grad_in, grad_out)

time: 138 us -> 136 us (0.986)
  blocking collectives: 22.8 us -> 36.1 us
  waiting for transfers between devices: 35.9 us -> 24.2 us
  other arithmetic: 6.93 us -> 3.68 us
    all_to_all x0 -> x1, blocking collectives: none -> 14.3 us  [on_device(): lax.all_to_all(pieces, ('hi', 'col'), split_axis=0, concat_axis=0, tiled=...]
    all_to_all x1 -> x0, waiting for transfers between devices: 10.5 us -> none  [on_device(): lax.all_to_all(pieces, ('x', 'hi', 'col'), split_axis=0, concat_axis=0, t...]
    all_to_all x1 -> x0, starting transfers between devices: 4.8 us -> none  [on_device(): lax.all_to_all(pieces, ('x', 'hi', 'col'), split_axis=0, concat_axis=0, t...]
    all_to_all x1, waiting for transfers between devices: 16.3 us -> 11.9 us  [on_device(): lax.all_to_all(sent, everyone, split_axis=0, concat_axis=0, tiled=True)]
    ppermute x0 -> x3, starting transfers between devices: none -> 3.86 us  [on_device(): lax.ppermute(parts[step], 'x', [(i, i ^ step) for i in range(X)])]
    unnamed x41 -> x51, local copies, waits for them, and re-layouts: 1.64 us -> 4.59 us
    squeeze x2 -> x1, local copies, waits for them, and re-layouts: 1.82 us -> 0.01 us  [on_device(): sent[0, 0]]
    all_to_all x1, waiting for transfers between devices: 7.75 us -> 9.32 us  [on_device(): lax.all_to_all(sent.reshape(X * Y * GROUP, 2 * SUB, LINE), everyone, spli...]
  transfers between devices with their start and end apart: 13 -> 15, of which waited for: 4 -> 5; matrix products, arithmetic and copies ran while one was open for 9% -> 6% of each run, Pallas kernels for 9% -> 9%
where the time goes in v3:
time: 136 us
  starting transfers between devices  38.5 us (28%)
  blocking collectives  36.1 us (27%)
  waiting for transfers between devices  24.2 us (18%)
  Pallas kernels  23.4 us (17%)
  local copies, waits for them, and re-layouts  8.87 us (7%)
  other arithmetic  3.68 us (3%)
    all_to_all x1, blocking collectives, on_device(): lax.all_to_all(sent, group, split_axis=0, concat_axis=0, tiled=True)  21.8 us
    pallas_call x5, Pallas kernels, call(): pl.pallas_call(kernel, out_shape=outs, in_specs=spaces, out_specs=out_spa...  14.3 us
    all_to_all x1, blocking collectives, on_device(): lax.all_to_all(pieces, ('hi', 'col'), split_axis=0, concat_axis=0, tiled=...  14.3 us
    all_to_all x1, waiting for transfers between devices, on_device(): lax.all_to_all(sent, everyone, split_axis=0, concat_axis=0, tiled=True)  11.9 us
    all_to_all x1, starting transfers between devices, on_device(): lax.all_to_all(sent.reshape(X * Y * GROUP, 2 * SUB, LINE), everyone, spli...  10.2 us
    all_to_all x1, starting transfers between devices, on_device(): lax.all_to_all(feature_map.reshape(GROUP, PLANES, 16, 128), group, split_...  9.6 us
    all_to_all x1, waiting for transfers between devices, on_device(): lax.all_to_all(sent.reshape(X * Y * GROUP, 2 * SUB, LINE), everyone, spli...  9.32 us
    pallas_call x1, Pallas kernels, on_device(): pl.pallas_call(mlp_kernel, out_shape=tuple((jax.ShapeDtypeStruct(shape, B...  9.04 us
  transfers between devices with their start and end apart: 15, of which 5 were waited for; matrix products, arithmetic and copies ran while one was open for 6% of the time, Pallas kernels for 9%

profile of v3, /device:TPU:1, one launch (start us, length us, event | category | flops | bytes accessed | tf_op | source)
XLA Modules:
  0.0 135.9 jit_solution(10836103300908526765)
XLA Ops:
  0.7 9.6 %all-to-all-start = ((bf16[16,4,16,128]{3,2,1,0:T(8,128)(2,1)}), bf16[16,4,16,128]{3,2,1,0:T(8,128)(2,1)S(1)}, u32[]{:S(2)}, u32[]{:S(2)}) async-start(bf16[16,4,16,128]{3,2,1,0:T(8,128)(2,1)} %bitcast.64), calls=%async_computation | async-start | bytes 524288 | tf_op jit(solution)/shard_map/all_to_all | solution.py:480
  10.4 0.4 collective-permute-start
  10.9 0.7 copy-done.17
  11.6 0.1 dynamic-slice_multiply_fusion
  11.8 0.2 copy.89
  12.0 0.1 copy.90
  12.1 0.1 copy.91
  12.2 0.1 copy.103
  12.4 0.2 copy-done.19
  12.9 0.1 copy.88
  13.1 0.1 copy.92
  13.7 0.1 select_dynamic-update-slice_fusion.3
  13.8 0.1 select_dynamic-update-slice_fusion.2
  13.9 0.2 select_dynamic-update-slice_fusion.1
  14.7 0.1 broadcast_in_dim.191.layer
  14.9 0.6 copy-done.7
  15.5 1.5 %shard_map.165 = (bf16[8,4,64,128]{3,2,1,0:T(8,128)(2,1)}, bf16[528,256]{1,0:T(8,128)(2,1)S(1)}, bf16[528,256]{1,0:T(8,128)(2,1)S(1)}) custom-call(s32[2]{0:T(128)S(1)} %pad_add_fusion.order, bf16[64,16,128]{2,1,0:T(8,128)(2,1)S(1)} %copy-done.1, f32[64,1,128]{2,1,0:T(1,128)S(1)} %broadcast_in_dim.191.layer, bf16[512,256]{1,0:T(8,128)(2,1)S(1)} %copy-done.4, ...), custom_call_target="tpu_custom_call" | custom-call | bytes 3500000 | tf_op jit(solution)/shard_map/pallas_call | solution.py:384
  17.0 1.9 %all-to-all-done.tiles = bf16[16,4,16,128]{3,2,1,0:T(8,128)(2,1)S(1)} async-done(((bf16[16,4,16,128]{3,2,1,0:T(8,128)(2,1)}), bf16[16,4,16,128]{3,2,1,0:T(8,128)(2,1)S(1)}, u32[]{:S(2)}, u32[]{:S(2)}) %all-to-all-start) | async-done | bytes 262176 | tf_op jit(solution)/shard_map/all_to_all | solution.py:480
  19.0 4.1 %all-to-all-start.2 = ((bf16[8,4,64,128]{3,2,1,0:T(8,128)(2,1)}), bf16[8,4,64,128]{3,2,1,0:T(8,128)(2,1)S(1)}, u32[]{:S(2)}, u32[]{:S(2)}) async-start(bf16[8,4,64,128]{3,2,1,0:T(8,128)(2,1)} %get-tuple-element.15), calls=%async_computation.2 | async-start | bytes 1048576 | tf_op jit(solution)/shard_map/all_to_all | solution.py:509
  23.1 0.2 select_dynamic-update-slice_fusion
  23.4 1.5 %collective-permute-start.1 = (bf16[528,256]{1,0:T(8,128)(2,1)S(1)}, bf16[528,256]{1,0:T(8,128)(2,1)S(1)}, u32[]{:S(2)}, u32[]{:S(2)}) collective-permute-start(bf16[528,256]{1,0:T(8,128)(2,1)S(1)} %get-tuple-element.14.mine_0), channel_id=1, source_target_pairs={{0,2},{2,0},{4,6},{6,4},{1,3},{3,1},{5,7},{7,5},{8,10},{10,8},{12,... | collective-permute-start | bytes 811016 | tf_op jit(solution)/shard_map/ppermute | solution.py:507
  24.9 2.4 %collective-permute-start.2 = (bf16[528,256]{1,0:T(8,128)(2,1)S(1)}, bf16[528,256]{1,0:T(8,128)(2,1)S(1)}, u32[]{:S(2)}, u32[]{:S(2)}) collective-permute-start(bf16[528,256]{1,0:T(8,128)(2,1)S(1)} %get-tuple-element.14.mine_0), channel_id=1, source_target_pairs={{0,4},{2,6},{4,0},{6,2},{1,5},{3,7},{5,1},{7,3},{8,12},{10,14},{12... | collective-permute-start | bytes 811016 | tf_op jit(solution)/shard_map/ppermute | solution.py:507
  27.5 5.9 %shard_map.166 = bf16[4,2,16,16,128]{4,3,2,1,0:T(8,128)(2,1)} custom-call(bf16[16,4,16,128]{3,2,1,0:T(8,128)(2,1)S(1)} %all-to-all-done.tiles, f32[125,8,128]{2,1,0:T(8,128)S(1)} %pad_maximum_fusion.1.taps, f32[8,512]{1,0:T(8,128)S(1)} %pad_maximum_fusion.2.shift), custom_call_target="tpu_custom_call" | custom-call | bytes 21000000 | tf_op jit(solution)/shard_map/pallas_call | solution.py:384
  33.4 0.8 copy-done.8
  34.2 10.2 %all-to-all-start.1 = ((bf16[128,16,128]{2,1,0:T(8,128)(2,1)}), bf16[128,16,128]{2,1,0:T(8,128)(2,1)S(1)}, u32[]{:S(2)}, u32[]{:S(2)}) async-start(bf16[128,16,128]{2,1,0:T(8,128)(2,1)} %bitcast.26), calls=%async_computation.1 | async-start | bytes 1048576 | tf_op jit(solution)/shard_map/all_to_all | solution.py:530
  44.4 1.1 collective-permute-start.4
  45.6 0.1 collective-permute-start.5
  45.7 0.4 collective-permute-start.6
  46.4 0.6 gather_fusion
  46.9 0.6 gather_fusion.1
  47.5 0.7 reshape.208.vectors
  48.2 0.6 copy.105
  48.8 9.3 %all-to-all-done.1.received_at = bf16[128,16,128]{2,1,0:T(8,128)(2,1)S(1)} async-done(((bf16[128,16,128]{2,1,0:T(8,128)(2,1)}), bf16[128,16,128]{2,1,0:T(8,128)(2,1)S(1)}, u32[]{:S(2)}, u32[]{:S(2)}) %all-to-all-start.1) | async-done | bytes 524320 | tf_op jit(solution)/shard_map/all_to_all | solution.py:530
  58.2 0.8 copy-done.9
  58.9 9.0 %shard_map.167 = (bf16[128,32,128]{2,1,0:T(8,128)(2,1)}, bf16[4,8,8,16,128]{4,3,2,1,0:T(8,128)(2,1)}, bf16[4,8,8,16,128]{4,3,2,1,0:T(8,128)(2,1)}) custom-call(s32[2]{0:T(128)} %copy-done.6, f32[4,256]{1,0:T(4,128)} %bitcast.67, f32[2,512]{1,0:T(2,128)} %reshape.208.vectors, bf16[128,16,128]{2,1,0:T(8,128)(2,1)} %copy-done.9, ...), custom_call_target="tpu_custom_call" | custom-call | tf_op jit(solution)/shard_map/pallas_call | solution.py:544
  68.0 0.6 collective-permute-start.7
  68.6 4.0 %all-to-all-start.3 = ((bf16[128,32,128]{2,1,0:T(8,128)(2,1)}), bf16[128,32,128]{2,1,0:T(8,128)(2,1)S(1)}, u32[]{:S(2)}, u32[]{:S(2)}) async-start(bf16[128,32,128]{2,1,0:T(8,128)(2,1)} %get-tuple-element.17), calls=%async_computation.3 | async-start | bytes 2097152 | tf_op jit(solution)/shard_map/all_to_all | solution.py:573
  72.7 0.6 copy-done.23
  73.3 2.3 %fusion.3 = (bf16[8,8,16,128]{3,2,1,0:T(8,128)(2,1)}, bf16[8,8,16,128]{3,2,1,0:T(8,128)(2,1)}, bf16[8,8,16,128]{3,2,1,0:T(8,128)(2,1)}, bf16[8,8,16,128]{3,2,1,0:T(8,128)(2,1)S(1)}) fusion(bf16[4,8,8,16,128]{4,3,2,1,0:T(8,128)(2,1)} %collective-permute-done.7, bf16[4,8,8,16,128]{4,3,2,1,0:T(8,128)(2,1)S(1)} %copy-done.10), kind=kLoop, calls=%fused_computation.11 | loop fusion | flops 2097152 | bytes 3145728 | tf_op jit(solution)/shard_map/convert_element_type | solution.py:425
  75.6 2.6 %collective-permute-start.10 = (bf16[8,8,16,128]{3,2,1,0:T(8,128)(2,1)}, bf16[8,8,16,128]{3,2,1,0:T(8,128)(2,1)S(1)}, u32[]{:S(2)}, u32[]{:S(2)}) collective-permute-start(bf16[8,8,16,128]{3,2,1,0:T(8,128)(2,1)} %get-tuple-element.26), channel_id=1, source_target_pairs={{0,6},{2,4},{4,2},{6,0},{1,7},{3,5},{5,3},{7,1},{8,14},{10,12},{12... | collective-permute-start | bytes 786440 | tf_op jit(solution)/shard_map/ppermute | solution.py:578
  78.2 1.3 collective-permute-start.9
  79.6 11.9 %all-to-all-done.3 = bf16[128,32,128]{2,1,0:T(8,128)(2,1)S(1)} async-done(((bf16[128,32,128]{2,1,0:T(8,128)(2,1)}), bf16[128,32,128]{2,1,0:T(8,128)(2,1)S(1)}, u32[]{:S(2)}, u32[]{:S(2)}) %all-to-all-start.3) | async-done | bytes 1048608 | tf_op jit(solution)/shard_map/all_to_all | solution.py:573
  91.5 5.5 %shard_map.168 = bf16[16,8,16,128]{3,2,1,0:T(8,128)(2,1)S(1)} custom-call(bf16[4,2,16,32,128]{4,3,2,1,0:T(8,128)(2,1)S(1)} %bitcast.60, bf16[16,4,16,128]{3,2,1,0:T(8,128)(2,1)S(1)} %all-to-all-done.tiles, f32[125,8,128]{2,1,0:T(8,128)S(1)} %pad_maximum_fusion.1.taps, f32[8,512]{1,0:T(8,128)S(1)} %get-tuple-element.56.scale, ...), custom_call_target="tpu_custom_call" | custom-call | bytes 21000000 | tf_op jit(solution)/shard_map/pallas_call | solution.py:384
  97.1 1.0 collective-permute-done.9.third
  98.1 0.1 shard_map.169
  98.2 14.3 %all_to_all.30 = bf16[8,8,16,128]{3,2,1,0:T(8,128)(2,1)S(1)} all-to-all(bf16[8,8,16,128]{3,2,1,0:T(8,128)(2,1)S(1)} %shard_map.169), channel_id=1, replica_groups=mesh['hi'=2,'core'=2,'col'=4,'x'=4,'y'=2] {'hi','col'}, dimensions={0} | all-to-all | bytes 524288 | tf_op jit(solution)/shard_map/all_to_all | solution.py:595
  112.7 21.8 %all_to_all.31.results = bf16[16,16,16,128]{3,2,1,0:T(8,128)(2,1)S(1)} all-to-all(bf16[16,16,16,128]{3,2,1,0:T(8,128)(2,1)S(1)} %pad_maximum_fusion), channel_id=1, replica_groups=mesh['hi'=2,'core'=2,'col'=4,'x'=4,'y'=2] {'hi','col','core'}, dimensions={0} | all-to-all | bytes 2097152 | tf_op jit(solution)/shard_map/all_to_all | solution.py:598
  134.6 1.3 shard_map.170
  (106 shorter events, 2.8 us)
Async XLA Ops:
  0.6 11.5 %copy-start = (f32[64,5,5]{0,2,1:T(8,128)S(1)}, f32[64,5,5]{0,2,1:T(8,128)}, u32[]{:S(2)}) copy-start(f32[64,5,5]{0,2,1:T(8,128)} %param.15) | copy-start | bytes 19204
  0.6 9.6 %copy-start.21 = (f32[64]{0:T(128)S(1)}, f32[64]{0:T(128)}, u32[]{:S(2)}) copy-start(f32[64]{0:T(128)} %param.21) | copy-start | bytes 772
  0.7 9.6 %copy-start.22 = (f32[64]{0:T(128)S(1)}, f32[64]{0:T(128)}, u32[]{:S(2)}) copy-start(f32[64]{0:T(128)} %param.20) | copy-start | bytes 772
  0.7 11.0 %copy-start.16 = (f32[3,64,4,5,5]{1,2,4,3,0:T(4,128)S(1)}, f32[3,64,4,5,5]{1,2,4,3,0:T(4,128)}, u32[]{:S(2)}) copy-start(f32[3,64,4,5,5]{1,2,4,3,0:T(4,128)} %param.18) | copy-start | bytes 230404
  0.7 18.3 %all-to-all-start = ((bf16[16,4,16,128]{3,2,1,0:T(8,128)(2,1)}), bf16[16,4,16,128]{3,2,1,0:T(8,128)(2,1)S(1)}, u32[]{:S(2)}, u32[]{:S(2)}) async-start(bf16[16,4,16,128]{3,2,1,0:T(8,128)(2,1)} %bitcast.64), calls=%async_computation | async-start | bytes 524288 | tf_op jit(solution)/shard_map/all_to_all | solution.py:480
  10.4 4.4 %collective-permute-start = (f32[1,128]{1,0:T(1,128)S(1)}, f32[1,128]{1,0:T(1,128)S(1)}, u32[]{:S(2)}, u32[]{:S(2)}) collective-permute-start(f32[1,128]{1,0:T(1,128)S(1)} %maximum_bitcast_fusion.norms), channel_id=1, source_target_pairs={{0,1},{1,0},{2,3},{3,2},{4,5},{5,4},{6,7},{7,6},{8,9},{9,8},{10,11... | collective-permute-start | bytes 1544 | tf_op jit(solution)/shard_map/ppermute | solution.py:485
  10.9 0.7 copy-start.17
  12.0 0.7 copy-start.19
  12.0 0.7 copy-start.20
  12.1 2.8 %copy-start.5 = (bf16[256,512]{1,0:T(8,128)(2,1)S(1)}, bf16[256,512]{1,0:T(8,128)(2,1)}, u32[]{:S(2)}) copy-start(bf16[256,512]{1,0:T(8,128)(2,1)} %w_out.1) | copy-start | bytes 786436
  13.1 1.7 %copy-start.18 = (f32[64]{0:T(128)S(1)}, f32[64]{0:T(128)}, u32[]{:S(2)}) copy-start(f32[64]{0:T(128)} %param.26) | copy-start | bytes 772
  13.2 1.7 %copy-start.1 = (bf16[64,16,128]{2,1,0:T(8,128)(2,1)S(1)}, bf16[64,16,128]{2,1,0:T(8,128)(2,1)}, u32[]{:S(2)}) copy-start(bf16[64,16,128]{2,1,0:T(8,128)(2,1)} %cotangent.1) | copy-start | bytes 786436
  13.2 1.7 %copy-start.4 = (bf16[512,256]{1,0:T(8,128)(2,1)S(1)}, bf16[512,256]{1,0:T(8,128)(2,1)}, u32[]{:S(2)}) copy-start(bf16[512,256]{1,0:T(8,128)(2,1)} %w_in.1) | copy-start | bytes 786436
  14.2 0.6 copy-start.6
  14.9 0.7 copy-start.7
  17.0 1.9 %copy-start.3 = (bf16[528,256]{1,0:T(8,128)(2,1)}, bf16[528,256]{1,0:T(8,128)(2,1)S(1)}, u32[]{:S(2)}) copy-start(bf16[528,256]{1,0:T(8,128)(2,1)S(1)} %get-tuple-element.16.others_0) | copy-start | bytes 811012
  17.0 29.1 %copy-start.2 = (bf16[528,256]{1,0:T(8,128)(2,1)}, bf16[528,256]{1,0:T(8,128)(2,1)S(1)}, u32[]{:S(2)}) copy-start(bf16[528,256]{1,0:T(8,128)(2,1)S(1)} %get-tuple-element.14.mine_0) | copy-start | bytes 811012
  19.0 14.4 %all-to-all-start.2 = ((bf16[8,4,64,128]{3,2,1,0:T(8,128)(2,1)}), bf16[8,4,64,128]{3,2,1,0:T(8,128)(2,1)S(1)}, u32[]{:S(2)}, u32[]{:S(2)}) async-start(bf16[8,4,64,128]{3,2,1,0:T(8,128)(2,1)} %get-tuple-element.15), calls=%async_computation.2 | async-start | bytes 1048576 | tf_op jit(solution)/shard_map/all_to_all | solution.py:509
  23.4 21.0 %collective-permute-start.1 = (bf16[528,256]{1,0:T(8,128)(2,1)S(1)}, bf16[528,256]{1,0:T(8,128)(2,1)S(1)}, u32[]{:S(2)}, u32[]{:S(2)}) collective-permute-start(bf16[528,256]{1,0:T(8,128)(2,1)S(1)} %get-tuple-element.14.mine_0), channel_id=1, source_target_pairs={{0,2},{2,0},{4,6},{6,4},{1,3},{3,1},{5,7},{7,5},{8,10},{10,8},{12,... | collective-permute-start | bytes 811016 | tf_op jit(solution)/shard_map/ppermute | solution.py:507
  24.9 20.6 %collective-permute-start.2 = (bf16[528,256]{1,0:T(8,128)(2,1)S(1)}, bf16[528,256]{1,0:T(8,128)(2,1)S(1)}, u32[]{:S(2)}, u32[]{:S(2)}) collective-permute-start(bf16[528,256]{1,0:T(8,128)(2,1)S(1)} %get-tuple-element.14.mine_0), channel_id=1, source_target_pairs={{0,4},{2,6},{4,0},{6,2},{1,5},{3,7},{5,1},{7,3},{8,12},{10,14},{12... | collective-permute-start | bytes 811016 | tf_op jit(solution)/shard_map/ppermute | solution.py:507
  27.3 18.4 %collective-permute-start.3 = (bf16[528,256]{1,0:T(8,128)(2,1)S(1)}, bf16[528,256]{1,0:T(8,128)(2,1)S(1)}, u32[]{:S(2)}, u32[]{:S(2)}) collective-permute-start(bf16[528,256]{1,0:T(8,128)(2,1)S(1)} %get-tuple-element.14.mine_0), channel_id=1, source_target_pairs={{0,6},{2,4},{4,2},{6,0},{1,7},{3,5},{5,3},{7,1},{8,14},{10,12},{12... | collective-permute-start | bytes 811016 | tf_op jit(solution)/shard_map/ppermute | solution.py:507
  33.4 0.8 copy-start.8
  34.2 24.0 %all-to-all-start.1 = ((bf16[128,16,128]{2,1,0:T(8,128)(2,1)}), bf16[128,16,128]{2,1,0:T(8,128)(2,1)S(1)}, u32[]{:S(2)}, u32[]{:S(2)}) async-start(bf16[128,16,128]{2,1,0:T(8,128)(2,1)} %bitcast.26), calls=%async_computation.1 | async-start | bytes 1048576 | tf_op jit(solution)/shard_map/all_to_all | solution.py:530
  44.4 13.7 %copy-start.11 = (bf16[528,256]{1,0:T(8,128)(2,1)}, bf16[528,256]{1,0:T(8,128)(2,1)S(1)}, u32[]{:S(2)}) copy-start(bf16[528,256]{1,0:T(8,128)(2,1)S(1)} %collective-permute-done.1.mine_1) | copy-start | bytes 811012
  44.4 4.4 %collective-permute-start.4 = (bf16[528,256]{1,0:T(8,128)(2,1)S(1)}, bf16[528,256]{1,0:T(8,128)(2,1)S(1)}, u32[]{:S(2)}, u32[]{:S(2)}) collective-permute-start(bf16[528,256]{1,0:T(8,128)(2,1)S(1)} %collective-permute-done.1.mine_1), channel_id=1, source_target_pairs={{0,32},{32,0},{1,33},{33,1},{2,34},{34,2},{3,35},{35,3},{4,36},{36... | collective-permute-start | bytes 811016 | tf_op jit(solution)/shard_map/ppermute | solution.py:508
  45.6 12.6 %copy-start.12 = (bf16[528,256]{1,0:T(8,128)(2,1)}, bf16[528,256]{1,0:T(8,128)(2,1)S(1)}, u32[]{:S(2)}) copy-start(bf16[528,256]{1,0:T(8,128)(2,1)S(1)} %collective-permute-done.2.mine_2) | copy-start | bytes 811012
  45.6 3.2 %collective-permute-start.5 = (bf16[528,256]{1,0:T(8,128)(2,1)S(1)}, bf16[528,256]{1,0:T(8,128)(2,1)S(1)}, u32[]{:S(2)}, u32[]{:S(2)}) collective-permute-start(bf16[528,256]{1,0:T(8,128)(2,1)S(1)} %collective-permute-done.2.mine_2), channel_id=1, source_target_pairs={{0,32},{32,0},{1,33},{33,1},{2,34},{34,2},{3,35},{35,3},{4,36},{36... | collective-permute-start | bytes 811016 | tf_op jit(solution)/shard_map/ppermute | solution.py:508
  45.7 12.5 %copy-start.13 = (bf16[528,256]{1,0:T(8,128)(2,1)}, bf16[528,256]{1,0:T(8,128)(2,1)S(1)}, u32[]{:S(2)}) copy-start(bf16[528,256]{1,0:T(8,128)(2,1)S(1)} %collective-permute-done.3.mine_3) | copy-start | bytes 811012
  45.7 3.1 %collective-permute-start.6 = (bf16[528,256]{1,0:T(8,128)(2,1)S(1)}, bf16[528,256]{1,0:T(8,128)(2,1)}, u32[]{:S(2)}, u32[]{:S(2)}) collective-permute-start(bf16[528,256]{1,0:T(8,128)(2,1)S(1)} %collective-permute-done.3.mine_3), channel_id=1, source_target_pairs={{0,32},{32,0},{1,33},{33,1},{2,34},{34,2},{3,35},{35,3},{4,36},{36... | collective-permute-start | bytes 811016 | tf_op jit(solution)/shard_map/ppermute | solution.py:508
  48.8 9.4 %copy-start.14 = (bf16[528,256]{1,0:T(8,128)(2,1)}, bf16[528,256]{1,0:T(8,128)(2,1)S(1)}, u32[]{:S(2)}) copy-start(bf16[528,256]{1,0:T(8,128)(2,1)S(1)} %collective-permute-done.4.others_1) | copy-start | bytes 811012
  48.8 9.4 %copy-start.15 = (bf16[528,256]{1,0:T(8,128)(2,1)}, bf16[528,256]{1,0:T(8,128)(2,1)S(1)}, u32[]{:S(2)}) copy-start(bf16[528,256]{1,0:T(8,128)(2,1)S(1)} %collective-permute-done.5.others_2) | copy-start | bytes 811012
  58.1 0.8 copy-start.9
  68.0 5.3 %collective-permute-start.7 = (bf16[4,8,8,16,128]{4,3,2,1,0:T(8,128)(2,1)}, bf16[4,8,8,16,128]{4,3,2,1,0:T(8,128)(2,1)}, u32[]{:S(2)}, u32[]{:S(2)}) collective-permute-start(bf16[4,8,8,16,128]{4,3,2,1,0:T(8,128)(2,1)} %get-tuple-element.19), channel_id=1, source_target_pairs={{0,32},{32,0},{1,33},{33,1},{2,34},{34,2},{3,35},{35,3},{4,36},{36... | collective-permute-start | bytes 3145736 | tf_op jit(solution)/shard_map/ppermute | solution.py:575
  68.6 4.7 %copy-start.10 = (bf16[4,8,8,16,128]{4,3,2,1,0:T(8,128)(2,1)S(1)}, bf16[4,8,8,16,128]{4,3,2,1,0:T(8,128)(2,1)}, u32[]{:S(2)}) copy-start(bf16[4,8,8,16,128]{4,3,2,1,0:T(8,128)(2,1)} %get-tuple-element.18) | copy-start | bytes 3145732
  68.6 22.9 %all-to-all-start.3 = ((bf16[128,32,128]{2,1,0:T(8,128)(2,1)}), bf16[128,32,128]{2,1,0:T(8,128)(2,1)S(1)}, u32[]{:S(2)}, u32[]{:S(2)}) async-start(bf16[128,32,128]{2,1,0:T(8,128)(2,1)} %get-tuple-element.17), calls=%async_computation.3 | async-start | bytes 2097152 | tf_op jit(solution)/shard_map/all_to_all | solution.py:573
  72.6 0.7 copy-start.23
  75.6 21.5 %collective-permute-start.10 = (bf16[8,8,16,128]{3,2,1,0:T(8,128)(2,1)}, bf16[8,8,16,128]{3,2,1,0:T(8,128)(2,1)S(1)}, u32[]{:S(2)}, u32[]{:S(2)}) collective-permute-start(bf16[8,8,16,128]{3,2,1,0:T(8,128)(2,1)} %get-tuple-element.26), channel_id=1, source_target_pairs={{0,6},{2,4},{4,2},{6,0},{1,7},{3,5},{5,3},{7,1},{8,14},{10,12},{12... | collective-permute-start | bytes 786440 | tf_op jit(solution)/shard_map/ppermute | solution.py:578
  78.2 18.9 %collective-permute-start.8 = (bf16[8,8,16,128]{3,2,1,0:T(8,128)(2,1)}, bf16[8,8,16,128]{3,2,1,0:T(8,128)(2,1)S(1)}, u32[]{:S(2)}, u32[]{:S(2)}) collective-permute-start(bf16[8,8,16,128]{3,2,1,0:T(8,128)(2,1)} %get-tuple-element.28), channel_id=1, source_target_pairs={{0,2},{2,0},{4,6},{6,4},{1,3},{3,1},{5,7},{7,5},{8,10},{10,8},{12,... | collective-permute-start | bytes 786440 | tf_op jit(solution)/shard_map/ppermute | solution.py:578
  78.2 19.9 %collective-permute-start.9 = (bf16[8,8,16,128]{3,2,1,0:T(8,128)(2,1)}, bf16[8,8,16,128]{3,2,1,0:T(8,128)(2,1)S(1)}, u32[]{:S(2)}, u32[]{:S(2)}) collective-permute-start(bf16[8,8,16,128]{3,2,1,0:T(8,128)(2,1)} %get-tuple-element.27), channel_id=1, source_target_pairs={{0,4},{2,6},{4,0},{6,2},{1,5},{3,7},{5,1},{7,3},{8,12},{10,14},{12... | collective-permute-start | bytes 786440 | tf_op jit(solution)/shard_map/ppermute | solution.py:578

commit v4 on v3

--- a/solution.py
+++ b/solution.py
@@ -255,13 +255,20 @@
 
 
 def mlp_kernel(
-    order, biases, vectors, received_at, received_scaled_at,
+    order, biases, vectors, received_at, twins,
     mine_0, mine_1, mine_2, mine_3, others_0, others_1, others_2, others_3, sent_at, kept_at, given_at,
     received, received_scaled, packs, mixed, scaled, projected, grads, sent, kept, given, arrived, left,
 ):
     halves = ((mine_0, others_0), (mine_1, others_1), (mine_2, others_2), (mine_3, others_3))
-    sources = (received_at, received_scaled_at, *[half for pair in halves for half in pair])
-    targets = (received, received_scaled, *[packs.at[index, half] for index in range(X) for half in range(2)])
+    share = CHANS // (X * Y)
+    blocks = [pair[0].at[CHANS + 16 : CHANS + 16 + 2 * share] for pair in halves]
+    sources = (received_at, *blocks, twins, *[half.at[:CHANS] for pair in halves for half in pair])
+    targets = (
+        received,
+        *[received_scaled.at[0, index] for index in range(X)],
+        received_scaled.at[1],
+        *[packs.at[index, half] for index in range(X) for half in range(2)],
+    )
     arrivals = [
         pltpu.make_async_copy(source, target, arrived.at[i]) for i, (source, target) in enumerate(zip(sources, targets))
     ]
@@ -290,11 +297,15 @@
                     mixed[rows, place : place + LINE] = lines[line]
 
     loop(CHANS // 16, 4, arrange)
-    arrivals[1].wait()
-    share = CHANS // (X * Y)
-    for block in range(X * Y):
-        for line in range(LINES):
-            scaled[block * share : block * share + share, line * LINE : line * LINE + LINE] = received_scaled[block, line]
+    for index in range(X + 1):
+        arrivals[1 + index].wait()
+    for index in range(X):
+        for twin in range(Y):
+            chip = (order[0] ^ index) * Y + (order[2] ^ twin)
+            rows = pl.ds(pl.multiple_of(chip * share, share), share)
+            for pair in range(LINES // 2):
+                area = slice(pair * share, pair * share + share)
+                scaled[rows, pair * 2 * LINE : (pair + 1) * 2 * LINE] = received_scaled[twin, index, area]
     values = mixed[...]
     average = jnp.sum(values, 0, keepdims=True) / CHANS
     rescale = lax.rsqrt(jnp.sum(values * values, 0, keepdims=True) / CHANS - average * average + EPSILON)
@@ -306,8 +317,8 @@
     scaled_now = scaled[...]
     normed_turned, scaled_turned = normed.T, scaled_now.T
     for index in range(X):
-        arrivals[2 + 2 * index].wait()
-        arrivals[3 + 2 * index].wait()
+        arrivals[6 + 2 * index].wait()
+        arrivals[7 + 2 * index].wait()
         w_in, w_out, activated, grad_hidden = hidden_parts(
             packs.at[index], order[1], biases[index : index + 1], normed_turned, scaled_turned
         )
@@ -392,20 +403,25 @@
     )(*ops)
 
 
-def prepare_kernel(order, cotangent, layer, w_in, w_out, b_in, norms, other, scaled, mine, others):
+def scale_kernel(cotangent, layer, scaled):
     for block in range(0, CHANS // (X * Y), 16):
         rows = [
             jnp.swapaxes(cotangent[part : part + SUB].astype(F32) * layer[part : part + SUB], 0, 1)
             for part in (block, block + SUB)
         ]
-        rounded = jnp.concatenate(rows, 1).astype(BF16)
-        for where in range(X):
-            for twin in range(Y):
-                scaled[where * Y + twin, :, block : block + 16] = rounded[where * LINES : where * LINES + LINES]
+        scaled[:, block : block + 16] = jnp.concatenate(rows, 1).astype(BF16)
+
+
+def prepare_kernel(
+    order, w_in, w_out, b_in, norms, other, scaled, pack_0, pack_1, pack_2, pack_3, others
+):
+    packs = (pack_0, pack_1, pack_2, pack_3)
     for half in range(2):
         area = slice(half * HID, half * HID + HID)
         first, second = w_in[area], w_out[:, area]
-        mine[area] = jnp.where(order[1] == 0, first, second)
+        mine = jnp.where(order[1] == 0, first, second)
+        for pack in packs:
+            pack[area] = mine
         others[area] = jnp.where(order[1] == 0, second, first)
     left = [b_in[...], jnp.concatenate([norms[...], other[...]], 1)]
     rows = []
@@ -414,8 +430,14 @@
         left = [value - part for value, part in zip(left, parts)]
         rows.extend(parts)
     small = jnp.concatenate(rows + [jnp.zeros((10, HID), F32)], 0).astype(BF16)
-    mine[CHANS:] = small
-    others[CHANS:] = small
+    share = CHANS // (X * Y)
+    for step, pack in enumerate(packs):
+        pack[CHANS : CHANS + 16] = small
+        start = (order[0] ^ step) * LINES
+        for pair in range(LINES // 2):
+            first = CHANS + 16 + pair * share
+            lines = (scaled[start + 2 * pair], scaled[start + 2 * pair + 1])
+            pack[first : first + share] = jnp.concatenate(lines, 1)
 
 
 def summed(*terms):
@@ -483,30 +505,24 @@
     share = CHANS // (X * Y)
     norms = jnp.concatenate([norm_gain, norm_bias]).reshape(1, 2 * share)
     other = lax.ppermute(norms, "y", [(0, 1), (1, 0)])
-    order = jnp.stack([x_here, core_here]).astype(jnp.int32)
-    scaled, mine, others = call(
+    order = jnp.stack([x_here, core_here, y_here]).astype(jnp.int32)
+    scaled = call(
+        scale_kernel,
+        jax.ShapeDtypeStruct((16, share, LINE), BF16),
+        [],
+        (cotangent, jnp.broadcast_to(layer_scale[:, None, None], (share, 1, LINE))),
+        1,
+    )
+    *mine, others = call(
         prepare_kernel,
-        (
-            jax.ShapeDtypeStruct((X * Y, LINES, share, LINE), BF16),
-            jax.ShapeDtypeStruct((CHANS + 16, HID), BF16),
-            jax.ShapeDtypeStruct((CHANS + 16, HID), BF16),
-        ),
+        (jax.ShapeDtypeStruct((CHANS + 16 + 2 * share, HID), BF16),) * X + (jax.ShapeDtypeStruct((CHANS, HID), BF16),),
         [],
-        (
-            order,
-            cotangent,
-            jnp.broadcast_to(layer_scale[:, None, None], (share, 1, LINE)),
-            w_in,
-            w_out,
-            b_in.reshape(1, HID),
-            norms,
-            other,
-        ),
+        (order, w_in, w_out, b_in.reshape(1, HID), norms, other, scaled),
         1,
     )
-    mine = [mine] + [lax.ppermute(mine, "x", [(i, i ^ step) for i in range(X)]) for step in range(1, X)]
-    others = [others] + [lax.ppermute(one, "core", [(0, 1), (1, 0)]) for one in mine[1:]]
-    scaled = lax.all_to_all(scaled, ("x", "y"), split_axis=0, concat_axis=0, tiled=True)
+    mine = mine[:1] + [lax.ppermute(mine[step], "x", [(i, i ^ step) for i in range(X)]) for step in range(1, X)]
+    others = [others] + [lax.ppermute(one[:CHANS], "core", [(0, 1), (1, 0)]) for one in mine[1:]]
+    twins = lax.ppermute(jnp.stack([one[CHANS + 16 :] for one in mine]), "y", [(0, 1), (1, 0)])
 
     scale_own = own_planes(base_scale, 0, place)
     taps = tap_table(
@@ -548,8 +564,8 @@
         out_specs=(anywhere,) * 3,
         scratch_shapes=[
             pltpu.VMEM(received.shape, BF16),
-            pltpu.VMEM(scaled.shape, BF16),
-            pltpu.VMEM((X, 2, CHANS + 16, HID), BF16),
+            pltpu.VMEM((Y, X, 2 * share, HID), BF16),
+            pltpu.VMEM((X, 2, CHANS, HID), BF16),
             pltpu.VMEM((CHANS, SPOTS), F32),
             pltpu.VMEM((CHANS, SPOTS), BF16),
             pltpu.VMEM((CHANS, SPOTS), F32),
@@ -557,7 +573,7 @@
             pltpu.VMEM(blocks, BF16),
             pltpu.VMEM(pieces, BF16),
             pltpu.VMEM(pieces, BF16),
-            pltpu.SemaphoreType.DMA((10,)),
+            pltpu.SemaphoreType.DMA((14,)),
             pltpu.SemaphoreType.DMA((12,)),
         ],
         compiler_params=pltpu.CompilerParams(vmem_limit_bytes=MLP_VMEM),
@@ -566,7 +582,7 @@
         biases,
         vectors,
         received,
-        scaled,
+        twins,
         *mine,
         *others,
     )

time: 136 us -> 136 us (level)
  waiting for transfers between devices: 24.2 us -> 13.3 us
  local copies, waits for them, and re-layouts: 8.87 us -> 17.3 us
  starting transfers between devices: 38.5 us -> 40.6 us
    all_to_all x1, waiting for transfers between devices: 9.32 us -> 0.49 us  [on_device(): lax.all_to_all(sent.reshape(X * Y * GROUP, 2 * SUB, LINE), everyone, spli...]
    all_to_all x1, starting transfers between devices: 3.96 us -> 8.6 us  [on_device(): lax.all_to_all(sent, everyone, split_axis=0, concat_axis=0, tiled=True)]
    all_to_all x1 -> x0, starting transfers between devices: 4.13 us -> none  [on_device(): lax.all_to_all(scaled, ('x', 'y'), split_axis=0, concat_axis=0, tiled=True)]
    slice x0 -> x3, local copies, waits for them, and re-layouts: none -> 2.9 us  [on_device(): one[:CHANS]]
    another operation x0 -> x4, local copies, waits for them, and re-layouts: none -> 2.54 us  [on_device(): jnp.stack([one[CHANS + 16:] for one in mine])]
    slice x4, local copies, waits for them, and re-layouts: 0.01 us -> 2.03 us  [on_device(): extras = jnp.stack([one[CHANS:CHANS + 6] for one in mine])]
    all_to_all x1, waiting for transfers between devices: 1.92 us -> 0.01 us  [on_device(): lax.all_to_all(feature_map.reshape(GROUP, PLANES, 16, 128), group, split_...]
    ppermute x6 -> x7, starting transfers between devices: 5.68 us -> 6.9 us  [the longest x3 3.86 us: on_device(): lax.ppermute(mine[step], 'x', [(i, i ^ step) for i in range(X)])]
  transfers between devices with their start and end apart: 15 -> 15, of which waited for: 5 -> 3; matrix products, arithmetic and copies ran while one was open for 6% -> 12% of each run, Pallas kernels for 9% -> 9%
where the time goes in v4:
time: 136 us; the launch traced here: 135 us
  starting transfers between devices  40.6 us (30%)
  blocking collectives  36.5 us (27%)
  Pallas kernels  22.7 us (17%)
  local copies, waits for them, and re-layouts  17.3 us (13%)
  waiting for transfers between devices  13.3 us (10%)
  other arithmetic  3.72 us (3%)
    all_to_all x1, blocking collectives, on_device(): lax.all_to_all(sent, group, split_axis=0, concat_axis=0, tiled=True)  22.2 us
    all_to_all x1, blocking collectives, on_device(): lax.all_to_all(pieces, ('hi', 'col'), split_axis=0, concat_axis=0, tiled=...  14.3 us
    pallas_call x6, Pallas kernels, call(): pl.pallas_call(kernel, out_shape=outs, in_specs=spaces, out_specs=out_spa...  13.6 us
    all_to_all x1, waiting for transfers between devices, on_device(): lax.all_to_all(sent, everyone, split_axis=0, concat_axis=0, tiled=True)  12 us
    all_to_all x1, starting transfers between devices, on_device(): lax.all_to_all(sent.reshape(X * Y * GROUP, 2 * SUB, LINE), everyone, spli...  10.7 us
    all_to_all x1, starting transfers between devices, on_device(): lax.all_to_all(feature_map.reshape(GROUP, PLANES, 16, 128), group, split_...  9.6 us
    pallas_call x1, Pallas kernels, on_device(): pl.pallas_call(mlp_kernel, out_shape=tuple((jax.ShapeDtypeStruct(shape, B...  9.08 us
    all_to_all x1, starting transfers between devices, on_device(): lax.all_to_all(sent, everyone, split_axis=0, concat_axis=0, tiled=True)  8.6 us
  transfers between devices with their start and end apart: 15, of which 3 were waited for; matrix products, arithmetic and copies ran while one was open for 12% of the time, Pallas kernels for 9%

profile of v4, /device:TPU:1, one launch (start us, length us, event | category | flops | bytes accessed | tf_op | source)
XLA Modules:
  0.0 135.3 jit_solution(15549456688548998489)
XLA Ops:
  0.7 9.6 %all-to-all-start = ((bf16[16,4,16,128]{3,2,1,0:T(8,128)(2,1)}), bf16[16,4,16,128]{3,2,1,0:T(8,128)(2,1)S(1)}, u32[]{:S(2)}, u32[]{:S(2)}) async-start(bf16[16,4,16,128]{3,2,1,0:T(8,128)(2,1)} %bitcast.73), calls=%async_computation | async-start | bytes 524288 | tf_op jit(solution)/shard_map/all_to_all | solution.py:502
  10.4 0.4 collective-permute-start
  10.9 0.7 copy-done.13
  11.8 0.2 copy.89
  12.4 0.5 copy-done.15
  14.6 0.2 select_dynamic-update-slice_fusion.1
  14.8 0.2 select_dynamic-update-slice_fusion
  15.3 0.6 copy-done.14
  16.2 0.3 copy-done.6
  16.5 0.5 copy-done.3
  17.0 0.7 shard_map.166
  17.7 0.7 copy-done.5
  18.4 2.5 %collective-permute-start.3 = (bf16[656,256]{1,0:T(8,128)(2,1)S(1)}, bf16[656,256]{1,0:T(8,128)(2,1)}, u32[]{:S(2)}, u32[]{:S(2)}) collective-permute-start(bf16[656,256]{1,0:T(8,128)(2,1)S(1)} %get-tuple-element.19), channel_id=1, source_target_pairs={{0,6},{2,4},{4,2},{6,0},{1,7},{3,5},{5,3},{7,1},{8,14},{10,12},{12... | collective-permute-start | bytes 1007624 | tf_op jit(solution)/shard_map/ppermute | solution.py:523
  20.9 1.4 %collective-permute-start.2 = (bf16[656,256]{1,0:T(8,128)(2,1)S(1)}, bf16[656,256]{1,0:T(8,128)(2,1)}, u32[]{:S(2)}, u32[]{:S(2)}) collective-permute-start(bf16[656,256]{1,0:T(8,128)(2,1)S(1)} %get-tuple-element.18), channel_id=1, source_target_pairs={{0,4},{2,6},{4,0},{6,2},{1,5},{3,7},{5,1},{7,3},{8,12},{10,14},{12... | collective-permute-start | bytes 1007624 | tf_op jit(solution)/shard_map/ppermute | solution.py:523
  22.3 5.9 %shard_map.167 = bf16[4,2,16,16,128]{4,3,2,1,0:T(8,128)(2,1)} custom-call(bf16[16,4,16,128]{3,2,1,0:T(8,128)(2,1)S(1)} %all-to-all-done.tiles, f32[125,8,128]{2,1,0:T(8,128)S(1)} %pad_maximum_fusion.1.taps, f32[8,512]{1,0:T(8,128)S(1)} %pad_maximum_fusion.3.shift), custom_call_target="tpu_custom_call" | custom-call | bytes 21000000 | tf_op jit(solution)/shard_map/pallas_call | solution.py:395
  28.2 10.7 %all-to-all-start.1 = ((bf16[128,16,128]{2,1,0:T(8,128)(2,1)}), bf16[128,16,128]{2,1,0:T(8,128)(2,1)S(1)}, u32[]{:S(2)}, u32[]{:S(2)}) async-start(bf16[128,16,128]{2,1,0:T(8,128)(2,1)} %bitcast.27), calls=%async_computation.1 | async-start | bytes 1048576 | tf_op jit(solution)/shard_map/all_to_all | solution.py:546
  38.9 0.8 slice_bitcast_fusion
  39.7 0.8 slice_bitcast_fusion.1
  40.6 0.8 slice_bitcast_fusion.2
  41.5 1.5 %collective-permute-start.4 = (bf16[4,128,256]{2,1,0:T(8,128)(2,1)S(1)}, bf16[4,128,256]{2,1,0:T(8,128)(2,1)S(1)}, u32[]{:S(2)}, u32[]{:S(2)}) collective-permute-start(bf16[4,128,256]{2,1,0:T(8,128)(2,1)S(1)} %pad_maximum_fusion.2), channel_id=1, source_target_pairs={{0,1},{1,0},{2,3},{3,2},{4,5},{5,4},{6,7},{7,6},{8,9},{9,8},{10,11... | collective-permute-start | bytes 786440 | tf_op jit(solution)/shard_map/ppermute | solution.py:525
  42.9 1.0 slice.192
  43.9 0.7 collective-permute-start.5
  44.6 1.0 slice.193
  45.7 1.0 slice.194
  46.7 0.8 collective-permute-start.7
  47.5 0.7 slice.172
  48.2 0.7 slice.173
  48.9 0.7 slice.174
  49.7 0.6 gather_fusion
  50.3 0.6 gather_fusion.1
  50.9 0.7 reshape.208.vectors
  51.5 0.6 copy.105
  52.2 0.5 all-to-all-done.1.received_at
  52.7 0.2 copy-done.10
  52.9 0.5 copy-done.8
  53.5 9.1 %shard_map.168 = (bf16[128,32,128]{2,1,0:T(8,128)(2,1)}, bf16[4,8,8,16,128]{4,3,2,1,0:T(8,128)(2,1)}, bf16[4,8,8,16,128]{4,3,2,1,0:T(8,128)(2,1)}) custom-call(s32[3]{0:T(128)} %copy-done.6, f32[4,256]{1,0:T(4,128)} %bitcast.76, f32[2,512]{1,0:T(2,128)} %reshape.208.vectors, bf16[128,16,128]{2,1,0:T(8,128)(2,1)} %copy-done.8, ...), custom_call_target="tpu_custom_call" | custom-call | tf_op jit(solution)/shard_map/pallas_call | solution.py:560
  62.5 0.6 collective-permute-start.8
  63.1 8.6 %all-to-all-start.2 = ((bf16[128,32,128]{2,1,0:T(8,128)(2,1)}), bf16[128,32,128]{2,1,0:T(8,128)(2,1)S(1)}, u32[]{:S(2)}, u32[]{:S(2)}) async-start(bf16[128,32,128]{2,1,0:T(8,128)(2,1)} %get-tuple-element.21), calls=%async_computation.2 | async-start | bytes 2097152 | tf_op jit(solution)/shard_map/all_to_all | solution.py:589
  71.8 0.6 copy-done.19
  72.5 2.3 %fusion.3 = (bf16[8,8,16,128]{3,2,1,0:T(8,128)(2,1)}, bf16[8,8,16,128]{3,2,1,0:T(8,128)(2,1)}, bf16[8,8,16,128]{3,2,1,0:T(8,128)(2,1)}, bf16[8,8,16,128]{3,2,1,0:T(8,128)(2,1)S(1)}) fusion(bf16[4,8,8,16,128]{4,3,2,1,0:T(8,128)(2,1)} %collective-permute-done.8, bf16[4,8,8,16,128]{4,3,2,1,0:T(8,128)(2,1)S(1)} %copy-done.9), kind=kLoop, calls=%fused_computation.11 | loop fusion | flops 2097152 | bytes 3145728 | tf_op jit(solution)/shard_map/convert_element_type | solution.py:447
  74.8 2.9 %collective-permute-start.10 = (bf16[8,8,16,128]{3,2,1,0:T(8,128)(2,1)}, bf16[8,8,16,128]{3,2,1,0:T(8,128)(2,1)S(1)}, u32[]{:S(2)}, u32[]{:S(2)}) collective-permute-start(bf16[8,8,16,128]{3,2,1,0:T(8,128)(2,1)} %get-tuple-element.31), channel_id=1, source_target_pairs={{0,4},{2,6},{4,0},{6,2},{1,5},{3,7},{5,1},{7,3},{8,12},{10,14},{12... | collective-permute-start | bytes 786440 | tf_op jit(solution)/shard_map/ppermute | solution.py:594
  77.7 0.9 collective-permute-start.11
  78.7 12.0 %all-to-all-done.2 = bf16[128,32,128]{2,1,0:T(8,128)(2,1)S(1)} async-done(((bf16[128,32,128]{2,1,0:T(8,128)(2,1)}), bf16[128,32,128]{2,1,0:T(8,128)(2,1)S(1)}, u32[]{:S(2)}, u32[]{:S(2)}) %all-to-all-start.2) | async-done | bytes 1048608 | tf_op jit(solution)/shard_map/all_to_all | solution.py:589
  90.7 5.5 %shard_map.169 = bf16[16,8,16,128]{3,2,1,0:T(8,128)(2,1)S(1)} custom-call(bf16[4,2,16,32,128]{4,3,2,1,0:T(8,128)(2,1)S(1)} %bitcast.69, bf16[16,4,16,128]{3,2,1,0:T(8,128)(2,1)S(1)} %all-to-all-done.tiles, f32[125,8,128]{2,1,0:T(8,128)S(1)} %pad_maximum_fusion.1.taps, f32[8,512]{1,0:T(8,128)S(1)} %get-tuple-element.60.scale, ...), custom_call_target="tpu_custom_call" | custom-call | bytes 21000000 | tf_op jit(solution)/shard_map/pallas_call | solution.py:395
  96.3 0.8 collective-permute-done.11.fourth
  97.2 14.3 %all_to_all.25 = bf16[8,8,16,128]{3,2,1,0:T(8,128)(2,1)S(1)} all-to-all(bf16[8,8,16,128]{3,2,1,0:T(8,128)(2,1)S(1)} %shard_map.170), channel_id=1, replica_groups=mesh['hi'=2,'core'=2,'col'=4,'x'=4,'y'=2] {'hi','col'}, dimensions={0} | all-to-all | bytes 524288 | tf_op jit(solution)/shard_map/all_to_all | solution.py:611
  111.8 22.2 %all_to_all.26.results = bf16[16,16,16,128]{3,2,1,0:T(8,128)(2,1)S(1)} all-to-all(bf16[16,16,16,128]{3,2,1,0:T(8,128)(2,1)S(1)} %pad_maximum_fusion), channel_id=1, replica_groups=mesh['hi'=2,'core'=2,'col'=4,'x'=4,'y'=2] {'hi','col','core'}, dimensions={0} | all-to-all | bytes 2097152 | tf_op jit(solution)/shard_map/all_to_all | solution.py:614
  133.9 1.3 shard_map.171
  (107 shorter events, 4.3 us)
Async XLA Ops:
  0.6 11.5 %copy-start = (f32[64,5,5]{0,2,1:T(8,128)S(1)}, f32[64,5,5]{0,2,1:T(8,128)}, u32[]{:S(2)}) copy-start(f32[64,5,5]{0,2,1:T(8,128)} %param.15) | copy-start | bytes 19204
  0.6 9.6 %copy-start.17 = (f32[64]{0:T(128)S(1)}, f32[64]{0:T(128)}, u32[]{:S(2)}) copy-start(f32[64]{0:T(128)} %param.21) | copy-start | bytes 772
  0.7 9.6 %copy-start.18 = (f32[64]{0:T(128)S(1)}, f32[64]{0:T(128)}, u32[]{:S(2)}) copy-start(f32[64]{0:T(128)} %param.20) | copy-start | bytes 772
  0.7 11.0 %copy-start.12 = (f32[3,64,4,5,5]{1,2,4,3,0:T(4,128)S(1)}, f32[3,64,4,5,5]{1,2,4,3,0:T(4,128)}, u32[]{:S(2)}) copy-start(f32[3,64,4,5,5]{1,2,4,3,0:T(4,128)} %param.18) | copy-start | bytes 230404
  0.7 21.6 %all-to-all-start = ((bf16[16,4,16,128]{3,2,1,0:T(8,128)(2,1)}), bf16[16,4,16,128]{3,2,1,0:T(8,128)(2,1)S(1)}, u32[]{:S(2)}, u32[]{:S(2)}) async-start(bf16[16,4,16,128]{3,2,1,0:T(8,128)(2,1)} %bitcast.73), calls=%async_computation | async-start | bytes 524288 | tf_op jit(solution)/shard_map/all_to_all | solution.py:502
  10.4 5.8 %collective-permute-start = (f32[1,128]{1,0:T(1,128)S(1)}, f32[1,128]{1,0:T(1,128)S(1)}, u32[]{:S(2)}, u32[]{:S(2)}) collective-permute-start(f32[1,128]{1,0:T(1,128)S(1)} %maximum_bitcast_fusion.norms), channel_id=1, source_target_pairs={{0,1},{1,0},{2,3},{3,2},{4,5},{5,4},{6,7},{7,6},{8,9},{9,8},{10,11... | collective-permute-start | bytes 1544 | tf_op jit(solution)/shard_map/ppermute | solution.py:507
  10.9 0.7 copy-start.13
  12.2 0.7 copy-start.15
  12.2 0.7 copy-start.16
  15.0 1.0 copy-start.1
  15.2 0.7 copy-start.14
  15.9 0.6 copy-start.6
  16.0 1.0 copy-start.3
  16.0 1.0 copy-start.4
  16.2 0.9 copy-start.7
  17.7 0.7 copy-start.5
  18.4 29.0 %copy-start.2 = (bf16[656,256]{1,0:T(8,128)(2,1)}, bf16[656,256]{1,0:T(8,128)(2,1)S(1)}, u32[]{:S(2)}) copy-start(bf16[656,256]{1,0:T(8,128)(2,1)S(1)} %get-tuple-element.16.mine_0) | copy-start | bytes 1007620
  18.4 20.5 %collective-permute-start.3 = (bf16[656,256]{1,0:T(8,128)(2,1)S(1)}, bf16[656,256]{1,0:T(8,128)(2,1)}, u32[]{:S(2)}, u32[]{:S(2)}) collective-permute-start(bf16[656,256]{1,0:T(8,128)(2,1)S(1)} %get-tuple-element.19), channel_id=1, source_target_pairs={{0,6},{2,4},{4,2},{6,0},{1,7},{3,5},{5,3},{7,1},{8,14},{10,12},{12... | collective-permute-start | bytes 1007624 | tf_op jit(solution)/shard_map/ppermute | solution.py:523
  20.9 19.7 %collective-permute-start.1 = (bf16[656,256]{1,0:T(8,128)(2,1)S(1)}, bf16[656,256]{1,0:T(8,128)(2,1)}, u32[]{:S(2)}, u32[]{:S(2)}) collective-permute-start(bf16[656,256]{1,0:T(8,128)(2,1)S(1)} %get-tuple-element.17), channel_id=1, source_target_pairs={{0,2},{2,0},{4,6},{6,4},{1,3},{3,1},{5,7},{7,5},{8,10},{10,8},{12,... | collective-permute-start | bytes 1007624 | tf_op jit(solution)/shard_map/ppermute | solution.py:523
  20.9 18.8 %collective-permute-start.2 = (bf16[656,256]{1,0:T(8,128)(2,1)S(1)}, bf16[656,256]{1,0:T(8,128)(2,1)}, u32[]{:S(2)}, u32[]{:S(2)}) collective-permute-start(bf16[656,256]{1,0:T(8,128)(2,1)S(1)} %get-tuple-element.18), channel_id=1, source_target_pairs={{0,4},{2,6},{4,0},{6,2},{1,5},{3,7},{5,1},{7,3},{8,12},{10,14},{12... | collective-permute-start | bytes 1007624 | tf_op jit(solution)/shard_map/ppermute | solution.py:523
  28.2 24.5 %all-to-all-start.1 = ((bf16[128,16,128]{2,1,0:T(8,128)(2,1)}), bf16[128,16,128]{2,1,0:T(8,128)(2,1)S(1)}, u32[]{:S(2)}, u32[]{:S(2)}) async-start(bf16[128,16,128]{2,1,0:T(8,128)(2,1)} %bitcast.27), calls=%async_computation.1 | async-start | bytes 1048576 | tf_op jit(solution)/shard_map/all_to_all | solution.py:546
  41.5 10.6 %collective-permute-start.4 = (bf16[4,128,256]{2,1,0:T(8,128)(2,1)S(1)}, bf16[4,128,256]{2,1,0:T(8,128)(2,1)S(1)}, u32[]{:S(2)}, u32[]{:S(2)}) collective-permute-start(bf16[4,128,256]{2,1,0:T(8,128)(2,1)S(1)} %pad_maximum_fusion.2), channel_id=1, source_target_pairs={{0,1},{1,0},{2,3},{3,2},{4,5},{5,4},{6,7},{7,6},{8,9},{9,8},{10,11... | collective-permute-start | bytes 786440 | tf_op jit(solution)/shard_map/ppermute | solution.py:525
  43.9 8.2 %collective-permute-start.5 = (bf16[512,256]{1,0:T(8,128)(2,1)S(1)}, bf16[512,256]{1,0:T(8,128)(2,1)S(1)}, u32[]{:S(2)}, u32[]{:S(2)}) collective-permute-start(bf16[512,256]{1,0:T(8,128)(2,1)S(1)} %slice.192), channel_id=1, source_target_pairs={{0,32},{32,0},{1,33},{33,1},{2,34},{34,2},{3,35},{35,3},{4,36},{36... | collective-permute-start | bytes 786440 | tf_op jit(solution)/shard_map/ppermute | solution.py:524
  45.6 6.5 %collective-permute-start.6 = (bf16[512,256]{1,0:T(8,128)(2,1)S(1)}, bf16[512,256]{1,0:T(8,128)(2,1)}, u32[]{:S(2)}, u32[]{:S(2)}) collective-permute-start(bf16[512,256]{1,0:T(8,128)(2,1)S(1)} %slice.193), channel_id=1, source_target_pairs={{0,32},{32,0},{1,33},{33,1},{2,34},{34,2},{3,35},{35,3},{4,36},{36... | collective-permute-start | bytes 786440 | tf_op jit(solution)/shard_map/ppermute | solution.py:524
  46.7 5.5 %collective-permute-start.7 = (bf16[512,256]{1,0:T(8,128)(2,1)S(1)}, bf16[512,256]{1,0:T(8,128)(2,1)}, u32[]{:S(2)}, u32[]{:S(2)}) collective-permute-start(bf16[512,256]{1,0:T(8,128)(2,1)S(1)} %slice.194), channel_id=1, source_target_pairs={{0,32},{32,0},{1,33},{33,1},{2,34},{34,2},{3,35},{35,3},{4,36},{36... | collective-permute-start | bytes 786440 | tf_op jit(solution)/shard_map/ppermute | solution.py:524
  52.1 0.7 copy-start.10
  52.1 0.8 copy-start.11
  52.7 0.8 copy-start.8
  62.5 10.0 %collective-permute-start.8 = (bf16[4,8,8,16,128]{4,3,2,1,0:T(8,128)(2,1)}, bf16[4,8,8,16,128]{4,3,2,1,0:T(8,128)(2,1)}, u32[]{:S(2)}, u32[]{:S(2)}) collective-permute-start(bf16[4,8,8,16,128]{4,3,2,1,0:T(8,128)(2,1)} %get-tuple-element.23), channel_id=1, source_target_pairs={{0,32},{32,0},{1,33},{33,1},{2,34},{34,2},{3,35},{35,3},{4,36},{36... | collective-permute-start | bytes 3145736 | tf_op jit(solution)/shard_map/ppermute | solution.py:591
  63.1 9.3 %copy-start.9 = (bf16[4,8,8,16,128]{4,3,2,1,0:T(8,128)(2,1)S(1)}, bf16[4,8,8,16,128]{4,3,2,1,0:T(8,128)(2,1)}, u32[]{:S(2)}) copy-start(bf16[4,8,8,16,128]{4,3,2,1,0:T(8,128)(2,1)} %get-tuple-element.22) | copy-start | bytes 3145732
  63.1 27.6 %all-to-all-start.2 = ((bf16[128,32,128]{2,1,0:T(8,128)(2,1)}), bf16[128,32,128]{2,1,0:T(8,128)(2,1)S(1)}, u32[]{:S(2)}, u32[]{:S(2)}) async-start(bf16[128,32,128]{2,1,0:T(8,128)(2,1)} %get-tuple-element.21), calls=%async_computation.2 | async-start | bytes 2097152 | tf_op jit(solution)/shard_map/all_to_all | solution.py:589
  71.8 0.7 copy-start.19
  74.8 21.5 %collective-permute-start.10 = (bf16[8,8,16,128]{3,2,1,0:T(8,128)(2,1)}, bf16[8,8,16,128]{3,2,1,0:T(8,128)(2,1)S(1)}, u32[]{:S(2)}, u32[]{:S(2)}) collective-permute-start(bf16[8,8,16,128]{3,2,1,0:T(8,128)(2,1)} %get-tuple-element.31), channel_id=1, source_target_pairs={{0,4},{2,6},{4,0},{6,2},{1,5},{3,7},{5,1},{7,3},{8,12},{10,14},{12... | collective-permute-start | bytes 786440 | tf_op jit(solution)/shard_map/ppermute | solution.py:594
  77.7 19.4 %collective-permute-start.11 = (bf16[8,8,16,128]{3,2,1,0:T(8,128)(2,1)}, bf16[8,8,16,128]{3,2,1,0:T(8,128)(2,1)S(1)}, u32[]{:S(2)}, u32[]{:S(2)}) collective-permute-start(bf16[8,8,16,128]{3,2,1,0:T(8,128)(2,1)} %get-tuple-element.30), channel_id=1, source_target_pairs={{0,6},{2,4},{4,2},{6,0},{1,7},{3,5},{5,3},{7,1},{8,14},{10,12},{12... | collective-permute-start | bytes 786440 | tf_op jit(solution)/shard_map/ppermute | solution.py:594
  78.5 18.5 %collective-permute-start.9 = (bf16[8,8,16,128]{3,2,1,0:T(8,128)(2,1)}, bf16[8,8,16,128]{3,2,1,0:T(8,128)(2,1)S(1)}, u32[]{:S(2)}, u32[]{:S(2)}) collective-permute-start(bf16[8,8,16,128]{3,2,1,0:T(8,128)(2,1)} %get-tuple-element.32), channel_id=1, source_target_pairs={{0,2},{2,0},{4,6},{6,4},{1,3},{3,1},{5,7},{7,5},{8,10},{10,8},{12,... | collective-permute-start | bytes 786440 | tf_op jit(solution)/shard_map/ppermute | solution.py:594

commit v5 on v4

--- a/solution.py
+++ b/solution.py
@@ -521,7 +521,7 @@
         1,
     )
     mine = mine[:1] + [lax.ppermute(mine[step], "x", [(i, i ^ step) for i in range(X)]) for step in range(1, X)]
-    others = [others] + [lax.ppermute(one[:CHANS], "core", [(0, 1), (1, 0)]) for one in mine[1:]]
+    others = [others] + [lax.ppermute(one, "core", [(0, 1), (1, 0)]) for one in mine[1:]]
     twins = lax.ppermute(jnp.stack([one[CHANS + 16 :] for one in mine]), "y", [(0, 1), (1, 0)])
 
     scale_own = own_planes(base_scale, 0, place)

time: 136 us -> 136 us (level)
  local copies, waits for them, and re-layouts: 17.3 us -> 13 us
  waiting for transfers between devices: 13.3 us -> 17.4 us
    ppermute x1, waiting for transfers between devices: 0.01 us -> 3.77 us  [on_device(): lax.ppermute(jnp.stack([one[CHANS + 16:] for one in mine]), 'y', [(0, 1),...]
    slice x3 -> x0, local copies, waits for them, and re-layouts: 2.9 us -> none  [on_device(): one[:CHANS]]
    unnamed x43 -> x51, local copies, waits for them, and re-layouts: 5.57 us -> 4.89 us
  transfers between devices with their start and end apart: 15 -> 15, of which waited for: 3 -> 4; matrix products, arithmetic and copies ran while one was open for 12% -> 10% of each run, Pallas kernels for 9% -> 9%
where the time goes in v5:
time: 136 us; the launch traced here: 135 us
  starting transfers between devices  40.4 us (30%)
  blocking collectives  36.5 us (27%)
  Pallas kernels  22.7 us (17%)
  waiting for transfers between devices  17.4 us (13%)
  local copies, waits for them, and re-layouts  13 us (10%)
  other arithmetic  4.43 us (3%)
    all_to_all x1, blocking collectives, on_device(): lax.all_to_all(sent, group, split_axis=0, concat_axis=0, tiled=True)  22.2 us
    all_to_all x1, blocking collectives, on_device(): lax.all_to_all(pieces, ('hi', 'col'), split_axis=0, concat_axis=0, tiled=...  14.3 us
    pallas_call x6, Pallas kernels, call(): pl.pallas_call(kernel, out_shape=outs, in_specs=spaces, out_specs=out_spa...  13.6 us
    all_to_all x1, waiting for transfers between devices, on_device(): lax.all_to_all(sent, everyone, split_axis=0, concat_axis=0, tiled=True)  12 us
    all_to_all x1, starting transfers between devices, on_device(): lax.all_to_all(sent.reshape(X * Y * GROUP, 2 * SUB, LINE), everyone, spli...  10.7 us
    all_to_all x1, starting transfers between devices, on_device(): lax.all_to_all(feature_map.reshape(GROUP, PLANES, 16, 128), group, split_...  9.6 us
    pallas_call x1, Pallas kernels, on_device(): pl.pallas_call(mlp_kernel, out_shape=tuple((jax.ShapeDtypeStruct(shape, B...  9.06 us
    all_to_all x1, starting transfers between devices, on_device(): lax.all_to_all(sent, everyone, split_axis=0, concat_axis=0, tiled=True)  8.51 us
  transfers between devices with their start and end apart: 15, of which 4 were waited for; matrix products, arithmetic and copies ran while one was open for 10% of the time, Pallas kernels for 9%

profile of v5, /device:TPU:1, one launch (start us, length us, event | category | flops | bytes accessed | tf_op | source)
XLA Modules:
  0.0 135.4 jit_solution(17835330641541314554)
XLA Ops:
  0.7 9.6 %all-to-all-start = ((bf16[16,4,16,128]{3,2,1,0:T(8,128)(2,1)}), bf16[16,4,16,128]{3,2,1,0:T(8,128)(2,1)S(1)}, u32[]{:S(2)}, u32[]{:S(2)}) async-start(bf16[16,4,16,128]{3,2,1,0:T(8,128)(2,1)} %bitcast.73), calls=%async_computation | async-start | bytes 524288 | tf_op jit(solution)/shard_map/all_to_all | solution.py:502
  10.4 0.4 collective-permute-start
  10.9 0.7 copy-done.17
  11.6 0.1 dynamic-slice_multiply_fusion
  11.8 0.2 copy.89
  12.4 0.5 copy-done.19
  14.3 0.1 select_dynamic-update-slice_fusion.3
  14.5 0.1 select_dynamic-update-slice_fusion.2
  14.6 0.2 select_dynamic-update-slice_fusion.1
  14.8 0.2 select_dynamic-update-slice_fusion
  15.3 0.6 copy-done.18
  16.0 0.1 shard_map.165.scaled
  16.2 0.3 copy-done.6
  16.5 0.5 copy-done.4
  17.0 0.7 shard_map.166
  17.7 2.6 %collective-permute-start.3 = (bf16[656,256]{1,0:T(8,128)(2,1)S(1)}, bf16[656,256]{1,0:T(8,128)(2,1)S(1)}, u32[]{:S(2)}, u32[]{:S(2)}) collective-permute-start(bf16[656,256]{1,0:T(8,128)(2,1)S(1)} %get-tuple-element.19), channel_id=1, source_target_pairs={{0,6},{2,4},{4,2},{6,0},{1,7},{3,5},{5,3},{7,1},{8,14},{10,12},{12... | collective-permute-start | bytes 1007624 | tf_op jit(solution)/shard_map/ppermute | solution.py:523
  20.3 1.4 %collective-permute-start.2 = (bf16[656,256]{1,0:T(8,128)(2,1)S(1)}, bf16[656,256]{1,0:T(8,128)(2,1)}, u32[]{:S(2)}, u32[]{:S(2)}) collective-permute-start(bf16[656,256]{1,0:T(8,128)(2,1)S(1)} %get-tuple-element.18), channel_id=1, source_target_pairs={{0,4},{2,6},{4,0},{6,2},{1,5},{3,7},{5,1},{7,3},{8,12},{10,14},{12... | collective-permute-start | bytes 1007624 | tf_op jit(solution)/shard_map/ppermute | solution.py:523
  21.7 0.6 slice_bitcast_fusion.3
  22.3 5.9 %shard_map.167 = bf16[4,2,16,16,128]{4,3,2,1,0:T(8,128)(2,1)} custom-call(bf16[16,4,16,128]{3,2,1,0:T(8,128)(2,1)S(1)} %all-to-all-done.tiles, f32[125,8,128]{2,1,0:T(8,128)S(1)} %pad_maximum_fusion.1.taps, f32[8,512]{1,0:T(8,128)S(1)} %pad_maximum_fusion.3.shift), custom_call_target="tpu_custom_call" | custom-call | bytes 21000000 | tf_op jit(solution)/shard_map/pallas_call | solution.py:395
  28.2 10.7 %all-to-all-start.1 = ((bf16[128,16,128]{2,1,0:T(8,128)(2,1)}), bf16[128,16,128]{2,1,0:T(8,128)(2,1)S(1)}, u32[]{:S(2)}, u32[]{:S(2)}) async-start(bf16[128,16,128]{2,1,0:T(8,128)(2,1)} %bitcast.27), calls=%async_computation.1 | async-start | bytes 1048576 | tf_op jit(solution)/shard_map/all_to_all | solution.py:546
  39.0 0.9 slice_bitcast_fusion.1
  39.9 0.9 slice_bitcast_fusion.2
  40.8 0.7 pad_maximum_fusion.2
  41.5 1.4 %collective-permute-start.4 = (bf16[4,128,256]{2,1,0:T(8,128)(2,1)}, bf16[4,128,256]{2,1,0:T(8,128)(2,1)S(1)}, u32[]{:S(2)}, u32[]{:S(2)}) collective-permute-start(bf16[4,128,256]{2,1,0:T(8,128)(2,1)} %pad_maximum_fusion.2), channel_id=1, source_target_pairs={{0,1},{1,0},{2,3},{3,2},{4,5},{5,4},{6,7},{7,6},{8,9},{9,8},{10,11... | collective-permute-start | bytes 786440 | tf_op jit(solution)/shard_map/ppermute | solution.py:525
  42.9 0.6 collective-permute-start.5
  43.5 0.5 collective-permute-start.7
  44.1 0.7 slice.160
  44.8 0.7 slice.161
  45.7 0.6 gather_fusion
  46.2 0.6 gather_fusion.1
  46.8 0.7 reshape.208.vectors
  47.5 0.6 copy.105
  48.1 3.8 %collective-permute-done.4.twins = bf16[4,128,256]{2,1,0:T(8,128)(2,1)S(1)} collective-permute-done((bf16[4,128,256]{2,1,0:T(8,128)(2,1)}, bf16[4,128,256]{2,1,0:T(8,128)(2,1)S(1)}, u32[]{:S(2)}, u32[]{:S(2)}) %collective-permute-start.4) | collective-permute-done | bytes 262176 | tf_op jit(solution)/shard_map/ppermute | solution.py:525
  51.9 0.8 all-to-all-done.1.received_at
  52.9 0.6 copy-done.8
  53.5 9.1 %shard_map.168 = (bf16[128,32,128]{2,1,0:T(8,128)(2,1)}, bf16[4,8,8,16,128]{4,3,2,1,0:T(8,128)(2,1)}, bf16[4,8,8,16,128]{4,3,2,1,0:T(8,128)(2,1)}) custom-call(s32[3]{0:T(128)} %copy-done.6, f32[4,256]{1,0:T(4,128)} %bitcast.76, f32[2,512]{1,0:T(2,128)} %reshape.208.vectors, bf16[128,16,128]{2,1,0:T(8,128)(2,1)} %copy-done.8, ...), custom_call_target="tpu_custom_call" | custom-call | tf_op jit(solution)/shard_map/pallas_call | solution.py:560
  62.5 0.9 collective-permute-start.8
  63.4 8.5 %all-to-all-start.2 = ((bf16[128,32,128]{2,1,0:T(8,128)(2,1)}), bf16[128,32,128]{2,1,0:T(8,128)(2,1)S(1)}, u32[]{:S(2)}, u32[]{:S(2)}) async-start(bf16[128,32,128]{2,1,0:T(8,128)(2,1)} %get-tuple-element.21), calls=%async_computation.2 | async-start | bytes 2097152 | tf_op jit(solution)/shard_map/all_to_all | solution.py:589
  72.0 0.6 copy-done.23
  72.7 2.3 %fusion.3 = (bf16[8,8,16,128]{3,2,1,0:T(8,128)(2,1)}, bf16[8,8,16,128]{3,2,1,0:T(8,128)(2,1)}, bf16[8,8,16,128]{3,2,1,0:T(8,128)(2,1)}, bf16[8,8,16,128]{3,2,1,0:T(8,128)(2,1)S(1)}) fusion(bf16[4,8,8,16,128]{4,3,2,1,0:T(8,128)(2,1)} %collective-permute-done.8, bf16[4,8,8,16,128]{4,3,2,1,0:T(8,128)(2,1)S(1)} %copy-done.9), kind=kLoop, calls=%fused_computation.11 | loop fusion | flops 2097152 | bytes 3145728 | tf_op jit(solution)/shard_map/convert_element_type | solution.py:447
  74.9 2.9 %collective-permute-start.10 = (bf16[8,8,16,128]{3,2,1,0:T(8,128)(2,1)}, bf16[8,8,16,128]{3,2,1,0:T(8,128)(2,1)S(1)}, u32[]{:S(2)}, u32[]{:S(2)}) collective-permute-start(bf16[8,8,16,128]{3,2,1,0:T(8,128)(2,1)} %get-tuple-element.31), channel_id=1, source_target_pairs={{0,4},{2,6},{4,0},{6,2},{1,5},{3,7},{5,1},{7,3},{8,12},{10,14},{12... | collective-permute-start | bytes 786440 | tf_op jit(solution)/shard_map/ppermute | solution.py:594
  77.8 0.9 collective-permute-start.11
  78.9 12.0 %all-to-all-done.2 = bf16[128,32,128]{2,1,0:T(8,128)(2,1)S(1)} async-done(((bf16[128,32,128]{2,1,0:T(8,128)(2,1)}), bf16[128,32,128]{2,1,0:T(8,128)(2,1)S(1)}, u32[]{:S(2)}, u32[]{:S(2)}) %all-to-all-start.2) | async-done | bytes 1048608 | tf_op jit(solution)/shard_map/all_to_all | solution.py:589
  90.9 5.5 %shard_map.169 = bf16[16,8,16,128]{3,2,1,0:T(8,128)(2,1)S(1)} custom-call(bf16[4,2,16,32,128]{4,3,2,1,0:T(8,128)(2,1)S(1)} %bitcast.69, bf16[16,4,16,128]{3,2,1,0:T(8,128)(2,1)S(1)} %all-to-all-done.tiles, f32[125,8,128]{2,1,0:T(8,128)S(1)} %pad_maximum_fusion.1.taps, f32[8,512]{1,0:T(8,128)S(1)} %get-tuple-element.60.scale, ...), custom_call_target="tpu_custom_call" | custom-call | bytes 21000000 | tf_op jit(solution)/shard_map/pallas_call | solution.py:395
  96.4 0.8 collective-permute-done.11.fourth
  97.4 14.3 %all_to_all.25 = bf16[8,8,16,128]{3,2,1,0:T(8,128)(2,1)S(1)} all-to-all(bf16[8,8,16,128]{3,2,1,0:T(8,128)(2,1)S(1)} %shard_map.170), channel_id=1, replica_groups=mesh['hi'=2,'core'=2,'col'=4,'x'=4,'y'=2] {'hi','col'}, dimensions={0} | all-to-all | bytes 524288 | tf_op jit(solution)/shard_map/all_to_all | solution.py:611
  112.0 22.2 %all_to_all.26.results = bf16[16,16,16,128]{3,2,1,0:T(8,128)(2,1)S(1)} all-to-all(bf16[16,16,16,128]{3,2,1,0:T(8,128)(2,1)S(1)} %pad_maximum_fusion), channel_id=1, replica_groups=mesh['hi'=2,'core'=2,'col'=4,'x'=4,'y'=2] {'hi','col','core'}, dimensions={0} | all-to-all | bytes 2097152 | tf_op jit(solution)/shard_map/all_to_all | solution.py:614
  134.1 1.3 shard_map.171
  (112 shorter events, 3.7 us)
Async XLA Ops:
  0.6 11.5 %copy-start = (f32[64,5,5]{0,2,1:T(8,128)S(1)}, f32[64,5,5]{0,2,1:T(8,128)}, u32[]{:S(2)}) copy-start(f32[64,5,5]{0,2,1:T(8,128)} %param.15) | copy-start | bytes 19204
  0.6 9.6 %copy-start.21 = (f32[64]{0:T(128)S(1)}, f32[64]{0:T(128)}, u32[]{:S(2)}) copy-start(f32[64]{0:T(128)} %param.21) | copy-start | bytes 772
  0.7 9.6 %copy-start.22 = (f32[64]{0:T(128)S(1)}, f32[64]{0:T(128)}, u32[]{:S(2)}) copy-start(f32[64]{0:T(128)} %param.20) | copy-start | bytes 772
  0.7 11.0 %copy-start.16 = (f32[3,64,4,5,5]{1,2,4,3,0:T(4,128)S(1)}, f32[3,64,4,5,5]{1,2,4,3,0:T(4,128)}, u32[]{:S(2)}) copy-start(f32[3,64,4,5,5]{1,2,4,3,0:T(4,128)} %param.18) | copy-start | bytes 230404
  0.7 21.6 %all-to-all-start = ((bf16[16,4,16,128]{3,2,1,0:T(8,128)(2,1)}), bf16[16,4,16,128]{3,2,1,0:T(8,128)(2,1)S(1)}, u32[]{:S(2)}, u32[]{:S(2)}) async-start(bf16[16,4,16,128]{3,2,1,0:T(8,128)(2,1)} %bitcast.73), calls=%async_computation | async-start | bytes 524288 | tf_op jit(solution)/shard_map/all_to_all | solution.py:502
  10.4 5.8 %collective-permute-start = (f32[1,128]{1,0:T(1,128)S(1)}, f32[1,128]{1,0:T(1,128)S(1)}, u32[]{:S(2)}, u32[]{:S(2)}) collective-permute-start(f32[1,128]{1,0:T(1,128)S(1)} %maximum_bitcast_fusion.norms), channel_id=1, source_target_pairs={{0,1},{1,0},{2,3},{3,2},{4,5},{5,4},{6,7},{7,6},{8,9},{9,8},{10,11... | collective-permute-start | bytes 1544 | tf_op jit(solution)/shard_map/ppermute | solution.py:507
  10.9 0.7 copy-start.17
  12.2 0.7 copy-start.19
  12.2 0.7 copy-start.20
  15.0 1.0 copy-start.1
  15.2 0.7 copy-start.18
  15.9 0.6 copy-start.6
  16.0 1.0 copy-start.4
  16.0 1.0 copy-start.5
  16.2 0.9 copy-start.7
  17.7 10.5 %copy-start.3 = (bf16[512,256]{1,0:T(8,128)(2,1)}, bf16[512,256]{1,0:T(8,128)(2,1)S(1)}, u32[]{:S(2)}) copy-start(bf16[512,256]{1,0:T(8,128)(2,1)S(1)} %get-tuple-element.20.others_0) | copy-start | bytes 786436
  17.7 26.3 %copy-start.2 = (bf16[656,256]{1,0:T(8,128)(2,1)}, bf16[656,256]{1,0:T(8,128)(2,1)S(1)}, u32[]{:S(2)}) copy-start(bf16[656,256]{1,0:T(8,128)(2,1)S(1)} %get-tuple-element.16.mine_0) | copy-start | bytes 1007620
  17.7 21.2 %collective-permute-start.3 = (bf16[656,256]{1,0:T(8,128)(2,1)S(1)}, bf16[656,256]{1,0:T(8,128)(2,1)S(1)}, u32[]{:S(2)}, u32[]{:S(2)}) collective-permute-start(bf16[656,256]{1,0:T(8,128)(2,1)S(1)} %get-tuple-element.19), channel_id=1, source_target_pairs={{0,6},{2,4},{4,2},{6,0},{1,7},{3,5},{5,3},{7,1},{8,14},{10,12},{12... | collective-permute-start | bytes 1007624 | tf_op jit(solution)/shard_map/ppermute | solution.py:523
  20.3 19.6 %collective-permute-start.1 = (bf16[656,256]{1,0:T(8,128)(2,1)S(1)}, bf16[656,256]{1,0:T(8,128)(2,1)}, u32[]{:S(2)}, u32[]{:S(2)}) collective-permute-start(bf16[656,256]{1,0:T(8,128)(2,1)S(1)} %get-tuple-element.17), channel_id=1, source_target_pairs={{0,2},{2,0},{4,6},{6,4},{1,3},{3,1},{5,7},{7,5},{8,10},{10,8},{12,... | collective-permute-start | bytes 1007624 | tf_op jit(solution)/shard_map/ppermute | solution.py:523
  20.3 18.7 %collective-permute-start.2 = (bf16[656,256]{1,0:T(8,128)(2,1)S(1)}, bf16[656,256]{1,0:T(8,128)(2,1)}, u32[]{:S(2)}, u32[]{:S(2)}) collective-permute-start(bf16[656,256]{1,0:T(8,128)(2,1)S(1)} %get-tuple-element.18), channel_id=1, source_target_pairs={{0,4},{2,6},{4,0},{6,2},{1,5},{3,7},{5,1},{7,3},{8,12},{10,14},{12... | collective-permute-start | bytes 1007624 | tf_op jit(solution)/shard_map/ppermute | solution.py:523
  28.2 24.5 %all-to-all-start.1 = ((bf16[128,16,128]{2,1,0:T(8,128)(2,1)}), bf16[128,16,128]{2,1,0:T(8,128)(2,1)S(1)}, u32[]{:S(2)}, u32[]{:S(2)}) async-start(bf16[128,16,128]{2,1,0:T(8,128)(2,1)} %bitcast.27), calls=%async_computation.1 | async-start | bytes 1048576 | tf_op jit(solution)/shard_map/all_to_all | solution.py:546
  38.9 6.6 %copy-start.10 = (bf16[656,256]{1,0:T(8,128)(2,1)}, bf16[656,256]{1,0:T(8,128)(2,1)S(1)}, u32[]{:S(2)}) copy-start(bf16[656,256]{1,0:T(8,128)(2,1)S(1)} %collective-permute-done.3.mine_3) | copy-start | bytes 1007620
  39.9 0.9 copy-start.15
  41.5 10.4 %collective-permute-start.4 = (bf16[4,128,256]{2,1,0:T(8,128)(2,1)}, bf16[4,128,256]{2,1,0:T(8,128)(2,1)S(1)}, u32[]{:S(2)}, u32[]{:S(2)}) collective-permute-start(bf16[4,128,256]{2,1,0:T(8,128)(2,1)} %pad_maximum_fusion.2), channel_id=1, source_target_pairs={{0,1},{1,0},{2,3},{3,2},{4,5},{5,4},{6,7},{7,6},{8,9},{9,8},{10,11... | collective-permute-start | bytes 786440 | tf_op jit(solution)/shard_map/ppermute | solution.py:525
  42.9 9.0 %collective-permute-start.5 = (bf16[656,256]{1,0:T(8,128)(2,1)}, bf16[656,256]{1,0:T(8,128)(2,1)S(1)}, u32[]{:S(2)}, u32[]{:S(2)}) collective-permute-start(bf16[656,256]{1,0:T(8,128)(2,1)} %collective-permute-done.1.mine_1), channel_id=1, source_target_pairs={{0,32},{32,0},{1,33},{33,1},{2,34},{34,2},{3,35},{35,3},{4,36},{36... | collective-permute-start | bytes 1007624 | tf_op jit(solution)/shard_map/ppermute | solution.py:524
  43.5 8.3 %collective-permute-start.6 = (bf16[656,256]{1,0:T(8,128)(2,1)}, bf16[656,256]{1,0:T(8,128)(2,1)S(1)}, u32[]{:S(2)}, u32[]{:S(2)}) collective-permute-start(bf16[656,256]{1,0:T(8,128)(2,1)} %collective-permute-done.2.mine_2), channel_id=1, source_target_pairs={{0,32},{32,0},{1,33},{33,1},{2,34},{34,2},{3,35},{35,3},{4,36},{36... | collective-permute-start | bytes 1007624 | tf_op jit(solution)/shard_map/ppermute | solution.py:524
  43.5 8.4 %collective-permute-start.7 = (bf16[656,256]{1,0:T(8,128)(2,1)S(1)}, bf16[656,256]{1,0:T(8,128)(2,1)S(1)}, u32[]{:S(2)}, u32[]{:S(2)}) collective-permute-start(bf16[656,256]{1,0:T(8,128)(2,1)S(1)} %collective-permute-done.3.mine_3), channel_id=1, source_target_pairs={{0,32},{32,0},{1,33},{33,1},{2,34},{34,2},{3,35},{35,3},{4,36},{36... | collective-permute-start | bytes 1007624 | tf_op jit(solution)/shard_map/ppermute | solution.py:524
  51.9 0.8 copy-start.14
  51.9 0.8 copy-start.11
  51.9 0.9 copy-start.12
  51.9 1.0 copy-start.13
  52.7 0.8 copy-start.8
  62.5 10.1 %collective-permute-start.8 = (bf16[4,8,8,16,128]{4,3,2,1,0:T(8,128)(2,1)}, bf16[4,8,8,16,128]{4,3,2,1,0:T(8,128)(2,1)}, u32[]{:S(2)}, u32[]{:S(2)}) collective-permute-start(bf16[4,8,8,16,128]{4,3,2,1,0:T(8,128)(2,1)} %get-tuple-element.23), channel_id=1, source_target_pairs={{0,32},{32,0},{1,33},{33,1},{2,34},{34,2},{3,35},{35,3},{4,36},{36... | collective-permute-start | bytes 3145736 | tf_op jit(solution)/shard_map/ppermute | solution.py:591
  63.4 9.3 %copy-start.9 = (bf16[4,8,8,16,128]{4,3,2,1,0:T(8,128)(2,1)S(1)}, bf16[4,8,8,16,128]{4,3,2,1,0:T(8,128)(2,1)}, u32[]{:S(2)}) copy-start(bf16[4,8,8,16,128]{4,3,2,1,0:T(8,128)(2,1)} %get-tuple-element.22) | copy-start | bytes 3145732
  63.4 27.5 %all-to-all-start.2 = ((bf16[128,32,128]{2,1,0:T(8,128)(2,1)}), bf16[128,32,128]{2,1,0:T(8,128)(2,1)S(1)}, u32[]{:S(2)}, u32[]{:S(2)}) async-start(bf16[128,32,128]{2,1,0:T(8,128)(2,1)} %get-tuple-element.21), calls=%async_computation.2 | async-start | bytes 2097152 | tf_op jit(solution)/shard_map/all_to_all | solution.py:589
  71.9 0.7 copy-start.23
  74.9 21.5 %collective-permute-start.10 = (bf16[8,8,16,128]{3,2,1,0:T(8,128)(2,1)}, bf16[8,8,16,128]{3,2,1,0:T(8,128)(2,1)S(1)}, u32[]{:S(2)}, u32[]{:S(2)}) collective-permute-start(bf16[8,8,16,128]{3,2,1,0:T(8,128)(2,1)} %get-tuple-element.31), channel_id=1, source_target_pairs={{0,4},{2,6},{4,0},{6,2},{1,5},{3,7},{5,1},{7,3},{8,12},{10,14},{12... | collective-permute-start | bytes 786440 | tf_op jit(solution)/shard_map/ppermute | solution.py:594
  77.8 19.4 %collective-permute-start.11 = (bf16[8,8,16,128]{3,2,1,0:T(8,128)(2,1)}, bf16[8,8,16,128]{3,2,1,0:T(8,128)(2,1)S(1)}, u32[]{:S(2)}, u32[]{:S(2)}) collective-permute-start(bf16[8,8,16,128]{3,2,1,0:T(8,128)(2,1)} %get-tuple-element.30), channel_id=1, source_target_pairs={{0,6},{2,4},{4,2},{6,0},{1,7},{3,5},{5,3},{7,1},{8,14},{10,12},{12... | collective-permute-start | bytes 786440 | tf_op jit(solution)/shard_map/ppermute | solution.py:594
  78.7 18.5 %collective-permute-start.9 = (bf16[8,8,16,128]{3,2,1,0:T(8,128)(2,1)}, bf16[8,8,16,128]{3,2,1,0:T(8,128)(2,1)S(1)}, u32[]{:S(2)}, u32[]{:S(2)}) collective-permute-start(bf16[8,8,16,128]{3,2,1,0:T(8,128)(2,1)} %get-tuple-element.32), channel_id=1, source_target_pairs={{0,2},{2,0},{4,6},{6,4},{1,3},{3,1},{5,7},{7,5},{8,10},{10,8},{12,... | collective-permute-start | bytes 786440 | tf_op jit(solution)/shard_map/ppermute | solution.py:594
